TPU v7x, 32 devices: a whole 2x2x4 slice. The times are simulated.
32 devices in a mesh: dp: 4 (over x, core), seq: 8 (over z, y).
Axes of the slice: x: 2, y: 2, z: 4, core: 2. Of those that a mesh axis runs over, the one named last changes fastest.
Arguments:
- tokens: bfloat16 [24, 2048, 512], P('dp', 'seq'), may hold values from -6 to 6
- document_starts: int32 [24, 16], P('dp'), may hold values from 0 to 2047, as said below
- attention_in: bfloat16 [512, 1536], replicated, may hold values from -0.375 to 0.375
- attention_out: bfloat16 [512, 512], replicated, may hold values from -1 to 1
- feedforward_in: bfloat16 [512, 1536], replicated, may hold values from -0.25 to 0.25
- feedforward_out: bfloat16 [768, 512], replicated, may hold values from -0.21875 to 0.21875
- gain_first: float32 [512], replicated, may hold values from 0.1 to 1.9
- gain_second: float32 [512], replicated, may hold values from 0.1 to 1.9
- result_grad: bfloat16 [24, 2048, 512], P('dp', 'seq'), may hold values from -6 to 6
Outputs:
- activations: bfloat16 [24, 2048, 512], P('dp', 'seq')
- grad_tokens: float32 [24, 2048, 512], P('dp', 'seq')
- grad_attention_in: float32 [512, 1536], replicated
- grad_attention_out: float32 [512, 512], replicated
- grad_feedforward_in: float32 [512, 1536], replicated
- grad_feedforward_out: float32 [768, 512], replicated
- grad_gain_first: float32 [512], replicated
- grad_gain_second: float32 [512], replicated
Inputs may be any that keep to these rules, and one draw needn't show every extreme that they name: `document_starts`: in each row the 16 document starts rise strictly from 0.
All inputs are finite; a program needn't handle non-finite values.
Results may differ from a plain program's by a relative error of at most 0.014.
The roundings to bfloat16 on the way count: a program that leaves them out, or rounds other values in their place, can miss the bound.
Values may be sent and summed in bfloat16 or wider, within the bound.
No kernel may reach another device: no remote copies, remote signals or barrier semaphores. Data moves between devices by JAX's collectives and lax.ppermute only.
A program may use at most 192 MiB of HBM per device.

v0:
```python
import jax
import jax.numpy as jnp
from jax import lax
from jax.sharding import PartitionSpec as P

HEADS = 8
HEAD_DIM = 64
HALF_WIN = 64


EPSILON = 1e-05
ROTARY_BASE = 10000.0


def with_halo(block, sides, width):
    for axis, dim in sides:
        count = lax.axis_size(axis)
        forward = [(i, i + 1) for i in range(count - 1)]
        backward = [(target, source) for source, target in forward]
        low = lax.ppermute(
            lax.slice_in_dim(block, block.shape[dim] - width, None, axis=dim), axis, forward
        )
        high = lax.ppermute(lax.slice_in_dim(block, 0, width, axis=dim), axis, backward)
        block = jnp.concatenate([low, block, high], axis=dim)
    return block


def shifted_2(block, axis, distance):
    devices = range(lax.axis_size(axis))
    route = [(i - distance, i) for i in devices if i - distance in devices]
    return lax.ppermute(block, axis, route)


def norm_rows(values, scaling):
    center = jnp.mean(values, axis=-1, keepdims=True)
    shifted = values - center
    spread = jnp.mean(shifted * shifted, axis=-1, keepdims=True)
    return shifted * lax.rsqrt(spread + EPSILON) * scaling


def rotary_tables(positions):
    inverse = ROTARY_BASE ** (-(jnp.arange(0, HEAD_DIM, 2).astype(jnp.float32) / HEAD_DIM))
    angles = positions.astype(jnp.float32)[:, None] * inverse[None, :]
    angles = jnp.concatenate([angles, angles], axis=-1)
    return (jnp.cos(angles), jnp.sin(angles))


def rotate(values, cosine, sines):
    middle_col = values.shape[-1] // 2
    turned = jnp.concatenate([-values[..., middle_col:], values[..., :middle_col]], axis=-1)
    return values * cosine[:, None, :] + turned * sines[:, None, :]


def rotate_back(gradients, cosine, sines):
    scaled = gradients * sines[:, None, :]
    middle_col = scaled.shape[-1] // 2
    turned = jnp.concatenate([scaled[..., middle_col:], -scaled[..., :middle_col]], axis=-1)
    return gradients * cosine[:, None, :] + turned


def gated_gelu(gate_in, lift_in):
    return jax.nn.gelu(gate_in, approximate=False) * lift_in


def shards(
    tokens,
    document_starts,
    attention_in,
    attention_out,
    feedforward_in,
    feedforward_out,
    gain_first,
    gain_second,
    result_grad,
):
    row_count, own_len, model_width = tokens.shape
    hidden_width = feedforward_out.shape[0]
    margin = HALF_WIN
    keys_len = own_len + 2 * margin
    row_len = own_len * lax.axis_size("seq")
    start_pos = lax.axis_index("seq") * own_len
    own_positions = start_pos + jnp.arange(own_len, dtype=jnp.int32)
    key_positions = start_pos - margin + jnp.arange(keys_len, dtype=jnp.int32)
    query_docs = jnp.sum(
        (document_starts[:, None, :] <= own_positions[None, :, None]).astype(jnp.int32), axis=2
    )
    key_docs = jnp.sum(
        (document_starts[:, None, :] <= key_positions[None, :, None]).astype(jnp.int32), axis=2
    )
    inside = (key_positions >= 0) & (key_positions < row_len)
    distance = own_positions[:, None] - key_positions[None, :]
    allowed = (jnp.abs(distance) <= margin) & inside[None, :]
    allowed = (allowed[None] & (query_docs[:, :, None] == key_docs[:, None, :]))[:, None]
    score_scale = HEAD_DIM ** (-0.5)
    head_shape = (row_count, own_len, HEADS, HEAD_DIM)
    inputs = tokens.astype(jnp.float32).reshape(row_count * own_len, model_width)
    normed_one = norm_rows(inputs, gain_first).astype(jnp.bfloat16)
    projected = jnp.dot(normed_one, attention_in, preferred_element_type=jnp.float32)
    cosine, sines = rotary_tables(own_positions)
    queries = rotate(projected[:, :model_width].reshape(head_shape), cosine, sines).astype(
        jnp.bfloat16
    )
    rotated_keys = rotate(
        projected[:, model_width : 2 * model_width].reshape(head_shape), cosine, sines
    ).astype(jnp.bfloat16)
    value_part = (
        projected[:, 2 * model_width :]
        .astype(jnp.bfloat16)
        .reshape(row_count, own_len, model_width)
    )
    key_value = jnp.concatenate(
        [rotated_keys.reshape(row_count, own_len, model_width), value_part], axis=2
    )
    wide_pairs = with_halo(key_value, (("seq", 1),), margin)
    wide_keys = wide_pairs[..., :model_width].reshape(row_count, keys_len, HEADS, HEAD_DIM)
    wide_values = wide_pairs[..., model_width:].reshape(row_count, keys_len, HEADS, HEAD_DIM)

    def score_table():
        raw = (
            jnp.einsum("mqhd,mkhd->mhqk", queries, wide_keys, preferred_element_type=jnp.float32)
            * score_scale
        )
        return jnp.where(allowed, raw, -jnp.inf)

    scores = score_table()
    row_max = jnp.max(scores, axis=-1, keepdims=True)
    weights = jnp.exp(scores - row_max)
    row_total = jnp.sum(weights, axis=-1, keepdims=True)
    prob_low = (weights / row_total).astype(jnp.bfloat16)
    attended = jnp.einsum(
        "mhqk,mkhd->mqhd", prob_low, wide_values, preferred_element_type=jnp.float32
    )
    attended_low = attended.reshape(row_count * own_len, model_width).astype(jnp.bfloat16)
    middle = inputs + jnp.dot(attended_low, attention_out, preferred_element_type=jnp.float32)
    normed_two = norm_rows(middle, gain_second).astype(jnp.bfloat16)
    gate_up = jnp.dot(normed_two, feedforward_in, preferred_element_type=jnp.float32)
    gate_half = gate_up[:, :hidden_width]
    lift_half = gate_up[:, hidden_width:]
    mixed = gated_gelu(gate_half, lift_half).astype(jnp.bfloat16)
    result = middle + jnp.dot(mixed, feedforward_out, preferred_element_type=jnp.float32)
    activations = result.astype(jnp.bfloat16).reshape(row_count, own_len, model_width)
    grad_top = result_grad.reshape(row_count * own_len, model_width)
    grad_down = jnp.einsum("tf,td->fd", mixed, grad_top, preferred_element_type=jnp.float32)
    grad_mixed = jnp.einsum(
        "td,fd->tf", grad_top, feedforward_out, preferred_element_type=jnp.float32
    )
    unused, gelu_pull = jax.vjp(gated_gelu, gate_half, lift_half)
    grad_gate, grad_lift = gelu_pull(grad_mixed)
    grad_gate_up = jnp.concatenate([grad_gate, grad_lift], axis=1).astype(jnp.bfloat16)
    grad_up_weight = jnp.einsum(
        "td,tf->df", normed_two, grad_gate_up, preferred_element_type=jnp.float32
    )
    grad_normed_two = jnp.einsum(
        "tf,df->td", grad_gate_up, feedforward_in, preferred_element_type=jnp.float32
    )
    unused, norm_pull = jax.vjp(norm_rows, middle, gain_second)
    grad_middle_norm, grad_gain_two = norm_pull(grad_normed_two)
    grad_middle = grad_top.astype(jnp.float32) + grad_middle_norm
    second_sums = (grad_up_weight, grad_down, grad_gain_two)
    grad_branch = grad_middle.astype(jnp.bfloat16)
    grad_out_weight = jnp.einsum(
        "td,te->de", attended_low, grad_branch, preferred_element_type=jnp.float32
    )
    grad_attended = jnp.einsum(
        "te,de->td", grad_branch, attention_out, preferred_element_type=jnp.float32
    )
    grad_attended = grad_attended.astype(jnp.bfloat16).reshape(head_shape)
    probabilities = jnp.exp(score_table() - row_max) / row_total
    prob_again = probabilities.astype(jnp.bfloat16)
    grad_wide_values = jnp.einsum(
        "mhqk,mqhd->mkhd", prob_again, grad_attended, preferred_element_type=jnp.float32
    )
    grad_probs = jnp.einsum(
        "mqhd,mkhd->mhqk", grad_attended, wide_values, preferred_element_type=jnp.float32
    )
    inner_sum = jnp.sum(probabilities * grad_probs, axis=-1, keepdims=True)
    grad_scores = (probabilities * (grad_probs - inner_sum)).astype(jnp.bfloat16) * score_scale
    grad_queries = jnp.einsum(
        "mhqk,mkhd->mqhd", grad_scores, wide_keys, preferred_element_type=jnp.float32
    )
    grad_wide_keys = jnp.einsum(
        "mhqk,mqhd->mkhd", grad_scores, queries, preferred_element_type=jnp.float32
    )
    grad_wide = jnp.concatenate(
        [
            grad_wide_keys.reshape(row_count, keys_len, model_width),
            grad_wide_values.reshape(row_count, keys_len, model_width),
        ],
        axis=2,
    )
    from_below = shifted_2(grad_wide[:, own_len + margin :].astype(jnp.bfloat16), "seq", 1).astype(
        jnp.float32
    )
    from_above = shifted_2(grad_wide[:, :margin].astype(jnp.bfloat16), "seq", -1).astype(
        jnp.float32
    )
    grad_pairs = grad_wide[:, margin : margin + own_len]
    grad_pairs = grad_pairs.at[:, :margin].add(from_below)
    grad_pairs = grad_pairs.at[:, own_len - margin :].add(from_above)
    grad_keys = rotate_back(grad_pairs[..., :model_width].reshape(head_shape), cosine, sines)
    grad_queries = rotate_back(grad_queries, cosine, sines)
    grad_projected = jnp.concatenate(
        [
            grad_queries.reshape(row_count * own_len, model_width),
            grad_keys.reshape(row_count * own_len, model_width),
            grad_pairs[..., model_width:].reshape(row_count * own_len, model_width),
        ],
        axis=1,
    ).astype(jnp.bfloat16)
    grad_in_weight = jnp.einsum(
        "td,tf->df", normed_one, grad_projected, preferred_element_type=jnp.float32
    )
    grad_normed_one = jnp.einsum(
        "tf,df->td", grad_projected, attention_in, preferred_element_type=jnp.float32
    )
    unused, first_pull = jax.vjp(norm_rows, inputs, gain_first)
    grad_input_norm, grad_gain_one = first_pull(grad_normed_one)
    grad_tokens = (grad_middle + grad_input_norm).reshape(row_count, own_len, model_width)
    totals = lax.psum(
        (
            grad_in_weight,
            grad_out_weight,
            second_sums[0],
            second_sums[1],
            grad_gain_one,
            second_sums[2],
        ),
        ("dp", "seq"),
    )
    return (
        activations,
        grad_tokens,
        totals[0],
        totals[1],
        totals[2],
        totals[3],
        totals[4],
        totals[5],
    )


def solution(mesh):
    placed = (
        P("dp", "seq", None),
        P("dp", None),
        P(),
        P(),
        P(),
        P(),
        P(),
        P(),
        P("dp", "seq", None),
    )
    return jax.shard_map(
        shards,
        mesh=mesh,
        in_specs=placed,
        out_specs=(P("dp", "seq", None), P("dp", "seq", None), P(), P(), P(), P(), P(), P()),
        check_vma=False,
    )
```

profile of v0, /device:TPU:0, one launch (start us, length us, event | category | flops | bytes accessed | tf_op | source)
XLA Modules:
  0.0 639.5 jit_solution(14629376139584641251)
XLA Ops:
  12.6 2.7 fusion.86
  16.7 3.4 fusion.79
  20.3 2.6 copy.73
  22.9 3.5 copy.71
  26.5 3.5 copy.70
  30.0 4.8 reshape.351
  34.9 2.6 slice_negate_fusion
  43.5 2.4 copy.75
  47.2 2.4 copy.74
  49.6 6.5 %collective-permute-start = (bf16[6,64,1024]{2,1,0:T(8,128)(2,1)}, bf16[6,64,1024]{2,1,0:T(8,128)(2,1)}, u32[]{:S(2)}, u32[]{:S(2)}) collective-permute-start(bf16[6,64,1024]{2,1,0:T(8,128)(2,1)} %copy.74), channel_id=1, source_target_pairs={{0,1},{1,2},{2,3},{3,4},{4,5},{5,6},{6,7},{8,9},{9,10},{10,11},{11... | collective-permute-start | bytes 2359304 | tf_op jit(solution)/shard_map/ppermute | solution.py:20
  58.2 3.1 copy.101
  61.4 5.6 reshape.366
  66.9 6.1 copy.79
  73.0 2.4 slice_negate_fusion.3
  77.9 2.4 copy.77
  80.4 5.3 collective-permute-done
  85.6 2.4 copy.76
  88.1 5.4 pad_maximum_fusion.1
  93.5 2.7 fusion.81
  96.2 11.8 %fusion.84 = (f32[6,8,256]{2,1,0:T(8,128)S(1)}, f32[6,8,256,384]{3,2,1,0:T(8,128)}) fusion(pred[6,256,384]{2,1,0:T(8,128)(4,1)} %compare_and_fusion, bf16[6,256,8,64]{1,3,2,0:T(8,128)(2,1)} %fusion.37, bf16[6,384,8,64]{1,3,2,0:T(8,128)(2,1)} %bitcast.121), kind=kOutput, calls=%fused_computation.148 | convolution fusion | flops 622854528 | bytes 23445504 | tf_op jit(solution)/shard_map/sub | solution.py:127
  108.1 9.6 %fusion.57 = bf16[6,256,8,64]{1,3,2,0:T(8,128)(2,1)S(1)} fusion(bf16[6,384,8,64]{1,3,2,0:T(8,128)(2,1)} %bitcast.105, f32[6,8,256,384]{3,2,1,0:T(8,128)} %get-tuple-element.69, f32[6,8,256]{2,1,0:T(8,128)S(1)} %get-tuple-element.68), kind=kOutput, calls=%fused_computation.107 | convolution fusion | flops 614203392 | bytes 22855680 | tf_op jit(solution)/shard_map/mhqk,mkhd->mqhd/dot_general | solution.py:130
  121.1 2.9 fusion.76
  124.1 12.1 %add_convert_fusion = (bf16[1536,768]{0,1:T(8,128)(2,1)S(1)}, f32[1536,768]{0,1:T(8,128)S(1)}, f32[1536,768]{0,1:T(8,128)S(1)}) fusion(f32[1536,1536]{0,1:T(8,128)S(1)} %fusion.76, bf16[1536,512]{1,0:T(8,128)(2,1)S(1)} %bitcast.114, bf16[768,512]{1,0:T(8,128)(2,1)S(1)} %copy-done.54), kind=kOutput, calls=%fused_computation.33 | convolution fusion | flops 1294073856 | bytes 23592960 | tf_op jit(solution)/shard_map/td,fd->tf/dot_general | solution.py:144
  136.2 3.8 multiply_convert_fusion.1
  140.0 4.9 fusion.41
  144.8 4.6 multiply_reduce_fusion.1
  153.9 3.0 reshape.367
  156.9 3.4 copy.84
  160.4 10.0 %fusion.31 = f32[6,8,64,384]{3,2,1,0:T(8,128)} fusion(bf16[6,256,8,64]{1,3,2,0:T(8,128)(2,1)S(1)} %copy.84, f32[6,8,256,384]{3,2,1,0:T(8,128)} %get-tuple-element.69, f32[6,8,256]{2,1,0:T(8,128)S(1)} %get-tuple-element.68), kind=kOutput, calls=%fused_computation.47 | convolution fusion | flops 613416960 | bytes 25214976 | tf_op jit(solution)/shard_map/mhqk,mqhd->mkhd/dot_general | solution.py:170
  170.3 8.1 %fusion.87 = f32[6,8,256,384]{3,2,1,0:T(8,128)} fusion(bf16[6,256,8,64]{1,3,2,0:T(8,128)(2,1)S(1)} %copy.84, bf16[6,384,8,64]{1,3,2,0:T(8,128)(2,1)S(1)} %bitcast.106), kind=kOutput, calls=%fused_computation.151 | convolution fusion | flops 603979776 | bytes 22806528 | tf_op jit(solution)/shard_map/mqhd,mkhd->mhqk/dot_general | solution.py:173
  178.4 85.6 %fusion.12 = f32[6,8,64,256]{3,2,1,0:T(8,128)} fusion(bf16[6,384,8,64]{1,3,2,0:T(8,128)(2,1)} %bitcast.122, f32[6,8,256,384]{3,2,1,0:T(8,128)} %fusion.87, f32[6,8,256,384]{3,2,1,0:T(8,128)} %get-tuple-element.69, f32[6,8,256]{2,1,0:T(8,128)S(1)} %get-tuple-element.68), kind=kOutput, calls=%fused_computation.20 | convolution fusion | flops 651178368 | bytes 43302912 | tf_op jit(solution)/shard_map/mhqk,mkhd->mqhd/dot_general | solution.py:178
  264.0 76.8 %fusion.10 = f32[6,8,64,384]{3,2,1,0:T(8,128)} fusion(bf16[6,256,8,64]{1,3,2,0:T(8,128)(2,1)S(1)} %copy-done.32, f32[6,8,256,384]{3,2,1,0:T(8,128)} %fusion.87, f32[6,8,256,384]{3,2,1,0:T(8,128)} %get-tuple-element.69, f32[6,8,256]{2,1,0:T(8,128)S(1)} %get-tuple-element.68), kind=kOutput, calls=%fused_computation.18 | convolution fusion | flops 651178368 | bytes 44089344 | tf_op jit(solution)/shard_map/mhqk,mqhd->mkhd/dot_general | solution.py:181
  340.8 6.1 copy.88
  346.8 6.2 copy.87
  353.0 6.9 %fusion.6 = bf16[6,384,1024]{2,1,0:T(8,128)(2,1)} fusion(f32[6,384,512]{2,1,0:T(8,128)} %copy.88, f32[6,384,512]{2,1,0:T(8,128)} %copy.87), kind=kLoop, calls=%fused_computation.13 | loop fusion | flops 9437184 | bytes 14155776 | tf_op jit(solution)/shard_map/convert.7
  361.7 4.7 collective-permute-start.2
  371.0 2.5 fusion.89
  373.5 26.6 %collective-permute-done.2 = bf16[6,64,1024]{2,1,0:T(8,128)(2,1)S(1)} collective-permute-done((bf16[6,64,1024]{2,1,0:T(8,128)(2,1)S(1)}, bf16[6,64,1024]{2,1,0:T(8,128)(2,1)S(1)}, u32[]{:S(2)}, u32[]{:S(2)}) %collective-permute-start.2) | collective-permute-done | bytes 786464 | tf_op jit(solution)/shard_map/ppermute | solution.py:31
  404.8 3.6 copy.91
  408.4 3.5 copy.90
  412.0 3.6 bitcast_multiply_fusion
  427.3 6.6 %fusion.45 = f32[512,1536]{1,0:T(8,128)} fusion(bf16[1536,512]{1,0:T(8,128)(2,1)S(1)} %copy-done.29, bf16[1536,512]{0,1:T(8,128)(2,1)S(1)} %copy-done.25, bf16[1536,512]{0,1:T(8,128)(2,1)S(1)} %add_convert_fusion.1, bf16[1536,512]{0,1:T(8,128)(2,1)S(1)} %bitcast.125), kind=kOutput, calls=%fused_computation.92 | convolution fusion | flops 2430074880 | bytes 9437184 | tf_op jit(solution)/shard_map/td,tf->df/dot_general | solution.py:210
  434.0 5.6 fusion.43
  439.6 3.4 multiply_reduce_fusion.3
  446.5 43.5 %all-reduce = (f32[512]{0:T(512)}, f32[512]{0:T(512)}) all-reduce(f32[512]{0:T(512)S(1)} %get-tuple-element.34, f32[512]{0:T(512)S(1)} %copy-done.50), channel_id=1, replica_groups=mesh['dp'=4,'seq'=8] {'dp','seq'}, use_global_device_ids=true, to_apply=%region_18.19 | all-reduce | flops 1024 | bytes 8192 | tf_op jit(solution)/shard_map/psum | solution.py:219
  490.0 4.7 add_add_fusion.2
  494.7 128.9 %all-reduce.4.cloned.1.call-done = (f32[512,1536]{1,0:T(8,128)}, f32[512,512]{1,0:T(8,128)}, f32[512,1536]{1,0:T(8,128)}, f32[768,512]{1,0:T(8,128)}) async-done(((f32[512,1536]{1,0:T(8,128)}, f32[512,512]{1,0:T(8,128)}, f32[512,1536]{1,0:T(8,128)}, f32[768,512]{1,0:T(8,128)}), (f32[512,1536]{1,0:T(8,128)}, f32[512,512]{1,0:T(8,128)}, f32[512,1536]{1,0:T(8,128)}, ...) | async-done | bytes 8912912 | tf_op jit(solution)/shard_map/psum | solution.py:219
  623.6 3.9 copy.109
  (182 shorter events, 57.3 us)
Async XLA Ops:
  7.2 113.9 %copy-start = (bf16[512,1536]{1,0:T(8,128)(2,1)S(1)}, bf16[512,1536]{1,0:T(8,128)(2,1)}, u32[]{:S(2)}) copy-start(bf16[512,1536]{1,0:T(8,128)(2,1)} %param.17) | copy-start | bytes 4718596
  7.2 4.7 copy-start.3
  7.2 4.7 copy-start.47
  7.2 616.4 %all-reduce.4.cloned.1.call-start = ((), (), s32[]{:S(2)}) async-start(), calls=%async_computation | async-start | bytes 17825792 | tf_op jit(solution)/shard_map/psum | solution.py:219
  9.1 6.2 copy-start.39
  11.2 4.1 copy-start.45
  12.6 2.7 copy-start.28
  20.3 55.2 %copy-start.23 = (f32[256,64]{0,1:T(8,128)}, f32[256,64]{0,1:T(8,128)S(1)}, u32[]{:S(2)}) copy-start(f32[256,64]{0,1:T(8,128)S(1)} %get-tuple-element.66) | copy-start | bytes 196612
  20.3 55.2 %copy-start.35 = (f32[256,64]{0,1:T(8,128)}, f32[256,64]{0,1:T(8,128)S(1)}, u32[]{:S(2)}) copy-start(f32[256,64]{0,1:T(8,128)S(1)} %get-tuple-element.67) | copy-start | bytes 196612
  41.1 2.4 copy-start.9
  43.5 12.7 %copy-start.49 = (s32[6,16]{1,0:T(8,128)S(1)}, s32[6,16]{1,0:T(8,128)}, u32[]{:S(2)}) copy-start(s32[6,16]{1,0:T(8,128)} %param.14) | copy-start | bytes 1156
  45.9 32.0 %collective-permute-start.1 = (bf16[6,64,1024]{2,1,0:T(8,128)(2,1)}, bf16[6,64,1024]{2,1,0:T(8,128)(2,1)}, u32[]{:S(2)}, u32[]{:S(2)}) collective-permute-start(bf16[6,64,1024]{2,1,0:T(8,128)(2,1)} %copy.75), channel_id=1, source_target_pairs={{1,0},{2,1},{3,2},{4,3},{5,4},{6,5},{7,6},{9,8},{10,9},{11,10},{12... | collective-permute-start | bytes 2359304 | tf_op jit(solution)/shard_map/ppermute | solution.py:23
  49.6 36.0 %collective-permute-start = (bf16[6,64,1024]{2,1,0:T(8,128)(2,1)}, bf16[6,64,1024]{2,1,0:T(8,128)(2,1)}, u32[]{:S(2)}, u32[]{:S(2)}) collective-permute-start(bf16[6,64,1024]{2,1,0:T(8,128)(2,1)} %copy.74), channel_id=1, source_target_pairs={{0,1},{1,2},{2,3},{3,4},{4,5},{5,6},{6,7},{8,9},{9,10},{10,11},{11... | collective-permute-start | bytes 2359304 | tf_op jit(solution)/shard_map/ppermute | solution.py:20
  73.0 2.8 copy-start.7
  120.4 29.1 %copy-start.5 = (f32[1536,512]{1,0:T(8,128)}, f32[1536,512]{1,0:T(8,128)S(1)}, u32[]{:S(2)}) copy-start(f32[1536,512]{1,0:T(8,128)S(1)} %get-tuple-element.71) | copy-start | bytes 9437188
  121.1 3.0 copy-start.18
  121.1 3.0 copy-start.54
  160.3 10.0 %copy-start.10 = (bf16[6,384,512]{1,2,0:T(8,128)(2,1)S(1)}, bf16[6,384,512]{1,2,0:T(8,128)(2,1)}, u32[]{:S(2)}) copy-start(bf16[6,384,512]{1,2,0:T(8,128)(2,1)} %get-tuple-element.53) | copy-start | bytes 7077892
  178.4 85.6 %copy-start.32 = (bf16[6,256,8,64]{1,3,2,0:T(8,128)(2,1)S(1)}, bf16[6,256,8,64]{1,3,2,0:T(8,128)(2,1)}, u32[]{:S(2)}) copy-start(bf16[6,256,8,64]{1,3,2,0:T(8,128)(2,1)} %fusion.37) | copy-start | bytes 4718596
  346.8 23.3 %slice-start = ((s8[4718592]{0:T(1024)(128)(4,1)}), s8[524288]{0:T(1024)(128)(4,1)S(1)}, s32[]{:S(2)}) async-start(s8[4718592]{0:T(1024)(128)(4,1)} %bitcast.98), calls=%async_computation.1 | async-start | bytes 1048576
  353.0 17.1 %slice-start.1 = ((s8[4718592]{0:T(1024)(128)(4,1)}), s8[4194304]{0:T(1024)(128)(4,1)S(1)}, s32[]{:S(2)}) async-start(s8[4718592]{0:T(1024)(128)(4,1)} %bitcast.98), calls=%async_computation.2 | async-start | bytes 8388608
  359.9 6.5 %copy-start.12 = (bf16[64,8,6,256]{3,1,2,0:T(8,128)(2,1)S(1)}, bf16[64,8,6,256]{3,1,2,0:T(8,128)(2,1)}, u32[]{:S(2)}) copy-start(bf16[64,8,6,256]{3,1,2,0:T(8,128)(2,1)} %copy-done.11) | copy-start | bytes 4718596
  359.9 6.5 %copy-start.31 = (bf16[1536,512]{1,0:T(8,128)(2,1)S(1)}, bf16[1536,512]{1,0:T(8,128)(2,1)}, u32[]{:S(2)}) copy-start(bf16[1536,512]{1,0:T(8,128)(2,1)} %copy-done.30) | copy-start | bytes 4718596
  361.7 8.5 %copy-start.2 = (f32[6,384,512]{2,1,0:T(8,128)S(1)}, f32[6,384,512]{2,1,0:T(8,128)}, u32[]{:S(2)}) copy-start(f32[6,384,512]{2,1,0:T(8,128)} %copy.87) | copy-start | bytes 14155780
  361.7 38.5 %collective-permute-start.2 = (bf16[6,64,1024]{2,1,0:T(8,128)(2,1)S(1)}, bf16[6,64,1024]{2,1,0:T(8,128)(2,1)S(1)}, u32[]{:S(2)}, u32[]{:S(2)}) collective-permute-start(bf16[6,64,1024]{2,1,0:T(8,128)(2,1)S(1)} %get-tuple-element.51), channel_id=1, source_target_pairs={{0,1},{1,2},{2,3},{3,4},{4,5},{5,6},{6,7},{8,9},{9,10},{10,11},{11... | collective-permute-start | bytes 2359304 | tf_op jit(solution)/shard_map/ppermute | solution.py:31
  368.3 2.7 copy-start.19
  368.3 2.7 copy-start.22
  368.3 32.1 %collective-permute-start.3 = (bf16[6,64,1024]{2,1,0:T(8,128)(2,1)S(1)}, bf16[6,64,1024]{2,1,0:T(8,128)(2,1)S(1)}, u32[]{:S(2)}, u32[]{:S(2)}) collective-permute-start(bf16[6,64,1024]{2,1,0:T(8,128)(2,1)S(1)} %get-tuple-element.50), channel_id=1, source_target_pairs={{1,0},{2,1},{3,2},{4,3},{5,4},{6,5},{7,6},{9,8},{10,9},{11,10},{12... | collective-permute-start | bytes 2359304 | tf_op jit(solution)/shard_map/ppermute | solution.py:31
  408.4 3.6 copy-start.36
  415.5 1.9 copy-start.16
  422.2 2.8 copy-start.15
  425.0 2.3 copy-start.25
  425.0 2.3 copy-start.29
  433.9 5.6 copy-start.4
  433.9 5.6 copy-start.26
  434.0 5.6 copy-start.34
  434.0 5.6 copy-start.40
  434.0 5.6 copy-start.48
  434.0 5.6 copy-start.53
  439.6 3.5 copy-start.46
  439.6 5.1 copy-start.42
  443.1 3.4 copy-start.50
  443.1 46.9 %copy-start.20 = (bf16[6,256,512]{2,1,0:T(8,128)(2,1)S(1)}, bf16[6,256,512]{2,1,0:T(8,128)(2,1)}, u32[]{:S(2)}) copy-start(bf16[6,256,512]{2,1,0:T(8,128)(2,1)} %param.21) | copy-start | bytes 4718596
  443.1 46.9 %copy-start.44 = (f32[1536]{0:T(1024)S(1)}, f32[1536]{0:T(1024)}, u32[]{:S(2)}) copy-start(f32[1536]{0:T(1024)} %copy-done.43) | copy-start | bytes 18436
  623.6 3.9 copy-start.37
  623.6 4.9 copy-start.21
  628.5 2.5 copy-start.27
  628.5 3.7 copy-start.1
  (14 other events, 19.8 us)
Sparse Core Ops, SparseCore 0:
  434.1 189.5 all-reduce.3
where the time goes:
time: 648 us; the launch traced here: 639 us
  matrix products  251 us (39%)
  waiting for transfers between devices  161 us (25%)
  local copies, waits for them, and re-layouts  104 us (16%)
  other arithmetic  50.2 us (8%)
  blocking collectives  43.5 us (7%)
  between operations  15.4 us (2%)
  starting transfers between devices  14.3 us (2%)
    psum x1, waiting for transfers between devices, shards(): lax.psum((grad_in_weight, grad_out_weight, second_sums[0], second_sums[1]...  129 us
    dot_general x1, matrix products, shards(): jnp.einsum('mhqk,mkhd->mqhd', grad_scores, wide_keys, preferred_element_t...  85.6 us
    dot_general x1, matrix products, shards(): jnp.einsum('mhqk,mqhd->mkhd', grad_scores, queries, preferred_element_typ...  76.8 us
    psum x1, blocking collectives, shards(): lax.psum((grad_in_weight, grad_out_weight, second_sums[0], second_sums[1]...  43.5 us
    ppermute x2, waiting for transfers between devices, shifted_2(): return lax.ppermute(block, axis, route)  26.6 us
    unnamed x122, local copies, waits for them, and re-layouts  23.8 us
  transfers between devices with their start and end apart: 5, of which 3 were waited for; matrix products, arithmetic and copies ran while one was open for 7% of the time, Pallas kernels for 0%

commit v1 on v0

v1 whole, which is shorter than its diff:
```python
import functools

import jax
import jax.numpy as jnp
from jax import lax
from jax.experimental import pallas as pl
from jax.experimental.pallas import tpu as pltpu
from jax.sharding import PartitionSpec as P

HEADS = 8
HEAD_DIM = 64
HALF_WIN = 64
EPSILON = 1e-05
ROTARY_BASE = 10000.0
SCALE = HEAD_DIM**-0.5
BLOCKS = 32
GROUP = 4
WIDE = GROUP * HEAD_DIM
VMEM = 56 * 1024 * 1024

F32 = jnp.float32
BF16 = jnp.bfloat16


def dot(a, b, contract):
    return lax.dot_general(a, b, ((contract[:1], contract[1:]), ((), ())), preferred_element_type=F32)


def nn(a, b):
    return dot(a, b, (1, 0))


def nt(a, b):
    return dot(a, b, (1, 1))


def tn(a, b):
    return dot(a, b, (0, 0))


def normalize(values):
    shifted = values - jnp.mean(values, axis=-1, keepdims=True)
    inverse = lax.rsqrt(jnp.mean(shifted * shifted, axis=-1, keepdims=True) + EPSILON)
    return shifted * inverse, inverse


def norm_back(scaled_grad, unit, inverse):
    return (
        scaled_grad
        - jnp.mean(scaled_grad, axis=-1, keepdims=True)
        - unit * jnp.mean(scaled_grad * unit, axis=-1, keepdims=True)
    ) * inverse


def half_swap(values):
    lane = lax.broadcasted_iota(jnp.int32, values.shape, 1)
    return jnp.where(lane % HEAD_DIM < HEAD_DIM // 2, pltpu.roll(values, 96, 1), pltpu.roll(values, 32, 1))


def rotate(values, cosine, sines):
    parts = [values[:, c : c + 128] for c in range(0, values.shape[1], 128)]
    return jnp.concatenate([p * cosine + half_swap(p) * sines for p in parts], axis=1)


def rotate_back(values, cosine, sines):
    parts = [values[:, c : c + 128] for c in range(0, values.shape[1], 128)]
    return jnp.concatenate([p * cosine - half_swap(p) * sines for p in parts], axis=1)


def doc_ids(starts_ref, row, positions):
    total = jnp.zeros(positions.shape, jnp.int32)
    for j in range(starts_ref.shape[1]):
        total += (positions >= starts_ref[row, j]).astype(jnp.int32)
    return total


def mask_bias(starts_ref, row, first_query, queries, first_key, keys, row_len, turned):
    q_dim, shape = (1, (keys, queries)) if turned else (0, (queries, keys))
    q_shape = (1, queries) if turned else (queries, 1)
    k_shape = (keys, 1) if turned else (1, keys)
    q_pos = first_query + lax.broadcasted_iota(jnp.int32, q_shape, q_dim)
    k_pos = first_key + lax.broadcasted_iota(jnp.int32, k_shape, 1 - q_dim)
    q_doc = doc_ids(starts_ref, row, q_pos)
    k_doc = jnp.where(k_pos < row_len, doc_ids(starts_ref, row, k_pos), -1)
    distance = (
        lax.broadcasted_iota(jnp.int32, shape, q_dim)
        - lax.broadcasted_iota(jnp.int32, shape, 1 - q_dim)
        + (first_query - first_key)
    )
    allowed = (jnp.abs(distance) <= HALF_WIN) & (q_doc == k_doc)
    return jnp.where(allowed, 0.0, -jnp.inf)


def by_head(values):
    head = lax.broadcasted_iota(jnp.int32, values.shape, 1) // HEAD_DIM
    zero = jnp.zeros_like(values)
    return jnp.concatenate([jnp.where(head == h, values, zero) for h in range(GROUP)], axis=0)


def pick_heads(stacked, count):
    head = lax.broadcasted_iota(jnp.int32, (count, stacked.shape[1]), 1) // HEAD_DIM
    out = stacked[:count]
    for h in range(1, GROUP):
        out = jnp.where(head == h, stacked[h * count : (h + 1) * count], out)
    return out


def attend(queries, keys, values, bias):
    count = queries.shape[0]
    outs = []
    for c in range(0, queries.shape[1], WIDE):
        scores = nt(by_head(queries[:, c : c + WIDE]), keys[:, c : c + WIDE])
        probs = []
        for h in range(GROUP):
            part = scores[h * count : (h + 1) * count] + bias
            part = jnp.exp(part - jnp.max(part, axis=-1, keepdims=True))
            probs.append((part * (1.0 / jnp.sum(part, axis=-1, keepdims=True))).astype(BF16))
        outs.append(pick_heads(nn(jnp.concatenate(probs, axis=0), values[:, c : c + WIDE]), count))
    return jnp.concatenate(outs, axis=1).astype(BF16)


def gelu_parts(gate):
    bell = jnp.exp(-0.5 * gate * gate)
    t = 1.0 / (1.0 + (0.3275911 * 0.7071067811865476) * jnp.abs(gate))
    tail = t * (
        0.5 * 0.254829592
        + t * (0.5 * -0.284496736 + t * (0.5 * 1.421413741 + t * (0.5 * -1.453152027 + t * (0.5 * 1.061405429))))
    )
    tail = tail * bell
    return jnp.where(gate < 0, tail, 1.0 - tail), gate * bell * 0.3989422804014327


def dense_chain(inputs, attended, top, out_ref, up_ref, down_ref, gain_two, sums):
    sum_up, sum_down, sum_out = sums
    hidden = down_ref.shape[0]
    middle = inputs + nn(attended, out_ref[...])
    unit, inverse = normalize(middle)
    normed = (unit * gain_two).astype(BF16)
    result = middle
    grad_normed = None
    for c in range(0, hidden, 256):
        gate = nn(normed, up_ref[:, c : c + 256])
        lift = nn(normed, up_ref[:, hidden + c : hidden + c + 256])
        grad_mixed = nt(top, down_ref[c : c + 256])
        phi, slope = gelu_parts(gate)
        active = gate * phi
        mixed = (active * lift).astype(BF16)
        grad_gate = (grad_mixed * lift * (phi + slope)).astype(BF16)
        grad_lift = (grad_mixed * active).astype(BF16)
        result = result + nn(mixed, down_ref[c : c + 256])
        part = nt(grad_gate, up_ref[:, c : c + 256]) + nt(grad_lift, up_ref[:, hidden + c : hidden + c + 256])
        grad_normed = part if grad_normed is None else grad_normed + part
        sum_down[c : c + 256] += tn(mixed, top)
        sum_up[:, c : c + 256] += tn(normed, grad_gate)
        sum_up[:, hidden + c : hidden + c + 256] += tn(normed, grad_lift)
    grad_middle = top.astype(F32) + norm_back(grad_normed * gain_two, unit, inverse)
    branch = grad_middle.astype(BF16)
    sum_out[...] += tn(attended, branch)
    return result.astype(BF16), grad_middle, nt(branch, out_ref[...]).astype(BF16)


def first_kernel(
    own_len,
    place_ref,
    starts_ref,
    tokens_ref,
    top_ref,
    in_ref,
    out_ref,
    up_ref,
    down_ref,
    gains_ref,
    cos_ref,
    sin_ref,
    normed_ref,
    queries_ref,
    keys_ref,
    values_ref,
    result_ref,
    grad_middle_ref,
    grad_attended_ref,
    sum_up,
    sum_down,
    sum_out,
):
    step = pl.program_id(0)
    pair, _, width = tokens_ref.shape
    lo, hi = HALF_WIN, own_len - HALF_WIN

    @pl.when(step == 0)
    def _():
        for ref in (sum_up, sum_down, sum_out):
            ref[...] = jnp.zeros_like(ref)

    cosine, sines = cos_ref[...], sin_ref[...]
    attended, inputs, tops = [], [], []
    for r in range(pair):
        row_inputs = tokens_ref[r].astype(F32)
        unit, _ = normalize(row_inputs)
        normed = (unit * gains_ref[0:1]).astype(BF16)
        normed_ref[r] = normed
        queries = (rotate(nn(normed, in_ref[:, :width]), cosine, sines) * SCALE).astype(BF16)
        keys = rotate(nn(normed, in_ref[:, width : 2 * width]), cosine, sines).astype(BF16)
        values = nn(normed, in_ref[:, 2 * width :]).astype(BF16)
        queries_ref[r] = queries
        keys_ref[r] = keys
        values_ref[r] = values
        bias = mask_bias(
            starts_ref, step * pair + r, place_ref[0] + lo, hi - lo, place_ref[0], own_len, place_ref[1], False
        )
        attended.append(attend(queries[lo:hi], keys, values, bias))
        inputs.append(row_inputs[lo:hi])
        tops.append(top_ref[r, lo:hi])
    result, grad_middle, grad_attended = dense_chain(
        jnp.concatenate(inputs, axis=0),
        jnp.concatenate(attended, axis=0),
        jnp.concatenate(tops, axis=0),
        out_ref,
        up_ref,
        down_ref,
        gains_ref[1:2],
        (sum_up, sum_down, sum_out),
    )
    shape = (pair, hi - lo, width)
    result_ref[...] = result.reshape(shape)
    grad_middle_ref[...] = grad_middle.reshape(shape)
    grad_attended_ref[...] = grad_attended.reshape(shape)


def second_kernel(
    own_len,
    place_ref,
    starts_ref,
    tokens_ref,
    low_ref,
    high_ref,
    top_ref,
    queries_ref,
    keys_ref,
    values_ref,
    in_ref,
    out_ref,
    up_ref,
    down_ref,
    gains_ref,
    cos_ref,
    sin_ref,
    begun_up,
    begun_down,
    begun_out,
    normed_ref,
    halo_keys_ref,
    halo_values_ref,
    result_ref,
    grad_middle_ref,
    grad_attended_ref,
    keep_ref,
    send_ref,
    sum_up,
    sum_down,
    sum_out,
):
    step = pl.program_id(0)
    pair, _, width = tokens_ref.shape
    win = HALF_WIN
    hidden = down_ref.shape[0]

    @pl.when(step == 0)
    def _():
        sum_up[...] = begun_up[...]
        sum_down[...] = begun_down[...]
        sum_out[...] = begun_out[...]

    cosine, sines = cos_ref[...], sin_ref[...]
    attended, inputs, tops = [], [], []
    for r in range(pair):
        unit, _ = normalize(jnp.concatenate([low_ref[r], high_ref[r]], axis=0).astype(F32))
        normed = (unit * gains_ref[0:1]).astype(BF16)
        keys = rotate(nn(normed, in_ref[:, width : 2 * width]), cosine, sines).astype(BF16)
        values = nn(normed, in_ref[:, 2 * width :]).astype(BF16)
        for side in range(2):
            part = slice(side * win, (side + 1) * win)
            normed_ref[r, side] = normed[part]
            halo_keys_ref[r, side] = keys[part]
            halo_values_ref[r, side] = values[part]
        for side in range(2):
            own = slice(0, win) if side == 0 else slice(own_len - win, own_len)
            first_query = place_ref[0] + own.start
            if side == 0:
                wide_keys = jnp.concatenate([keys[:win], keys_ref[r, : 2 * win]], axis=0)
                wide_values = jnp.concatenate([values[:win], values_ref[r, : 2 * win]], axis=0)
            else:
                wide_keys = jnp.concatenate([keys_ref[r, own_len - 2 * win :], keys[win:]], axis=0)
                wide_values = jnp.concatenate([values_ref[r, own_len - 2 * win :], values[win:]], axis=0)
            bias = mask_bias(
                starts_ref, step * pair + r, first_query, win, first_query - win, 3 * win, place_ref[1], False
            )
            attended.append(attend(queries_ref[r, own], wide_keys, wide_values, bias))
            inputs.append(tokens_ref[r, own].astype(F32))
            tops.append(top_ref[r, own])
    result, grad_middle, grad_attended = dense_chain(
        jnp.concatenate(inputs, axis=0),
        jnp.concatenate(attended, axis=0),
        jnp.concatenate(tops, axis=0),
        out_ref,
        up_ref,
        down_ref,
        gains_ref[1:2],
        (sum_up, sum_down, sum_out),
    )
    shape = (pair, 2, win, width)
    result_ref[...] = result.reshape(shape)
    grad_middle_ref[...] = grad_middle.reshape(shape)
    grad_attended_ref[...] = grad_attended.reshape(shape)

    @pl.when(step == pl.num_programs(0) - 1)
    def _():
        rows = width // BLOCKS
        for ref, base in ((keep_ref, 0), (send_ref, BLOCKS // 2)):

            @pl.loop(0, BLOCKS // 2)
            def _(i):
                block = place_ref[2] ^ (i + base)
                own_rows = pl.ds(pl.multiple_of(block * rows, rows), rows)
                for c in range(up_ref.shape[1] // width):
                    ref[i, c * rows : (c + 1) * rows] = sum_up[own_rows, c * width : (c + 1) * width].astype(BF16)
                at = up_ref.shape[1] // width * rows
                ref[i, at : at + rows] = sum_out[own_rows, :].astype(BF16)
                down_rows = hidden // BLOCKS
                ref[i, at + rows :] = sum_down[
                    pl.ds(pl.multiple_of(block * down_rows, down_rows), down_rows), :
                ].astype(BF16)


def third_kernel(
    own_len,
    place_ref,
    starts_ref,
    queries_ref,
    keys_ref,
    values_ref,
    halo_keys_ref,
    halo_values_ref,
    normed_ref,
    halo_normed_ref,
    mid_grad_ref,
    out_grad_ref,
    in_ref,
    cos_ref,
    sin_ref,
    own_ref,
    to_low_ref,
    to_high_ref,
    keep_ref,
    send_ref,
    sum_in,
):
    row = pl.program_id(0)
    width = queries_ref.shape[2]
    win = HALF_WIN
    count = own_len // 2
    span = count + 2 * win

    @pl.when(row == 0)
    def _():
        sum_in[...] = jnp.zeros_like(sum_in)

    keys = jnp.concatenate([halo_keys_ref[0, 0], keys_ref[0], halo_keys_ref[0, 1]], axis=0)
    values = jnp.concatenate([halo_values_ref[0, 0], values_ref[0], halo_values_ref[0, 1]], axis=0)
    normed = jnp.concatenate([halo_normed_ref[0, 0], normed_ref[0], halo_normed_ref[0, 1]], axis=0)
    grads = jnp.concatenate([out_grad_ref[0, 0], mid_grad_ref[0], out_grad_ref[0, 1]], axis=0)
    queries = queries_ref[0]
    biases = [
        mask_bias(
            starts_ref, row, place_ref[0] + b * count, count, place_ref[0] + b * count - win, span, place_ref[1], True
        )
        for b in range(2)
    ]
    cosine, sines = cos_ref[...], sin_ref[...]
    own = slice(win, win + own_len)
    grad_normed = jnp.zeros((own_len + 2 * win, width), F32)
    grad_own = jnp.zeros((own_len, width), F32)
    for c in range(0, width, WIDE):
        grad_keys, grad_values, grad_queries = [], [], []
        for b in range(2):
            k4 = keys[b * count : b * count + span, c : c + WIDE]
            v4 = values[b * count : b * count + span, c : c + WIDE]
            q4 = by_head(queries[b * count : (b + 1) * count, c : c + WIDE])
            g4 = by_head(grads[b * count : (b + 1) * count, c : c + WIDE])
            scores = nt(k4, q4)
            grad_probs = nt(v4, g4)
            lows, grad_scores = [], []
            for h in range(GROUP):
                cols = slice(h * count, (h + 1) * count)
                part = scores[:, cols] + biases[b]
                part = jnp.exp(part - jnp.max(part, axis=0, keepdims=True))
                part = part * (1.0 / jnp.sum(part, axis=0, keepdims=True))
                grad_part = grad_probs[:, cols]
                inner = jnp.sum(part * grad_part, axis=0, keepdims=True)
                lows.append(part.astype(BF16))
                grad_scores.append((part * (grad_part - inner)).astype(BF16))
            low = jnp.concatenate(lows, axis=1)
            grad_score = jnp.concatenate(grad_scores, axis=1)
            grad_values.append(nn(low, g4))
            grad_keys.append(nn(grad_score, q4))
            grad_queries.append(pick_heads(tn(grad_score, k4), count))

        def merge(parts):
            return jnp.concatenate(
                [parts[0][:count], parts[0][count:] + parts[1][: span - count], parts[1][span - count :]], axis=0
            )

        for part, at in ((merge(grad_keys), width), (merge(grad_values), 2 * width)):
            if at == width:
                part = rotate_back(part, cosine, sines)
            part = part.astype(BF16)
            sum_in[:, at + c : at + c + WIDE] += tn(normed, part)
            grad_normed = grad_normed + nt(part, in_ref[:, at + c : at + c + WIDE])
        part = jnp.concatenate(grad_queries, axis=0) * SCALE
        part = rotate_back(part, cosine[own], sines[own]).astype(BF16)
        sum_in[:, c : c + WIDE] += tn(normed[own], part)
        grad_own = grad_own + nt(part, in_ref[:, c : c + WIDE])
    own_ref[0] = grad_normed[own] + grad_own
    to_low_ref[0] = grad_normed[:win].astype(BF16)
    to_high_ref[0] = grad_normed[win + own_len :].astype(BF16)

    @pl.when(row == pl.num_programs(0) - 1)
    def _():
        rows = width // BLOCKS
        for ref, base in ((keep_ref, 0), (send_ref, BLOCKS // 2)):

            @pl.loop(0, BLOCKS // 2)
            def _(i):
                own_rows = pl.ds(pl.multiple_of((place_ref[2] ^ (i + base)) * rows, rows), rows)
                for c in range(in_ref.shape[1] // width):
                    ref[i, c * rows : (c + 1) * rows] = sum_in[own_rows, c * width : (c + 1) * width].astype(BF16)


def fourth_kernel(
    own_len,
    tokens_ref,
    own_ref,
    from_low_ref,
    from_high_ref,
    mid_grad_ref,
    out_grad_ref,
    gains_ref,
    mid_result_ref,
    out_result_ref,
    grad_ref,
    result_ref,
):
    win = HALF_WIN
    unit, inverse = normalize(tokens_ref[0].astype(F32))
    grads = jnp.concatenate(
        [
            own_ref[0, :win] + from_low_ref[0].astype(F32),
            own_ref[0, win : own_len - win],
            own_ref[0, own_len - win :] + from_high_ref[0].astype(F32),
        ],
        axis=0,
    )
    middle = jnp.concatenate([out_grad_ref[0, 0], mid_grad_ref[0], out_grad_ref[0, 1]], axis=0)
    grad_ref[0] = middle + norm_back(grads * gains_ref[0:1], unit, inverse)
    result_ref[0] = jnp.concatenate([out_result_ref[0, 0], mid_result_ref[0], out_result_ref[0, 1]], axis=0)


def place_kernel(place_ref, own_ref, other_ref, *out_refs):
    half = BLOCKS // 2
    for ref, base in ((own_ref, 0), (other_ref, half)):

        @pl.loop(0, half)
        def _(i):
            block = place_ref[2] ^ (i + base)
            at = 0
            for out in out_refs:
                rows = out.shape[0] // BLOCKS
                for c in range(0, out.shape[1], ref.shape[2]):
                    out[pl.ds(pl.multiple_of(block * rows, rows), rows), c : c + ref.shape[2]] = ref[
                        i, at : at + rows
                    ].astype(F32)
                    at += rows


def shift_route(size, distance):
    return [(i, i + distance) for i in range(size) if 0 <= i + distance < size]


def swap_route(flip):
    dp, seq = lax.axis_size("dp"), lax.axis_size("seq")

    def partner(i):
        d, s = divmod(i, seq)
        core, x, y, z, rest = flip
        return (d ^ (core + 2 * x)) * seq + (s ^ (y + 2 * z + 8 * rest))

    return [(i, partner(i)) for i in range(dp * seq)]


def swap(values, core=0, x=0, y=0, z=0, rest=0):
    return lax.ppermute(values, ("dp", "seq"), swap_route((core, x, y, z, rest)))


def add_all(*parts):
    return sum(p.astype(F32) for p in parts).astype(BF16)


def total_over_devices(keep, send):
    own = add_all(keep, swap(send, core=1))
    own = own.reshape((4, 4) + own.shape[1:])
    own = add_all(own[0], *[swap(own[k], x=k >> 1, y=k & 1) for k in (1, 2, 3)])
    own = add_all(own[0], *[swap(own[k], z=k) for k in (1, 2, 3)])
    rest = 1
    while 8 * rest < lax.axis_size("seq"):
        own = add_all(own, swap(own, rest=rest))
        rest *= 2
    own = jnp.stack([own] + [swap(own, z=k) for k in (1, 2, 3)])
    own = jnp.concatenate([own] + [swap(own, x=k >> 1, y=k & 1) for k in (1, 2, 3)])
    return own, swap(own, core=1)


def whole(array):
    return pl.BlockSpec(array.shape, lambda i: (0,) * array.ndim)


def rows_of(array, pair):
    return pl.BlockSpec((pair,) + array.shape[1:], lambda i: (i,) + (0,) * (array.ndim - 1))


SMEM = pl.BlockSpec(memory_space=pltpu.SMEM)


def params():
    return pltpu.CompilerParams(vmem_limit_bytes=VMEM)


def cost(flops, moved, special=0):
    return pl.CostEstimate(flops=int(flops), bytes_accessed=int(moved), transcendentals=int(special))


def shards(
    tokens,
    document_starts,
    attention_in,
    attention_out,
    feedforward_in,
    feedforward_out,
    gain_first,
    gain_second,
    result_grad,
):
    rows, own_len, width = tokens.shape
    hidden = feedforward_out.shape[0]
    win = HALF_WIN
    seq = lax.axis_size("seq")
    s, d = lax.axis_index("seq"), lax.axis_index("dp")
    start = s * own_len
    block = (d % 2) * 16 + (d // 2) * 8 + (s % 2) * 4 + (s // 2) % 4
    place = jnp.stack([start, jnp.int32(own_len * seq), block]).astype(jnp.int32)
    gains = jnp.stack([gain_first, gain_second])
    inverse = ROTARY_BASE ** (-(jnp.arange(0, HEAD_DIM, 2).astype(F32) / HEAD_DIM))
    positions = start - win + jnp.arange(own_len + 2 * win, dtype=jnp.int32)
    angles = positions.astype(F32)[:, None] * inverse[None, :]
    cosine, sines = jnp.cos(angles), jnp.sin(angles)
    cosine = jnp.concatenate([cosine] * 4, axis=1)
    sines = jnp.concatenate([-sines, sines] * 2, axis=1)
    own_cos, own_sin = cosine[win : win + own_len], sines[win : win + own_len]
    halo_cos = jnp.concatenate([cosine[:win], cosine[win + own_len :]])
    halo_sin = jnp.concatenate([sines[:win], sines[win + own_len :]])

    up_route, down_route = shift_route(seq, 1), shift_route(seq, -1)
    low_tokens = lax.ppermute(tokens[:, own_len - win :], "seq", up_route)
    high_tokens = lax.ppermute(tokens[:, :win], "seq", down_route)

    def shape(*dims, kind=BF16):
        return jax.ShapeDtypeStruct(dims, kind)

    weights = (attention_in, attention_out, feedforward_in, feedforward_out)
    pair = 2
    mid = own_len - 2 * win
    sums = [shape(*w.shape, kind=F32) for w in (feedforward_in, feedforward_out, attention_out)]
    outs = [shape(rows, own_len, width)] * 4 + [
        shape(rows, mid, width),
        shape(rows, mid, width, kind=F32),
        shape(rows, mid, width),
    ]
    small = (gains, own_cos, own_sin)
    normed, queries, keys, values, mid_result, mid_grad, mid_attended, sum_up, sum_down, sum_out = pl.pallas_call(
        functools.partial(first_kernel, own_len),
        grid=(rows // pair,),
        in_specs=[SMEM, SMEM, rows_of(tokens, pair), rows_of(tokens, pair)] + [whole(a) for a in weights + small],
        out_specs=[rows_of(o, pair) for o in outs] + [whole(o) for o in sums],
        out_shape=outs + sums,
        compiler_params=params(),
        cost_estimate=cost(16e9, 30e6),
        name="first",
    )(place, document_starts, tokens, result_grad, *weights, *small)

    outs = [shape(rows, 2, win, width)] * 4 + [
        shape(rows, 2, win, width, kind=F32),
        shape(rows, 2, win, width),
    ]
    piece = (2 * feedforward_in.shape[1] + 2 * width + 2 * hidden) // (2 * BLOCKS)
    piece = (feedforward_in.shape[1] // width * width + width + hidden) // BLOCKS
    blocks = [shape(BLOCKS // 2, piece, width)] * 2
    small = (gains, halo_cos, halo_sin)
    begun = (sum_up, sum_down, sum_out)
    by_row = (tokens, low_tokens, high_tokens, result_grad, queries, keys, values)
    halo_normed, halo_keys, halo_values, out_result, out_grad, out_attended, keep_one, send_one = pl.pallas_call(
        functools.partial(second_kernel, own_len),
        grid=(rows // pair,),
        in_specs=[SMEM, SMEM]
        + [rows_of(a, pair) for a in by_row]
        + [whole(a) for a in weights + small + begun],
        out_specs=[rows_of(o, pair) for o in outs] + [whole(o) for o in blocks],
        out_shape=outs + blocks,
        scratch_shapes=[pltpu.VMEM(o.shape, F32) for o in sums],
        compiler_params=params(),
        cost_estimate=cost(16e9, 30e6),
        name="second",
    )(place, document_starts, *by_row, *weights, *small, *begun)

    outs = [shape(rows, own_len, width, kind=F32), shape(rows, win, width), shape(rows, win, width)]
    piece = attention_in.shape[1] // width * width // BLOCKS
    blocks = [shape(BLOCKS // 2, piece, width)] * 2
    by_row = (queries, keys, values, halo_keys, halo_values, normed, halo_normed, mid_attended, out_attended)
    small = (attention_in, cosine, sines)
    own_grad, to_low, to_high, keep_two, send_two = pl.pallas_call(
        functools.partial(third_kernel, own_len),
        grid=(rows,),
        in_specs=[SMEM, SMEM] + [rows_of(a, 1) for a in by_row] + [whole(a) for a in small],
        out_specs=[rows_of(o, 1) for o in outs] + [whole(o) for o in blocks],
        out_shape=outs + blocks,
        scratch_shapes=[pltpu.VMEM(attention_in.shape, F32)],
        compiler_params=params(),
        cost_estimate=cost(20e9, 30e6),
        name="third",
    )(place, document_starts, *by_row, *small)

    total_one = total_over_devices(keep_one, send_one)
    total_two = total_over_devices(keep_two, send_two)
    from_high = lax.ppermute(to_low, "seq", down_route)
    from_low = lax.ppermute(to_high, "seq", up_route)

    outs = [shape(rows, own_len, width, kind=F32), shape(rows, own_len, width)]
    by_row = (tokens, own_grad, from_low, from_high, mid_grad, out_grad)
    results = (mid_result, out_result)
    grad_tokens, activations = pl.pallas_call(
        functools.partial(fourth_kernel, own_len),
        grid=(rows,),
        in_specs=[rows_of(a, 1) for a in by_row] + [whole(gains)] + [rows_of(a, 1) for a in results],
        out_specs=[rows_of(o, 1) for o in outs],
        out_shape=outs,
        compiler_params=params(),
        cost_estimate=cost(1e7, 15e6),
        name="fourth",
    )(*by_row, gains, *results)

    def placed(parts, *weights):
        return pl.pallas_call(
            place_kernel,
            grid=(1,),
            in_specs=[SMEM] + [whole(a) for a in parts],
            out_specs=[whole(w) for w in weights],
            out_shape=[shape(*w.shape, kind=F32) for w in weights],
            compiler_params=params(),
            cost_estimate=cost(1e6, 8e6),
            name="place",
        )(place, *parts)

    grad_up, grad_out, grad_down = placed(total_one, feedforward_in, attention_out, feedforward_out)
    (grad_in,) = placed(total_two, attention_in)
    grad_gain_one = jnp.sum(grad_in * attention_in.astype(F32), axis=1) / gain_first
    grad_gain_two = jnp.sum(grad_up * feedforward_in.astype(F32), axis=1) / gain_second
    return activations, grad_tokens, grad_in, grad_out, grad_up, grad_down, grad_gain_one, grad_gain_two


def solution(mesh):
    token, rest = P("dp", "seq", None), P()
    return jax.shard_map(
        shards,
        mesh=mesh,
        in_specs=(token, P("dp", None)) + (rest,) * 6 + (token,),
        out_specs=(token, token) + (rest,) * 6,
        check_vma=False,
    )
```

time: 648 us -> 238 us (0.37); the launches traced: 639 us -> 238 us
  matrix products: 251 us -> 0 us
  Pallas kernels: 0 us -> 100 us
  local copies, waits for them, and re-layouts: 104 us -> 6.72 us
  waiting for transfers between devices: 161 us -> 74 us
  blocking collectives: 43.5 us -> 0 us
  other arithmetic: 50.2 us -> 11.5 us
  starting transfers between devices: 14.3 us -> 44.2 us
  between operations: 15.4 us -> 1.15 us
    dot_general x17 -> x0, matrix products: 239 us -> none  [the longest x1 85.6 us: shards(): jnp.einsum('mhqk,mkhd->mqhd', grad_scores, wide_keys, preferred_element_t...]
    psum x1 -> x0, waiting for transfers between devices: 129 us -> none  [shards(): lax.psum((grad_in_weight, grad_out_weight, second_sums[0], second_sums[1]...]
    pallas_call x0 -> x6, Pallas kernels: none -> 100 us  [the longest x1 32 us: shards(): pl.pallas_call(functools.partial(third_kernel, own_len), grid=(rows,), in...]
    reshape x11 -> x0, local copies, waits for them, and re-layouts: 46.4 us -> none  [the longest x2 11.7 us: shards(): projected[:, :model_width].reshape(head_shape)]
    psum x1 -> x0, blocking collectives: 43.5 us -> none  [shards(): lax.psum((grad_in_weight, grad_out_weight, second_sums[0], second_sums[1]...]
    ppermute x4 -> x32, waiting for transfers between devices: 31.9 us -> 74 us  [the longest x28 57.9 us: swap(): lax.ppermute(values, ('dp', 'seq'), swap_route((core, x, y, z, rest)))]
    ppermute x4 -> x32, starting transfers between devices: 14.3 us -> 44.2 us  [the longest x28 33.3 us: swap(): lax.ppermute(values, ('dp', 'seq'), swap_route((core, x, y, z, rest)))]
    slice x10 -> x7, local copies, waits for them, and re-layouts: 23.6 us -> 2.74 us  [the longest x2 1.41 us: shards(): own_cos, own_sin = (cosine[win:win + own_len], sines[win:win + own_len])]
  transfers between devices with their start and end apart: 5 -> 32, of which waited for: 3 -> 15; matrix products, arithmetic and copies ran while one was open for 7% -> 4% of each run, Pallas kernels for 0% -> 15%
where the time goes in v1:
time: 238 us
  Pallas kernels  100 us (42%)
  waiting for transfers between devices  74 us (31%)
  starting transfers between devices  44.2 us (19%)
  other arithmetic  11.5 us (5%)
  local copies, waits for them, and re-layouts  6.72 us (3%)
    ppermute x28, waiting for transfers between devices, swap(): lax.ppermute(values, ('dp', 'seq'), swap_route((core, x, y, z, rest)))  57.9 us
    ppermute x28, starting transfers between devices, swap(): lax.ppermute(values, ('dp', 'seq'), swap_route((core, x, y, z, rest)))  33.3 us
    pallas_call x1, Pallas kernels, shards(): pl.pallas_call(functools.partial(third_kernel, own_len), grid=(rows,), in...  32 us
    pallas_call x1, Pallas kernels, shards(): pl.pallas_call(functools.partial(second_kernel, own_len), grid=(rows // p...  26.6 us
    pallas_call x1, Pallas kernels, shards(): pl.pallas_call(functools.partial(first_kernel, own_len), grid=(rows // pa...  25.2 us
    ppermute x1, waiting for transfers between devices, shards(): from_low = lax.ppermute(to_high, 'seq', up_route)  16.1 us
    pallas_call x2, Pallas kernels, placed(): pl.pallas_call(place_kernel, grid=(1,), in_specs=[SMEM] + [whole(a) for a...  8.37 us
    pallas_call x1, Pallas kernels, shards(): pl.pallas_call(functools.partial(fourth_kernel, own_len), grid=(rows,), i...  7.94 us
  transfers between devices with their start and end apart: 32, of which 15 were waited for; matrix products, arithmetic and copies ran while one was open for 4% of the time, Pallas kernels for 15%

profile of v1, /device:TPU:0, one launch (start us, length us, event | category | flops | bytes accessed | tf_op | source)
XLA Modules:
  0.0 237.7 jit_solution(2550716849687304480)
XLA Ops:
  0.6 1.2 fusion.9
  1.9 1.3 collective-permute-start.1
  3.2 5.5 %collective-permute-start = (bf16[6,64,512]{2,1,0:T(8,128)(2,1)S(1)}, bf16[6,64,512]{2,1,0:T(8,128)(2,1)S(1)}, u32[]{:S(2)}, u32[]{:S(2)}) collective-permute-start(bf16[6,64,512]{2,1,0:T(8,128)(2,1)S(1)} %get-tuple-element.69), channel_id=1, source_target_pairs={{0,1},{1,2},{2,3},{3,4},{4,5},{5,6},{6,7},{8,9},{9,10},{10,11},{11... | collective-permute-start | bytes 1179656 | tf_op jit(solution)/shard_map/ppermute | solution.py:572
  8.8 0.8 fusion.6
  12.5 25.2 %first.1 = (bf16[6,256,512]{2,1,0:T(8,128)(2,1)}, bf16[6,256,512]{2,1,0:T(8,128)(2,1)}, bf16[6,256,512]{2,1,0:T(8,128)(2,1)}, bf16[6,256,512]{2,1,0:T(8,128)(2,1...) custom-call(s32[3]{0:T(128)} %pad_add_fusion.place_ref, ...), custom_call_target="tpu_custom_call" | custom-call | flops 16000000000 | bytes 30000000 | tf_op jit(solution)/shard_map/first/pallas_call | solution.py:588
  39.9 26.6 %second.1 = (bf16[6,2,64,512]{3,2,1,0:T(8,128)(2,1)}, bf16[6,2,64,512]{3,2,1,0:T(8,128)(2,1)}, bf16[6,2,64,512]{3,2,1,0:T(8,128)(2,1)}, bf16[6,2,64,512]{3,2,1,0...) custom-call(s32[3]{0:T(128)} %pad_add_fusion.place_ref, ...), custom_call_target="tpu_custom_call" | custom-call | flops 16000000000 | bytes 30000000 | tf_op jit(solution)/shard_map/second/pallas_call | solution.py:609
  66.5 32.0 %third.1 = (f32[6,256,512]{2,1,0:T(8,128)}, bf16[6,64,512]{2,1,0:T(8,128)(2,1)}, bf16[6,64,512]{2,1,0:T(8,128)(2,1)}, bf16[16,48,512]{2,1,0:T(8,128)(2,1)}, bf16[16,48,512]{2,1,0:T(8,128)(2,1)}) custom-call(s32[3]{0:T(128)} %pad_add_fusion.place_ref, s32[6,16]{1,0:T(8,128)} %starts_ref.5, bf16[6,256,512]{2,1,0:T(8,128)(2,1)} %get-tuple-element.36.queries_ref, ...), custom_call_target="tpu_custom_call" | custom-call | flops 20000000000 | bytes 30000000 | tf_op jit(solution)/shard_map/third/pallas_call | solution.py:628
  99.1 2.2 collective-permute-done.4
  101.3 1.4 add_convert_fusion.1
  102.7 2.9 %collective-permute-start.5 = (bf16[4,48,512]{2,1,0:T(8,128)(2,1)S(1)}, bf16[4,48,512]{2,1,0:T(8,128)(2,1)S(1)}, u32[]{:S(2)}, u32[]{:S(2)}) collective-permute-start(bf16[4,48,512]{2,1,0:T(8,128)(2,1)S(1)} %get-tuple-element.73), channel_id=1, source_target_pairs={{0,1},{1,0},{2,3},{3,2},{4,5},{5,4},{6,7},{7,6},{8,9},{9,8},{10,11... | collective-permute-start | bytes 589832 | tf_op jit(solution)/shard_map/ppermute | solution.py:501
  105.7 1.0 collective-permute-start.7
  107.2 7.9 %collective-permute-done.5 = bf16[4,48,512]{2,1,0:T(8,128)(2,1)S(1)} collective-permute-done((bf16[4,48,512]{2,1,0:T(8,128)(2,1)S(1)}, bf16[4,48,512]{2,1,0:T(8,128)(2,1)S(1)}, u32[]{:S(2)}, u32[]{:S(2)}) %collective-permute-start.5) | collective-permute-done | bytes 196640 | tf_op jit(solution)/shard_map/ppermute | solution.py:501
  115.1 1.3 collective-permute-done.6
  116.5 1.7 collective-permute-start.8
  118.2 2.5 %collective-permute-start.10 = (bf16[48,512]{1,0:T(8,128)(2,1)S(1)}, bf16[48,512]{1,0:T(8,128)(2,1)S(1)}, u32[]{:S(2)}, u32[]{:S(2)}) collective-permute-start(bf16[48,512]{1,0:T(8,128)(2,1)S(1)} %get-tuple-element.80), channel_id=1, source_target_pairs={{0,6},{1,7},{2,4},{3,5},{4,2},{5,3},{6,0},{7,1},{8,14},{9,15},{10,... | collective-permute-start | bytes 147464 | tf_op jit(solution)/shard_map/ppermute | solution.py:501
  120.7 3.4 %collective-permute-done.10 = bf16[48,512]{1,0:T(8,128)(2,1)S(1)} collective-permute-done((bf16[48,512]{1,0:T(8,128)(2,1)S(1)}, bf16[48,512]{1,0:T(8,128)(2,1)S(1)}, u32[]{:S(2)}, u32[]{:S(2)}) %collective-permute-start.10) | collective-permute-done | bytes 49184 | tf_op jit(solution)/shard_map/ppermute | solution.py:501
  124.0 1.6 collective-permute-done.9
  125.7 2.2 collective-permute-start.13
  127.8 2.3 collective-permute-start.11
  130.6 2.1 collective-permute-start.19
  132.7 1.0 collective-permute-start.21
  134.3 2.9 %collective-permute-start.16 = (bf16[4,48,512]{2,1,0:T(8,128)(2,1)S(1)}, bf16[4,48,512]{2,1,0:T(8,128)(2,1)S(1)}, u32[]{:S(2)}, u32[]{:S(2)}) collective-permute-start(bf16[4,48,512]{2,1,0:T(8,128)(2,1)S(1)} %pad_maximum_fusion.3), channel_id=1, source_target_pairs={{0,17},{1,16},{2,19},{3,18},{4,21},{5,20},{6,23},{7,22},{8,25},{9,... | collective-permute-start | bytes 589832 | tf_op jit(solution)/shard_map/ppermute | solution.py:501
  137.7 10.8 %collective-permute-done.19 = bf16[4,88,512]{2,1,0:T(8,128)(2,1)S(1)} collective-permute-done((bf16[4,88,512]{2,1,0:T(8,128)(2,1)S(1)}, bf16[4,88,512]{2,1,0:T(8,128)(2,1)S(1)}, u32[]{:S(2)}, u32[]{:S(2)}) %collective-permute-start.19) | collective-permute-done | bytes 360480 | tf_op jit(solution)/shard_map/ppermute | solution.py:501
  148.5 2.7 %collective-permute-done.20 = bf16[4,88,512]{2,1,0:T(8,128)(2,1)S(1)} collective-permute-done((bf16[4,88,512]{2,1,0:T(8,128)(2,1)S(1)}, bf16[4,88,512]{2,1,0:T(8,128)(2,1)S(1)}, u32[]{:S(2)}, u32[]{:S(2)}) %collective-permute-start.20) | collective-permute-done | bytes 360480 | tf_op jit(solution)/shard_map/ppermute | solution.py:501
  151.6 2.1 collective-permute-start.24
  153.7 1.4 collective-permute-start.23
  155.0 1.5 collective-permute-done.22
  156.5 1.5 collective-permute-done.24
  158.1 5.7 %collective-permute-done.23 = bf16[88,512]{1,0:T(8,128)(2,1)S(1)} collective-permute-done((bf16[88,512]{1,0:T(8,128)(2,1)S(1)}, bf16[88,512]{1,0:T(8,128)(2,1)S(1)}, u32[]{:S(2)}, u32[]{:S(2)}) %collective-permute-start.23) | collective-permute-done | bytes 90144 | tf_op jit(solution)/shard_map/ppermute | solution.py:501
  163.9 2.1 collective-permute-start.27
  165.9 2.4 %collective-permute-start.25 = (bf16[88,512]{1,0:T(8,128)(2,1)S(1)}, bf16[88,512]{1,0:T(8,128)(2,1)S(1)}, u32[]{:S(2)}, u32[]{:S(2)}) collective-permute-start(bf16[88,512]{1,0:T(8,128)(2,1)S(1)} %get-tuple-element.65), channel_id=1, source_target_pairs={{0,2},{1,3},{2,0},{3,1},{4,6},{5,7},{6,4},{7,5},{8,10},{9,11},{10,... | collective-permute-start | bytes 270344 | tf_op jit(solution)/shard_map/ppermute | solution.py:501
  168.3 2.0 collective-permute-done.27
  170.3 1.9 collective-permute-done.26
  172.3 1.9 collective-permute-start.30
  174.7 1.1 collective-permute-start.28
  175.9 10.7 %collective-permute-done.28 = bf16[4,88,512]{2,1,0:T(8,128)(2,1)S(1)} collective-permute-done((bf16[4,88,512]{2,1,0:T(8,128)(2,1)S(1)}, bf16[4,88,512]{2,1,0:T(8,128)(2,1)S(1)}, u32[]{:S(2)}, u32[]{:S(2)}) %collective-permute-start.28) | collective-permute-done | bytes 360480 | tf_op jit(solution)/shard_map/ppermute | solution.py:501
  186.6 0.9 collective-permute-start.14
  187.7 4.6 %collective-permute-done.14 = bf16[4,48,512]{2,1,0:T(8,128)(2,1)S(1)} collective-permute-done((bf16[4,48,512]{2,1,0:T(8,128)(2,1)S(1)}, bf16[4,48,512]{2,1,0:T(8,128)(2,1)S(1)}, u32[]{:S(2)}, u32[]{:S(2)}) %collective-permute-start.14) | collective-permute-done | bytes 196640 | tf_op jit(solution)/shard_map/ppermute | solution.py:501
  192.5 2.8 %collective-permute-start.2 = (bf16[6,64,512]{2,1,0:T(8,128)(2,1)S(1)}, bf16[6,64,512]{2,1,0:T(8,128)(2,1)S(1)}, u32[]{:S(2)}, u32[]{:S(2)}) collective-permute-start(bf16[6,64,512]{2,1,0:T(8,128)(2,1)S(1)} %copy-done.15), channel_id=1, source_target_pairs={{0,1},{1,2},{2,3},{3,4},{4,5},{5,6},{6,7},{8,9},{9,10},{10,11},{11... | collective-permute-start | bytes 1179656 | tf_op jit(solution)/shard_map/ppermute | solution.py:643
  195.3 1.3 collective-permute-start.3
  196.6 16.1 %collective-permute-done.2.from_low_ref = bf16[6,64,512]{2,1,0:T(8,128)(2,1)S(1)} collective-permute-done((bf16[6,64,512]{2,1,0:T(8,128)(2,1)S(1)}, bf16[6,64,512]{2,1,0:T(8,128)(2,1)S(1)}, u32[]{:S(2)}, u32[]{:S(2)}) %collective-permute-start.2) | collective-permute-done | bytes 393248 | tf_op jit(solution)/shard_map/ppermute | solution.py:643
  213.6 7.9 %fourth.1 = (f32[6,256,512]{2,1,0:T(8,128)}, bf16[6,256,512]{2,1,0:T(8,128)(2,1)}) custom-call(bf16[6,256,512]{2,1,0:T(8,128)(2,1)} %tokens_ref.5, f32[6,256,512]{2,1,0:T(8,128)} %get-tuple-element.48.own_ref, bf16[6,64,512]{2,1,0:T(8,128)(2,1)} %copy-done.9, bf16[6,64,512]{2,1,0:T(8,128)(2,1)} %copy-done.10, f32[6,128,512]{2,1,0:T(8,128)} %get-tuple-element.51.mid_grad_ref, ...), custom_call_target="tpu_custom_call" | custom-call | flops 10000000 | bytes 15000000 | tf_op jit(solution)/shard_map/fourth/pallas_call | solution.py:648
  221.6 0.9 copy-done.6
  222.4 3.5 %place.2 = f32[512,1536]{1,0:T(8,128)} custom-call(s32[3]{0:T(128)} %pad_add_fusion.place_ref, bf16[16,48,512]{2,1,0:T(8,128)(2,1)} %copy-done.5, bf16[16,48,512]{2,1,0:T(8,128)(2,1)} %copy-done.6), custom_call_target="tpu_custom_call" | custom-call | flops 1000000 | bytes 8000000 | tf_op jit(solution)/shard_map/place/pallas_call | solution.py:660
  225.9 2.3 multiply_reduce_fusion.1
  228.8 1.1 copy-done.4
  229.9 4.9 %place.3 = (f32[512,1536]{1,0:T(8,128)}, f32[512,512]{1,0:T(8,128)}, f32[768,512]{1,0:T(8,128)}) custom-call(s32[3]{0:T(128)} %pad_add_fusion.place_ref, bf16[16,88,512]{2,1,0:T(8,128)(2,1)} %copy-done, bf16[16,88,512]{2,1,0:T(8,128)(2,1)} %copy-done.4), custom_call_target="tpu_custom_call" | custom-call | flops 1000000 | bytes 8000000 | tf_op jit(solution)/shard_map/place/pallas_call | solution.py:660
  234.8 2.3 multiply_reduce_fusion
  (99 shorter events, 11.4 us)
Async XLA Ops:
  1.8 9.5 %copy-start.11 = (f32[512]{0:T(512)S(1)}, f32[512]{0:T(512)}, u32[]{:S(2)}) copy-start(f32[512]{0:T(512)} %param.15) | copy-start | bytes 6148
  1.8 9.5 %copy-start.12 = (f32[512]{0:T(512)S(1)}, f32[512]{0:T(512)}, u32[]{:S(2)}) copy-start(f32[512]{0:T(512)} %param.16) | copy-start | bytes 6148
  1.9 37.2 %collective-permute-start.1 = (bf16[6,64,512]{2,1,0:T(8,128)(2,1)S(1)}, bf16[6,64,512]{2,1,0:T(8,128)(2,1)S(1)}, u32[]{:S(2)}, u32[]{:S(2)}) collective-permute-start(bf16[6,64,512]{2,1,0:T(8,128)(2,1)S(1)} %get-tuple-element.68), channel_id=1, source_target_pairs={{1,0},{2,1},{3,2},{4,3},{5,4},{6,5},{7,6},{9,8},{10,9},{11,10},{12... | collective-permute-start | bytes 1179656 | tf_op jit(solution)/shard_map/ppermute | solution.py:573
  3.2 35.9 %collective-permute-start = (bf16[6,64,512]{2,1,0:T(8,128)(2,1)S(1)}, bf16[6,64,512]{2,1,0:T(8,128)(2,1)S(1)}, u32[]{:S(2)}, u32[]{:S(2)}) collective-permute-start(bf16[6,64,512]{2,1,0:T(8,128)(2,1)S(1)} %get-tuple-element.69), channel_id=1, source_target_pairs={{0,1},{1,2},{2,3},{3,4},{4,5},{5,6},{6,7},{8,9},{9,10},{10,11},{11... | collective-permute-start | bytes 1179656 | tf_op jit(solution)/shard_map/ppermute | solution.py:572
  9.9 27.8 %copy-start.7 = (f32[384,128]{1,0:T(8,128)}, f32[384,128]{1,0:T(8,128)S(1)}, u32[]{:S(2)}) copy-start(f32[384,128]{1,0:T(8,128)S(1)} %get-tuple-element.89.cos_ref) | copy-start | bytes 589828
  9.9 28.5 %copy-start.8 = (f32[384,128]{1,0:T(8,128)}, f32[384,128]{1,0:T(8,128)S(1)}, u32[]{:S(2)}) copy-start(f32[384,128]{1,0:T(8,128)S(1)} %get-tuple-element.90.sin_ref) | copy-start | bytes 589828
  39.0 0.9 copy-start.17
  66.5 32.1 %copy-start.13 = (bf16[16,88,512]{2,1,0:T(8,128)(2,1)S(1)}, bf16[16,88,512]{2,1,0:T(8,128)(2,1)}, u32[]{:S(2)}) copy-start(bf16[16,88,512]{2,1,0:T(8,128)(2,1)} %get-tuple-element.60) | copy-start | bytes 4325380
  98.5 2.8 %collective-permute-start.4 = (bf16[16,48,512]{2,1,0:T(8,128)(2,1)}, bf16[16,48,512]{2,1,0:T(8,128)(2,1)S(1)}, u32[]{:S(2)}, u32[]{:S(2)}) collective-permute-start(bf16[16,48,512]{2,1,0:T(8,128)(2,1)} %get-tuple-element.58), channel_id=1, source_target_pairs={{0,8},{1,9},{2,10},{3,11},{4,12},{5,13},{6,14},{7,15},{8,0},{9,1},... | collective-permute-start | bytes 2359304 | tf_op jit(solution)/shard_map/ppermute | solution.py:501
  98.6 31.5 %collective-permute-start.18 = (bf16[16,88,512]{2,1,0:T(8,128)(2,1)S(1)}, bf16[16,88,512]{2,1,0:T(8,128)(2,1)S(1)}, u32[]{:S(2)}, u32[]{:S(2)}) collective-permute-start(bf16[16,88,512]{2,1,0:T(8,128)(2,1)S(1)} %copy-done.13), channel_id=1, source_target_pairs={{0,8},{1,9},{2,10},{3,11},{4,12},{5,13},{6,14},{7,15},{8,0},{9,1},... | collective-permute-start | bytes 4325384 | tf_op jit(solution)/shard_map/ppermute | solution.py:501
  102.7 27.4 %copy-start.3 = (bf16[16,88,512]{2,1,0:T(8,128)(2,1)S(1)}, bf16[16,88,512]{2,1,0:T(8,128)(2,1)}, u32[]{:S(2)}) copy-start(bf16[16,88,512]{2,1,0:T(8,128)(2,1)} %get-tuple-element.59) | copy-start | bytes 4325380
  102.7 12.3 %collective-permute-start.5 = (bf16[4,48,512]{2,1,0:T(8,128)(2,1)S(1)}, bf16[4,48,512]{2,1,0:T(8,128)(2,1)S(1)}, u32[]{:S(2)}, u32[]{:S(2)}) collective-permute-start(bf16[4,48,512]{2,1,0:T(8,128)(2,1)S(1)} %get-tuple-element.73), channel_id=1, source_target_pairs={{0,1},{1,0},{2,3},{3,2},{4,5},{5,4},{6,7},{7,6},{8,9},{9,8},{10,11... | collective-permute-start | bytes 589832 | tf_op jit(solution)/shard_map/ppermute | solution.py:501
  105.7 9.4 %collective-permute-start.7 = (bf16[4,48,512]{2,1,0:T(8,128)(2,1)S(1)}, bf16[4,48,512]{2,1,0:T(8,128)(2,1)S(1)}, u32[]{:S(2)}, u32[]{:S(2)}) collective-permute-start(bf16[4,48,512]{2,1,0:T(8,128)(2,1)S(1)} %get-tuple-element.74), channel_id=1, source_target_pairs={{0,17},{1,16},{2,19},{3,18},{4,21},{5,20},{6,23},{7,22},{8,25},{9,... | collective-permute-start | bytes 589832 | tf_op jit(solution)/shard_map/ppermute | solution.py:501
  106.7 9.7 %collective-permute-start.6 = (bf16[4,48,512]{2,1,0:T(8,128)(2,1)S(1)}, bf16[4,48,512]{2,1,0:T(8,128)(2,1)S(1)}, u32[]{:S(2)}, u32[]{:S(2)}) collective-permute-start(bf16[4,48,512]{2,1,0:T(8,128)(2,1)S(1)} %get-tuple-element.75), channel_id=1, source_target_pairs={{0,16},{1,17},{2,18},{3,19},{4,20},{5,21},{6,22},{7,23},{8,24},{9,... | collective-permute-start | bytes 589832 | tf_op jit(solution)/shard_map/ppermute | solution.py:501
  116.5 4.2 %collective-permute-start.8 = (bf16[48,512]{1,0:T(8,128)(2,1)S(1)}, bf16[48,512]{1,0:T(8,128)(2,1)S(1)}, u32[]{:S(2)}, u32[]{:S(2)}) collective-permute-start(bf16[48,512]{1,0:T(8,128)(2,1)S(1)} %get-tuple-element.79), channel_id=1, source_target_pairs={{0,2},{1,3},{2,0},{3,1},{4,6},{5,7},{6,4},{7,5},{8,10},{9,11},{10,... | collective-permute-start | bytes 147464 | tf_op jit(solution)/shard_map/ppermute | solution.py:501
  118.2 5.9 %collective-permute-start.10 = (bf16[48,512]{1,0:T(8,128)(2,1)S(1)}, bf16[48,512]{1,0:T(8,128)(2,1)S(1)}, u32[]{:S(2)}, u32[]{:S(2)}) collective-permute-start(bf16[48,512]{1,0:T(8,128)(2,1)S(1)} %get-tuple-element.80), channel_id=1, source_target_pairs={{0,6},{1,7},{2,4},{3,5},{4,2},{5,3},{6,0},{7,1},{8,14},{9,15},{10,... | collective-permute-start | bytes 147464 | tf_op jit(solution)/shard_map/ppermute | solution.py:501
  120.6 5.0 %collective-permute-start.9 = (bf16[48,512]{1,0:T(8,128)(2,1)S(1)}, bf16[48,512]{1,0:T(8,128)(2,1)S(1)}, u32[]{:S(2)}, u32[]{:S(2)}) collective-permute-start(bf16[48,512]{1,0:T(8,128)(2,1)S(1)} %get-tuple-element.81), channel_id=1, source_target_pairs={{0,4},{1,5},{2,6},{3,7},{4,0},{5,1},{6,2},{7,3},{8,12},{9,13},{10,... | collective-permute-start | bytes 147464 | tf_op jit(solution)/shard_map/ppermute | solution.py:501
  125.7 8.0 %collective-permute-start.13 = (bf16[48,512]{1,0:T(8,128)(2,1)S(1)}, bf16[48,512]{1,0:T(8,128)(2,1)S(1)}, u32[]{:S(2)}, u32[]{:S(2)}) collective-permute-start(bf16[48,512]{1,0:T(8,128)(2,1)S(1)} %get-tuple-element.67), channel_id=1, source_target_pairs={{0,6},{1,7},{2,4},{3,5},{4,2},{5,3},{6,0},{7,1},{8,14},{9,15},{10,... | collective-permute-start | bytes 147464 | tf_op jit(solution)/shard_map/ppermute | solution.py:501
  127.8 6.4 %collective-permute-start.12 = (bf16[48,512]{1,0:T(8,128)(2,1)S(1)}, bf16[48,512]{1,0:T(8,128)(2,1)S(1)}, u32[]{:S(2)}, u32[]{:S(2)}) collective-permute-start(bf16[48,512]{1,0:T(8,128)(2,1)S(1)} %get-tuple-element.67), channel_id=1, source_target_pairs={{0,4},{1,5},{2,6},{3,7},{4,0},{5,1},{6,2},{7,3},{8,12},{9,13},{10,... | collective-permute-start | bytes 147464 | tf_op jit(solution)/shard_map/ppermute | solution.py:501
  127.8 6.4 %collective-permute-start.11 = (bf16[48,512]{1,0:T(8,128)(2,1)S(1)}, bf16[48,512]{1,0:T(8,128)(2,1)S(1)}, u32[]{:S(2)}, u32[]{:S(2)}) collective-permute-start(bf16[48,512]{1,0:T(8,128)(2,1)S(1)} %get-tuple-element.67), channel_id=1, source_target_pairs={{0,2},{1,3},{2,0},{3,1},{4,6},{5,7},{6,4},{7,5},{8,10},{9,11},{10,... | collective-permute-start | bytes 147464 | tf_op jit(solution)/shard_map/ppermute | solution.py:501
  130.6 17.9 %collective-permute-start.19 = (bf16[4,88,512]{2,1,0:T(8,128)(2,1)S(1)}, bf16[4,88,512]{2,1,0:T(8,128)(2,1)S(1)}, u32[]{:S(2)}, u32[]{:S(2)}) collective-permute-start(bf16[4,88,512]{2,1,0:T(8,128)(2,1)S(1)} %get-tuple-element.70), channel_id=1, source_target_pairs={{0,1},{1,0},{2,3},{3,2},{4,5},{5,4},{6,7},{7,6},{8,9},{9,8},{10,11... | collective-permute-start | bytes 1081352 | tf_op jit(solution)/shard_map/ppermute | solution.py:501
  132.7 15.8 %collective-permute-start.21 = (bf16[4,88,512]{2,1,0:T(8,128)(2,1)S(1)}, bf16[4,88,512]{2,1,0:T(8,128)(2,1)S(1)}, u32[]{:S(2)}, u32[]{:S(2)}) collective-permute-start(bf16[4,88,512]{2,1,0:T(8,128)(2,1)S(1)} %get-tuple-element.71), channel_id=1, source_target_pairs={{0,17},{1,16},{2,19},{3,18},{4,21},{5,20},{6,23},{7,22},{8,25},{9,... | collective-permute-start | bytes 1081352 | tf_op jit(solution)/shard_map/ppermute | solution.py:501
  133.7 17.6 %collective-permute-start.20 = (bf16[4,88,512]{2,1,0:T(8,128)(2,1)S(1)}, bf16[4,88,512]{2,1,0:T(8,128)(2,1)S(1)}, u32[]{:S(2)}, u32[]{:S(2)}) collective-permute-start(bf16[4,88,512]{2,1,0:T(8,128)(2,1)S(1)} %get-tuple-element.72), channel_id=1, source_target_pairs={{0,16},{1,17},{2,18},{3,19},{4,20},{5,21},{6,22},{7,23},{8,24},{9,... | collective-permute-start | bytes 1081352 | tf_op jit(solution)/shard_map/ppermute | solution.py:501
  134.3 58.1 %collective-permute-start.16 = (bf16[4,48,512]{2,1,0:T(8,128)(2,1)S(1)}, bf16[4,48,512]{2,1,0:T(8,128)(2,1)S(1)}, u32[]{:S(2)}, u32[]{:S(2)}) collective-permute-start(bf16[4,48,512]{2,1,0:T(8,128)(2,1)S(1)} %pad_maximum_fusion.3), channel_id=1, source_target_pairs={{0,17},{1,16},{2,19},{3,18},{4,21},{5,20},{6,23},{7,22},{8,25},{9,... | collective-permute-start | bytes 589832 | tf_op jit(solution)/shard_map/ppermute | solution.py:501
  137.2 55.1 %collective-permute-start.15 = (bf16[4,48,512]{2,1,0:T(8,128)(2,1)S(1)}, bf16[4,48,512]{2,1,0:T(8,128)(2,1)S(1)}, u32[]{:S(2)}, u32[]{:S(2)}) collective-permute-start(bf16[4,48,512]{2,1,0:T(8,128)(2,1)S(1)} %pad_maximum_fusion.3), channel_id=1, source_target_pairs={{0,16},{1,17},{2,18},{3,19},{4,20},{5,21},{6,22},{7,23},{8,24},{9,... | collective-permute-start | bytes 589832 | tf_op jit(solution)/shard_map/ppermute | solution.py:501
  151.5 5.0 %collective-permute-start.22 = (bf16[88,512]{1,0:T(8,128)(2,1)S(1)}, bf16[88,512]{1,0:T(8,128)(2,1)S(1)}, u32[]{:S(2)}, u32[]{:S(2)}) collective-permute-start(bf16[88,512]{1,0:T(8,128)(2,1)S(1)} %get-tuple-element.76), channel_id=1, source_target_pairs={{0,2},{1,3},{2,0},{3,1},{4,6},{5,7},{6,4},{7,5},{8,10},{9,11},{10,... | collective-permute-start | bytes 270344 | tf_op jit(solution)/shard_map/ppermute | solution.py:501
  151.6 6.5 %collective-permute-start.24 = (bf16[88,512]{1,0:T(8,128)(2,1)S(1)}, bf16[88,512]{1,0:T(8,128)(2,1)S(1)}, u32[]{:S(2)}, u32[]{:S(2)}) collective-permute-start(bf16[88,512]{1,0:T(8,128)(2,1)S(1)} %get-tuple-element.77), channel_id=1, source_target_pairs={{0,6},{1,7},{2,4},{3,5},{4,2},{5,3},{6,0},{7,1},{8,14},{9,15},{10,... | collective-permute-start | bytes 270344 | tf_op jit(solution)/shard_map/ppermute | solution.py:501
  153.7 10.1 %collective-permute-start.23 = (bf16[88,512]{1,0:T(8,128)(2,1)S(1)}, bf16[88,512]{1,0:T(8,128)(2,1)S(1)}, u32[]{:S(2)}, u32[]{:S(2)}) collective-permute-start(bf16[88,512]{1,0:T(8,128)(2,1)S(1)} %get-tuple-element.78), channel_id=1, source_target_pairs={{0,4},{1,5},{2,6},{3,7},{4,0},{5,1},{6,2},{7,3},{8,12},{9,13},{10,... | collective-permute-start | bytes 270344 | tf_op jit(solution)/shard_map/ppermute | solution.py:501
  163.9 6.4 %collective-permute-start.27 = (bf16[88,512]{1,0:T(8,128)(2,1)S(1)}, bf16[88,512]{1,0:T(8,128)(2,1)S(1)}, u32[]{:S(2)}, u32[]{:S(2)}) collective-permute-start(bf16[88,512]{1,0:T(8,128)(2,1)S(1)} %get-tuple-element.65), channel_id=1, source_target_pairs={{0,6},{1,7},{2,4},{3,5},{4,2},{5,3},{6,0},{7,1},{8,14},{9,15},{10,... | collective-permute-start | bytes 270344 | tf_op jit(solution)/shard_map/ppermute | solution.py:501
  165.9 6.3 %collective-permute-start.26 = (bf16[88,512]{1,0:T(8,128)(2,1)S(1)}, bf16[88,512]{1,0:T(8,128)(2,1)S(1)}, u32[]{:S(2)}, u32[]{:S(2)}) collective-permute-start(bf16[88,512]{1,0:T(8,128)(2,1)S(1)} %get-tuple-element.65), channel_id=1, source_target_pairs={{0,4},{1,5},{2,6},{3,7},{4,0},{5,1},{6,2},{7,3},{8,12},{9,13},{10,... | collective-permute-start | bytes 270344 | tf_op jit(solution)/shard_map/ppermute | solution.py:501
  165.9 6.3 %collective-permute-start.25 = (bf16[88,512]{1,0:T(8,128)(2,1)S(1)}, bf16[88,512]{1,0:T(8,128)(2,1)S(1)}, u32[]{:S(2)}, u32[]{:S(2)}) collective-permute-start(bf16[88,512]{1,0:T(8,128)(2,1)S(1)} %get-tuple-element.65), channel_id=1, source_target_pairs={{0,2},{1,3},{2,0},{3,1},{4,6},{5,7},{6,4},{7,5},{8,10},{9,11},{10,... | collective-permute-start | bytes 270344 | tf_op jit(solution)/shard_map/ppermute | solution.py:501
  172.3 15.3 %collective-permute-start.30 = (bf16[4,88,512]{2,1,0:T(8,128)(2,1)S(1)}, bf16[4,88,512]{2,1,0:T(8,128)(2,1)S(1)}, u32[]{:S(2)}, u32[]{:S(2)}) collective-permute-start(bf16[4,88,512]{2,1,0:T(8,128)(2,1)S(1)} %pad_maximum_fusion), channel_id=1, source_target_pairs={{0,17},{1,16},{2,19},{3,18},{4,21},{5,20},{6,23},{7,22},{8,25},{9,... | collective-permute-start | bytes 1081352 | tf_op jit(solution)/shard_map/ppermute | solution.py:501
  174.1 13.4 %collective-permute-start.29 = (bf16[4,88,512]{2,1,0:T(8,128)(2,1)S(1)}, bf16[4,88,512]{2,1,0:T(8,128)(2,1)S(1)}, u32[]{:S(2)}, u32[]{:S(2)}) collective-permute-start(bf16[4,88,512]{2,1,0:T(8,128)(2,1)S(1)} %pad_maximum_fusion), channel_id=1, source_target_pairs={{0,16},{1,17},{2,18},{3,19},{4,20},{5,21},{6,22},{7,23},{8,24},{9,... | collective-permute-start | bytes 1081352 | tf_op jit(solution)/shard_map/ppermute | solution.py:501
  174.7 11.9 %collective-permute-start.28 = (bf16[4,88,512]{2,1,0:T(8,128)(2,1)S(1)}, bf16[4,88,512]{2,1,0:T(8,128)(2,1)S(1)}, u32[]{:S(2)}, u32[]{:S(2)}) collective-permute-start(bf16[4,88,512]{2,1,0:T(8,128)(2,1)S(1)} %pad_maximum_fusion), channel_id=1, source_target_pairs={{0,1},{1,0},{2,3},{3,2},{4,5},{5,4},{6,7},{7,6},{8,9},{9,8},{10,11... | collective-permute-start | bytes 1081352 | tf_op jit(solution)/shard_map/ppermute | solution.py:501
  175.8 16.6 %copy-start.15 = (bf16[6,64,512]{2,1,0:T(8,128)(2,1)S(1)}, bf16[6,64,512]{2,1,0:T(8,128)(2,1)}, u32[]{:S(2)}) copy-start(bf16[6,64,512]{2,1,0:T(8,128)(2,1)} %get-tuple-element.49) | copy-start | bytes 1179652
  175.8 19.4 %copy-start.14 = (bf16[6,64,512]{2,1,0:T(8,128)(2,1)S(1)}, bf16[6,64,512]{2,1,0:T(8,128)(2,1)}, u32[]{:S(2)}) copy-start(bf16[6,64,512]{2,1,0:T(8,128)(2,1)} %get-tuple-element.50) | copy-start | bytes 1179652
  186.6 5.7 %collective-permute-start.14 = (bf16[4,48,512]{2,1,0:T(8,128)(2,1)S(1)}, bf16[4,48,512]{2,1,0:T(8,128)(2,1)S(1)}, u32[]{:S(2)}, u32[]{:S(2)}) collective-permute-start(bf16[4,48,512]{2,1,0:T(8,128)(2,1)S(1)} %pad_maximum_fusion.3), channel_id=1, source_target_pairs={{0,1},{1,0},{2,3},{3,2},{4,5},{5,4},{6,7},{7,6},{8,9},{9,8},{10,11... | collective-permute-start | bytes 589832 | tf_op jit(solution)/shard_map/ppermute | solution.py:501
  187.6 33.9 %copy-start = (bf16[16,88,512]{2,1,0:T(8,128)(2,1)}, bf16[16,88,512]{2,1,0:T(8,128)(2,1)S(1)}, u32[]{:S(2)}) copy-start(bf16[16,88,512]{2,1,0:T(8,128)(2,1)S(1)} %constant_dynamic-update-slice_fusion.7.own_ref) | copy-start | bytes 4325380
  187.6 41.1 %collective-permute-start.31 = (bf16[16,88,512]{2,1,0:T(8,128)(2,1)S(1)}, bf16[16,88,512]{2,1,0:T(8,128)(2,1)S(1)}, u32[]{:S(2)}, u32[]{:S(2)}) collective-permute-start(bf16[16,88,512]{2,1,0:T(8,128)(2,1)S(1)} %constant_dynamic-update-slice_fusion.7.own_ref), channel_id=1, source_target_pairs={{0,8},{1,9},{2,10},{3,11},{4,12},{5,13},{6,14},{7,15},{8,0},{9,1},... | collective-permute-start | bytes 4325384 | tf_op jit(solution)/shard_map/ppermute | solution.py:501
  192.4 29.2 %copy-start.5 = (bf16[16,48,512]{2,1,0:T(8,128)(2,1)}, bf16[16,48,512]{2,1,0:T(8,128)(2,1)S(1)}, u32[]{:S(2)}) copy-start(bf16[16,48,512]{2,1,0:T(8,128)(2,1)S(1)} %constant_dynamic-update-slice_fusion.own_ref) | copy-start | bytes 2359300
  192.4 29.2 %collective-permute-start.17 = (bf16[16,48,512]{2,1,0:T(8,128)(2,1)S(1)}, bf16[16,48,512]{2,1,0:T(8,128)(2,1)S(1)}, u32[]{:S(2)}, u32[]{:S(2)}) collective-permute-start(bf16[16,48,512]{2,1,0:T(8,128)(2,1)S(1)} %constant_dynamic-update-slice_fusion.own_ref), channel_id=1, source_target_pairs={{0,8},{1,9},{2,10},{3,11},{4,12},{5,13},{6,14},{7,15},{8,0},{9,1},... | collective-permute-start | bytes 2359304 | tf_op jit(solution)/shard_map/ppermute | solution.py:501
  192.5 20.2 %collective-permute-start.2 = (bf16[6,64,512]{2,1,0:T(8,128)(2,1)S(1)}, bf16[6,64,512]{2,1,0:T(8,128)(2,1)S(1)}, u32[]{:S(2)}, u32[]{:S(2)}) collective-permute-start(bf16[6,64,512]{2,1,0:T(8,128)(2,1)S(1)} %copy-done.15), channel_id=1, source_target_pairs={{0,1},{1,2},{2,3},{3,4},{4,5},{5,6},{6,7},{8,9},{9,10},{10,11},{11... | collective-permute-start | bytes 1179656 | tf_op jit(solution)/shard_map/ppermute | solution.py:643
  195.3 17.4 %collective-permute-start.3 = (bf16[6,64,512]{2,1,0:T(8,128)(2,1)S(1)}, bf16[6,64,512]{2,1,0:T(8,128)(2,1)S(1)}, u32[]{:S(2)}, u32[]{:S(2)}) collective-permute-start(bf16[6,64,512]{2,1,0:T(8,128)(2,1)S(1)} %copy-done.14), channel_id=1, source_target_pairs={{1,0},{2,1},{3,2},{4,3},{5,4},{6,5},{7,6},{9,8},{10,9},{11,10},{12... | collective-permute-start | bytes 1179656 | tf_op jit(solution)/shard_map/ppermute | solution.py:642
  212.7 0.9 copy-start.10
  221.5 4.4 %copy-start.1 = (bf16[512,1536]{1,0:T(8,128)(2,1)S(1)}, bf16[512,1536]{1,0:T(8,128)(2,1)}, u32[]{:S(2)}) copy-start(bf16[512,1536]{1,0:T(8,128)(2,1)} %in_ref.5) | copy-start | bytes 4718596
  221.6 0.9 copy-start.6
  228.2 6.6 %copy-start.2 = (bf16[512,1536]{1,0:T(8,128)(2,1)S(1)}, bf16[512,1536]{1,0:T(8,128)(2,1)}, u32[]{:S(2)}) copy-start(bf16[512,1536]{1,0:T(8,128)(2,1)} %up_ref.3) | copy-start | bytes 4718596
  228.8 1.1 copy-start.4
  (2 other events, 1.5 us)

commit v2 on v0

v2 whole, which is shorter than its diff:
```python
import functools

import jax
import jax.numpy as jnp
import numpy as np
from jax import lax
from jax.experimental import pallas as pl
from jax.experimental.pallas import tpu as pltpu
from jax.sharding import PartitionSpec as P

HEADS = 8
HEAD_DIM = 64
HALF = HEAD_DIM // 2
HALF_WIN = 64
EPSILON = 1e-05
ROTARY_BASE = 10000.0
SCALE = HEAD_DIM**-0.5
BLOCKS = 32
GROUP = 4
WIDE = GROUP * HEAD_DIM
LANES = 128
MB = 1024 * 1024

F32 = jnp.float32
BF16 = jnp.bfloat16


def dot(a, b, contract):
    return lax.dot_general(a, b, ((contract[:1], contract[1:]), ((), ())), preferred_element_type=F32)


def nn(a, b):
    return dot(a, b, (1, 0))


def nt(a, b):
    return dot(a, b, (1, 1))


def tn(a, b):
    return dot(a, b, (0, 0))


def iota(shape, dim):
    return lax.broadcasted_iota(jnp.int32, shape, dim)


def flat(values):
    return values.reshape(-1, values.shape[-1])


def normalize(values):
    shifted = values - jnp.mean(values, axis=-1, keepdims=True)
    inverse = lax.rsqrt(jnp.mean(shifted * shifted, axis=-1, keepdims=True) + EPSILON)
    return shifted * inverse, inverse


def norm_back(scaled_grad, unit, inverse):
    return (
        scaled_grad
        - jnp.mean(scaled_grad, axis=-1, keepdims=True)
        - unit * jnp.mean(scaled_grad * unit, axis=-1, keepdims=True)
    ) * inverse


def halves_first():
    old, new = iota((WIDE, WIDE), 0), iota((WIDE, WIDE), 1)
    moved = (old % HEAD_DIM) // HALF * LANES + old // HEAD_DIM * HALF + old % HALF
    return (moved == new).astype(BF16)


def head_of(shape, halved):
    lane = iota(shape, 1)
    return lane % LANES // HALF if halved else lane // HEAD_DIM


def by_head(values, halved):
    head = head_of(values.shape, halved)
    zero = jnp.zeros_like(values)
    return jnp.concatenate([jnp.where(head == h, values, zero) for h in range(GROUP)], axis=0)


def pick_heads(stacked, halved):
    count = stacked.shape[0] // GROUP
    head = head_of((count, stacked.shape[1]), halved)
    out = stacked[:count]
    for h in range(1, GROUP):
        out = jnp.where(head == h, stacked[h * count : (h + 1) * count], out)
    return out


def turn(values, cosine, sines):
    first, second = values[:, :LANES], values[:, LANES:]
    return jnp.concatenate([first * cosine - second * sines, second * cosine + first * sines], axis=1)


def turn_back(values, cosine, sines):
    first, second = values[:, :LANES], values[:, LANES:]
    return jnp.concatenate([first * cosine + second * sines, second * cosine - first * sines], axis=1)


def project_kernel(
    tokens_ref,
    starts_ref,
    in_ref,
    gain_ref,
    base_ref,
    table_ref,
    normed_ref,
    queries_ref,
    keys_ref,
    values_ref,
    weight_ref,
    angles_ref,
    bounds_ref,
):
    rows, own_len, width = tokens_ref.shape
    win = HALF_WIN
    place = lax.axis_index("seq")
    start = place * own_len
    row_len = own_len * lax.axis_size("seq")

    base_cos, base_sin = base_ref[place, 0:1], base_ref[place, 1:2]
    angles_ref[0] = base_cos * table_ref[0] - base_sin * table_ref[1]
    angles_ref[1] = base_sin * table_ref[0] + base_cos * table_ref[1]

    lane = iota((rows, own_len - 2 * win + 4 * win), 1)
    mid = own_len - 2 * win
    pos = start + jnp.where(
        lane < mid, lane + win, jnp.where(lane < mid + 2 * win, lane % win, own_len - win + lane % win)
    )
    first, last = jnp.maximum(pos - win, 0), jnp.minimum(pos + win, row_len - 1)
    for j in range(starts_ref.shape[1]):
        cut = starts_ref[:, j : j + 1]
        first = jnp.maximum(first, jnp.where(cut <= pos, cut, 0))
        last = jnp.minimum(last, jnp.where(cut > pos, cut - 1, row_len))
    for r in range(rows):
        bounds_ref[r, 0:1] = first[r : r + 1]
        bounds_ref[r, 1:2] = last[r : r + 1]

    order = halves_first()
    for c in range(0, 2 * width, WIDE):
        weight_ref[:, c : c + WIDE] = nn(in_ref[:, c : c + WIDE], order).astype(BF16)
    weight_ref[:, 2 * width :] = in_ref[:, 2 * width :]

    pair = 2
    cosine, sines = angles_ref[0, win : win + own_len], angles_ref[1, win : win + own_len]
    cosine, sines = jnp.concatenate([cosine] * pair), jnp.concatenate([sines] * pair)

    @pl.loop(0, rows // pair)
    def _(i):
        at = pl.ds(i * pair, pair)
        unit, _ = normalize(flat(tokens_ref[at]).astype(F32))
        normed = (unit * gain_ref[...]).astype(BF16)
        normed_ref[at] = normed.reshape(pair, own_len, width)
        for c in range(0, width, WIDE):
            part = turn(nn(normed, weight_ref[:, c : c + WIDE]), cosine * SCALE, sines * SCALE)
            queries_ref[at, :, c : c + WIDE] = part.astype(BF16).reshape(pair, own_len, WIDE)
            part = turn(nn(normed, weight_ref[:, width + c : width + c + WIDE]), cosine, sines)
            keys_ref[at, :, c : c + WIDE] = part.astype(BF16).reshape(pair, own_len, WIDE)
        values_ref[at] = nn(normed, weight_ref[:, 2 * width :]).astype(BF16).reshape(pair, own_len, width)


def halo_kernel(low_ref, high_ref, weight_ref, gain_ref, angles_ref, normed_ref, keys_ref, values_ref):
    rows, win, width = low_ref.shape
    pair = 3
    span = angles_ref.shape[1]
    cosine = jnp.concatenate([angles_ref[0, :win], angles_ref[0, span - win :]] * pair)
    sines = jnp.concatenate([angles_ref[1, :win], angles_ref[1, span - win :]] * pair)

    @pl.loop(0, rows // pair)
    def _(i):
        at = pl.ds(i * pair, pair)
        unit, _ = normalize(flat(jnp.concatenate([low_ref[at], high_ref[at]], axis=1)).astype(F32))
        normed = (unit * gain_ref[...]).astype(BF16)
        normed_ref[at] = normed.reshape(pair, 2 * win, width)
        for c in range(0, width, WIDE):
            part = turn(nn(normed, weight_ref[:, width + c : width + c + WIDE]), cosine, sines)
            keys_ref[at, :, c : c + WIDE] = part.astype(BF16).reshape(pair, 2 * win, WIDE)
        values_ref[at] = nn(normed, weight_ref[:, 2 * width :]).astype(BF16).reshape(pair, 2 * win, width)


def bias_of(bounds_ref, row, lanes, first_key, keys):
    key = first_key + iota((keys, LANES), 0)
    first, last = bounds_ref[row, 0:1, lanes], bounds_ref[row, 1:2, lanes]
    return jnp.where((key >= first) & (key <= last), 0.0, -jnp.inf)


def probabilities(scores, bias):
    parts = []
    for c in range(0, scores.shape[1], LANES):
        part = scores[:, c : c + LANES] + bias
        part = jnp.exp(part - jnp.max(part, axis=0, keepdims=True))
        parts.append(part * (1.0 / jnp.sum(part, axis=0, keepdims=True)))
    return jnp.concatenate(parts, axis=1)


def attend_mid_kernel(queries_ref, keys_ref, values_ref, bounds_ref, attended_ref, probs_ref):
    rows, own_len, width = queries_ref.shape
    win = HALF_WIN
    mid = own_len - 2 * win
    start = lax.axis_index("seq") * own_len
    pair = 2

    @pl.loop(0, rows // pair)
    def _(i):
        for r in range(pair):
            row = i * pair + r
            bias = bias_of(bounds_ref, row, slice(0, mid), start, own_len)
            for g in range(width // WIDE):
                cols = slice(g * WIDE, (g + 1) * WIDE)
                probs = probabilities(
                    nt(keys_ref[row, :, cols], by_head(queries_ref[row, win : win + mid, cols], True)), bias
                )
                probs_ref[row, g] = probs
                out = tn(probs.astype(BF16), values_ref[row, :, cols])
                attended_ref[row, :, cols] = pick_heads(out, False).astype(BF16)


def wide_side(own, halo, side):
    win = HALF_WIN
    if side == 0:
        return jnp.concatenate([halo[:win], own[: 2 * win]], axis=0)
    return jnp.concatenate([own[own.shape[0] - 2 * win :], halo[win:]], axis=0)


def attend_out_kernel(
    queries_ref, keys_ref, values_ref, halo_keys_ref, halo_values_ref, bounds_ref, attended_ref, probs_ref
):
    rows, own_len, width = queries_ref.shape
    win = HALF_WIN
    mid = own_len - 2 * win
    start = lax.axis_index("seq") * own_len
    pair = 2

    @pl.loop(0, rows // pair)
    def _(i):
        for r in range(pair):
            row = i * pair + r
            for side in range(2):
                own = slice(0, win) if side == 0 else slice(own_len - win, own_len)
                lanes = slice(mid + side * LANES, mid + (side + 1) * LANES)
                bias = bias_of(bounds_ref, row, lanes, start + own.start - win, 3 * win)
                for g in range(width // WIDE):
                    cols = slice(g * WIDE, (g + 1) * WIDE)
                    keys = wide_side(keys_ref[row, :, cols], halo_keys_ref[row, :, cols], side)
                    values = wide_side(values_ref[row, :, cols], halo_values_ref[row, :, cols], side)
                    probs = probabilities(nt(keys, by_head(queries_ref[row, own, cols], True)), bias)
                    probs_ref[row, side, g] = probs
                    out = tn(probs.astype(BF16), values)
                    attended_ref[row, side * win : (side + 1) * win, cols] = pick_heads(out, False).astype(BF16)


def gelu_parts(gate):
    bell = jnp.exp(-0.5 * gate * gate)
    t = 1.0 / (1.0 + (0.3275911 * 0.7071067811865476) * jnp.abs(gate))
    tail = t * (
        0.5 * 0.254829592
        + t * (0.5 * -0.284496736 + t * (0.5 * 1.421413741 + t * (0.5 * -1.453152027 + t * (0.5 * 1.061405429))))
    )
    tail = tail * bell
    return jnp.where(gate < 0, tail, 1.0 - tail), gate * bell * 0.3989422804014327


def part_of(ref, at, outer):
    own_len, win = ref.shape[1], HALF_WIN
    if outer:
        return flat(jnp.concatenate([ref[at, :win], ref[at, own_len - win :]], axis=1))
    return flat(ref[at, win : own_len - win])


def dense_kernel(
    outer,
    tokens_ref,
    top_ref,
    attended_ref,
    out_ref,
    up_ref,
    down_ref,
    gain_ref,
    middle_ref,
    normed_ref,
    mixed_ref,
    grad_up_ref,
    grad_middle_ref,
    branch_ref,
    grad_attended_ref,
):
    rows, count, width = attended_ref.shape
    hidden = down_ref.shape[0]
    pair = 3

    @pl.loop(0, rows // pair)
    def _(i):
        at = pl.ds(i * pair, pair)

        def put(ref, values, cols=slice(None)):
            ref[at, :, cols] = values.reshape(pair, count, -1)

        top = part_of(top_ref, at, outer)
        middle = part_of(tokens_ref, at, outer).astype(F32) + nn(flat(attended_ref[at]), out_ref[...])
        put(middle_ref, middle)
        unit, inverse = normalize(middle)
        normed = (unit * gain_ref[...]).astype(BF16)
        put(normed_ref, normed)
        for c in range(0, hidden, 256):
            gate = nn(normed, up_ref[:, c : c + 256])
            lift = nn(normed, up_ref[:, hidden + c : hidden + c + 256])
            grad_mixed = nt(top, down_ref[c : c + 256])
            phi, slope = gelu_parts(gate)
            active = gate * phi
            put(mixed_ref, (active * lift).astype(BF16), slice(c, c + 256))
            put(grad_up_ref, (grad_mixed * lift * (phi + slope)).astype(BF16), slice(c, c + 256))
            put(grad_up_ref, (grad_mixed * active).astype(BF16), slice(hidden + c, hidden + c + 256))
        grad_normed = nt(flat(grad_up_ref[at]), up_ref[...])
        grad_middle = top.astype(F32) + norm_back(grad_normed * gain_ref[...], unit, inverse)
        put(grad_middle_ref, grad_middle)
        branch = grad_middle.astype(BF16)
        put(branch_ref, branch)
        put(grad_attended_ref, nt(branch, out_ref[...]).astype(BF16))


def both(mid_ref, out_ref, cols=slice(None)):
    return jnp.concatenate([flat(mid_ref[:, :, cols]), flat(out_ref[:, :, cols])], axis=0)


def store_blocks(keep_ref, send_ref, store):
    seq, dp = lax.axis_index("seq"), lax.axis_index("dp")
    place = (dp % 2) * 16 + (dp // 2) * 8 + (seq % 2) * 4 + (seq // 2) % 4
    for ref, base in ((keep_ref, 0), (send_ref, BLOCKS // 2)):

        @pl.loop(0, BLOCKS // 2)
        def _(i):
            store(ref, i, place ^ (i + base))


def weights_kernel(
    top_ref,
    mid_normed_ref,
    out_normed_ref,
    mid_grad_up_ref,
    out_grad_up_ref,
    mid_mixed_ref,
    out_mixed_ref,
    mid_attended_ref,
    out_attended_ref,
    mid_branch_ref,
    out_branch_ref,
    keep_ref,
    send_ref,
    up_sum,
    out_sum,
    down_sum,
):
    width = top_ref.shape[2]
    everything = slice(0, top_ref.shape[0])
    normed = both(mid_normed_ref, out_normed_ref)
    for c in range(0, up_sum.shape[1], 256):
        cols = slice(c, c + 256)
        up_sum[:, cols] = tn(normed, both(mid_grad_up_ref, out_grad_up_ref, cols)).astype(BF16)
    top = jnp.concatenate([part_of(top_ref, everything, False), part_of(top_ref, everything, True)], axis=0)
    for c in range(0, down_sum.shape[0], 256):
        down_sum[c : c + 256] = tn(both(mid_mixed_ref, out_mixed_ref, slice(c, c + 256)), top)
    out_sum[...] = tn(both(mid_attended_ref, out_attended_ref), both(mid_branch_ref, out_branch_ref)).astype(BF16)
    rows, down_rows = width // BLOCKS, down_sum.shape[0] // BLOCKS

    def store(ref, i, block):
        own = pl.ds(pl.multiple_of(block * rows, rows), rows)
        at = 0
        for c in range(0, up_sum.shape[1], width):
            ref[i, at : at + rows] = up_sum[own, c : c + width]
            at += rows
        ref[i, at : at + rows] = out_sum[own, :]
        at += rows
        ref[i, at:] = down_sum[pl.ds(pl.multiple_of(block * down_rows, down_rows), down_rows), :].astype(BF16)

    store_blocks(keep_ref, send_ref, store)


def attend_back_kernel(
    group,
    queries_ref,
    keys_ref,
    values_ref,
    halo_keys_ref,
    halo_values_ref,
    mid_grad_ref,
    out_grad_ref,
    mid_probs_ref,
    out_probs_ref,
    angles_ref,
    own_ref,
    halo_ref,
):
    rows, own_len, _ = queries_ref.shape
    win = HALF_WIN
    mid = own_len - 2 * win
    cols = slice(group * WIDE, (group + 1) * WIDE)
    cosine, sines = angles_ref[0], angles_ref[1]
    own_cos, own_sin = cosine[win : win + own_len], sines[win : win + own_len]
    halo_cos = jnp.concatenate([cosine[:win], cosine[win + own_len :]])
    halo_sin = jnp.concatenate([sines[:win], sines[win + own_len :]])
    pair = 2

    def unit(queries, keys, values, grads, probs):
        q4, g4 = by_head(queries, True), by_head(grads, False)
        grad_probs = nt(values, g4)
        lows, grad_scores = [], []
        for c in range(0, probs.shape[1], LANES):
            part, grad_part = probs[:, c : c + LANES], grad_probs[:, c : c + LANES]
            inner = jnp.sum(part * grad_part, axis=0, keepdims=True)
            lows.append(part.astype(BF16))
            grad_scores.append((part * (grad_part - inner)).astype(BF16))
        grad_scores = jnp.concatenate(grad_scores, axis=1)
        return (
            pick_heads(tn(grad_scores, keys), True),
            nn(grad_scores, q4),
            nn(jnp.concatenate(lows, axis=1), g4),
        )

    @pl.loop(0, rows // pair)
    def _(i):
        for r in range(pair):
            row = i * pair + r
            queries, keys, values = queries_ref[row, :, cols], keys_ref[row, :, cols], values_ref[row, :, cols]
            halo_keys, halo_values = halo_keys_ref[row, :, cols], halo_values_ref[row, :, cols]
            grads = out_grad_ref[row, :, cols]
            middle = unit(queries[win : win + mid], keys, values, mid_grad_ref[row, :, cols], mid_probs_ref[row, group])
            sides = [
                unit(
                    queries[:win] if side == 0 else queries[own_len - win :],
                    wide_side(keys, halo_keys, side),
                    wide_side(values, halo_values, side),
                    grads[side * win : (side + 1) * win],
                    out_probs_ref[row, side, group],
                )
                for side in range(2)
            ]
            low, high = sides
            own = [jnp.concatenate([low[0], middle[0], high[0]], axis=0) * SCALE]
            halo = []
            for k in (1, 2):
                own.append(middle[k] + jnp.concatenate([low[k][win:], high[k][: 2 * win]], axis=0))
                halo.append(jnp.concatenate([low[k][:win], high[k][2 * win :]], axis=0))
            own_ref[row, :, :WIDE] = turn_back(own[0], own_cos, own_sin).astype(BF16)
            own_ref[row, :, WIDE : 2 * WIDE] = turn_back(own[1], own_cos, own_sin).astype(BF16)
            own_ref[row, :, 2 * WIDE :] = own[2].astype(BF16)
            halo_ref[row, :, :WIDE] = turn_back(halo[0], halo_cos, halo_sin).astype(BF16)
            halo_ref[row, :, WIDE:] = halo[1].astype(BF16)


def weight_in_kernel(normed_ref, halo_normed_ref, *refs):
    *grads, keep_ref, send_ref, total = refs
    width = normed_ref.shape[2]
    normed, halo_normed = flat(normed_ref[...]), flat(halo_normed_ref[...])
    normed_all = jnp.concatenate([normed, halo_normed], axis=0)
    order = halves_first()
    for g in range(len(grads) // 2):
        own, halo = grads[2 * g : 2 * g + 2]
        for k in range(3):
            part = flat(own[:, :, k * WIDE : (k + 1) * WIDE])
            if k == 0:
                part = tn(normed, part)
            else:
                part = tn(normed_all, jnp.concatenate([part, flat(halo[:, :, (k - 1) * WIDE : k * WIDE])], axis=0))
            part = part.astype(BF16)
            if k < 2:
                part = nt(part, order).astype(BF16)
            total[:, k * width + g * WIDE : k * width + (g + 1) * WIDE] = part
    rows = width // BLOCKS

    def store(ref, i, block):
        own = pl.ds(pl.multiple_of(block * rows, rows), rows)
        for k in range(3):
            ref[i, k * rows : (k + 1) * rows] = total[own, k * width : (k + 1) * width]

    store_blocks(keep_ref, send_ref, store)


def grad_halo_kernel(weight_ref, *refs):
    *grads, low_ref, high_ref = refs
    rows, win, width = low_ref.shape
    total = None
    for g, ref in enumerate(grads):
        weight = jnp.concatenate(
            [weight_ref[:, k * width + g * WIDE : k * width + (g + 1) * WIDE] for k in (1, 2)], axis=1
        )
        part = nt(flat(ref[...]), weight)
        total = part if total is None else total + part
    total = total.astype(BF16).reshape(rows, 2 * win, width)
    low_ref[...] = total[:, :win]
    high_ref[...] = total[:, win:]


def grad_own_kernel(weight_ref, *refs):
    *grads, out_ref = refs
    rows, own_len, width = out_ref.shape
    pair = 2
    groups = len(grads)

    @pl.loop(0, rows // pair)
    def _(i):
        at = pl.ds(i * pair, pair)
        grad = jnp.concatenate([flat(ref[at]) for ref in grads], axis=1)
        weight = jnp.concatenate(
            [
                weight_ref[:, k * width + g * WIDE : k * width + (g + 1) * WIDE]
                for g in range(groups)
                for k in range(3)
            ],
            axis=1,
        )
        out_ref[at] = nt(grad, weight).reshape(pair, own_len, width)


def result_kernel(mid_middle_ref, out_middle_ref, mid_mixed_ref, out_mixed_ref, down_ref, result_ref):
    own_len, win = result_ref.shape[1], HALF_WIN
    pair = 3

    @pl.loop(0, result_ref.shape[0] // pair)
    def _(i):
        at = pl.ds(i * pair, pair)

        def result(middle_ref, mixed_ref):
            total = flat(middle_ref[at]) + nn(flat(mixed_ref[at]), down_ref[...])
            return total.astype(BF16).reshape(middle_ref[at].shape)

        result_ref[at, win : own_len - win] = result(mid_middle_ref, mid_mixed_ref)
        outer = result(out_middle_ref, out_mixed_ref)
        result_ref[at, :win] = outer[:, :win]
        result_ref[at, own_len - win :] = outer[:, win:]


def finish_kernel(
    tokens_ref, own_ref, from_low_ref, from_high_ref, mid_grad_ref, out_grad_ref, gain_ref, grad_ref
):
    own_len, win = tokens_ref.shape[1], HALF_WIN

    @pl.loop(0, tokens_ref.shape[0])
    def _(row):
        unit, inverse = normalize(tokens_ref[row].astype(F32))
        own = own_ref[row]
        grads = jnp.concatenate(
            [
                own[:win] + from_low_ref[row].astype(F32),
                own[win : own_len - win],
                own[own_len - win :] + from_high_ref[row].astype(F32),
            ],
            axis=0,
        )
        outer = out_grad_ref[row]
        middle = jnp.concatenate([outer[:win], mid_grad_ref[row], outer[win:]], axis=0)
        grad_ref[row] = middle + norm_back(grads * gain_ref[...], unit, inverse)


def place_kernel(own_ref, other_ref, *out_refs):
    def store(ref, i, block):
        at = 0
        for out in out_refs:
            rows = out.shape[0] // BLOCKS
            for c in range(0, out.shape[1], ref.shape[2]):
                out[pl.ds(pl.multiple_of(block * rows, rows), rows), c : c + ref.shape[2]] = ref[
                    i, at : at + rows
                ].astype(F32)
                at += rows

    store_blocks(own_ref, other_ref, store)


def shift_route(size, distance):
    return [(i, i + distance) for i in range(size) if 0 <= i + distance < size]


def swap_route(core, x, y, z, rest):
    dp, seq = lax.axis_size("dp"), lax.axis_size("seq")

    def partner(i):
        d, s = divmod(i, seq)
        return (d ^ (core + 2 * x)) * seq + (s ^ (y + 2 * z + 8 * rest))

    return [(i, partner(i)) for i in range(dp * seq)]


def swap(values, core=0, x=0, y=0, z=0, rest=0):
    return lax.ppermute(values, ("dp", "seq"), swap_route(core, x, y, z, rest))


def add_all(*parts):
    return sum(p.astype(F32) for p in parts).astype(BF16)


def total_over_devices(keep, send):
    own = add_all(keep, swap(send, core=1))
    own = own.reshape((4, 4) + own.shape[1:])
    own = add_all(own[0], *[swap(own[k], x=k >> 1, y=k & 1) for k in (1, 2, 3)])
    own = add_all(own[0], *[swap(own[k], z=k) for k in (1, 2, 3)])
    rest = 1
    while 8 * rest < lax.axis_size("seq"):
        own = add_all(own, swap(own, rest=rest))
        rest *= 2
    own = jnp.stack([own] + [swap(own, z=k) for k in (1, 2, 3)])
    own = jnp.concatenate([own] + [swap(own, x=k >> 1, y=k & 1) for k in (1, 2, 3)])
    return own, swap(own, core=1)


def shape(*dims, kind=BF16):
    return jax.ShapeDtypeStruct(dims, kind)


def call(name, kernel, outs, *args, grant=16, flops=1e9, scratch=()):
    spec = pl.BlockSpec(memory_space=pltpu.VMEM)
    moved = sum(int(np.prod(a.shape)) * a.dtype.itemsize for a in (*args, *outs))
    return pl.pallas_call(
        kernel,
        out_shape=outs,
        in_specs=[spec] * len(args),
        out_specs=[spec] * len(outs),
        scratch_shapes=scratch,
        compiler_params=pltpu.CompilerParams(vmem_limit_bytes=grant * MB),
        cost_estimate=pl.CostEstimate(flops=int(flops), bytes_accessed=moved, transcendentals=0),
        name=name,
    )(*args)


def angle_tables(own_len, pieces):
    inverse = ROTARY_BASE ** (-(np.arange(0, HEAD_DIM, 2) / HEAD_DIM))
    inverse = np.tile(inverse, LANES // HALF)
    base = np.arange(pieces)[:, None] * own_len * inverse
    local = (np.arange(own_len + 2 * HALF_WIN) - HALF_WIN)[:, None] * inverse
    return [jnp.asarray(np.stack([np.cos(a), np.sin(a)], axis=d), F32) for a, d in ((base, 1), (local, 0))]


def shards(
    tokens,
    document_starts,
    attention_in,
    attention_out,
    feedforward_in,
    feedforward_out,
    gain_first,
    gain_second,
    result_grad,
):
    rows, own_len, width = tokens.shape
    hidden = feedforward_out.shape[0]
    win = HALF_WIN
    mid = own_len - 2 * win
    seq = lax.axis_size("seq")
    groups = width // WIDE
    gain_one, gain_two = gain_first[None], gain_second[None]

    up_route, down_route = shift_route(seq, 1), shift_route(seq, -1)
    low_tokens = lax.ppermute(tokens[:, own_len - win :], "seq", up_route)
    high_tokens = lax.ppermute(tokens[:, :win], "seq", down_route)

    row_shape = shape(rows, own_len, width)
    normed, queries, keys, values, weight, angles, bounds = call(
        "project",
        project_kernel,
        [row_shape] * 4
        + [
            shape(*attention_in.shape),
            shape(2, own_len + 2 * win, LANES, kind=F32),
            shape(rows, 2, mid + 4 * win, kind=jnp.int32),
        ],
        tokens,
        document_starts,
        attention_in,
        gain_one,
        *angle_tables(own_len, seq),
        flops=3e9,
    )
    mid_attended, mid_probs = call(
        "attend_mid",
        attend_mid_kernel,
        [shape(rows, mid, width), shape(rows, groups, own_len, GROUP * mid, kind=F32)],
        queries,
        keys,
        values,
        bounds,
        flops=2e9,
    )

    def dense(name, outer, attended):
        count = attended.shape[1]
        return call(
            name,
            functools.partial(dense_kernel, outer),
            [
                shape(rows, count, width, kind=F32),
                shape(rows, count, width),
                shape(rows, count, hidden),
                shape(rows, count, 2 * hidden),
                shape(rows, count, width, kind=F32),
                shape(rows, count, width),
                shape(rows, count, width),
            ],
            tokens,
            result_grad,
            attended,
            attention_out,
            feedforward_in,
            feedforward_out,
            gain_two,
            flops=5e9,
        )

    mid_middle, mid_normed, mid_mixed, mid_grad_up, mid_grad, mid_branch, mid_grad_attended = dense(
        "dense_mid", False, mid_attended
    )

    halo_normed, halo_keys, halo_values = call(
        "halo",
        halo_kernel,
        [shape(rows, 2 * win, width)] * 3,
        low_tokens,
        high_tokens,
        weight,
        gain_one,
        angles,
        flops=1e9,
    )
    out_attended, out_probs = call(
        "attend_out",
        attend_out_kernel,
        [shape(rows, 2 * win, width), shape(rows, 2, groups, 3 * win, GROUP * win, kind=F32)],
        queries,
        keys,
        values,
        halo_keys,
        halo_values,
        bounds,
        flops=2e9,
    )
    out_middle, out_normed, out_mixed, out_grad_up, out_grad, out_branch, out_grad_attended = dense(
        "dense_out", True, out_attended
    )

    piece = (feedforward_in.shape[1] // width * width + width + hidden) // BLOCKS
    keep_one, send_one = call(
        "weights",
        weights_kernel,
        [shape(BLOCKS // 2, piece, width)] * 2,
        result_grad,
        mid_normed,
        out_normed,
        mid_grad_up,
        out_grad_up,
        mid_mixed,
        out_mixed,
        mid_attended,
        out_attended,
        mid_branch,
        out_branch,
        flops=5e9,
        scratch=[
            pltpu.VMEM(feedforward_in.shape, BF16),
            pltpu.VMEM(attention_out.shape, BF16),
            pltpu.VMEM(feedforward_out.shape, F32),
        ],
    )

    own_grads, halo_grads = [], []
    for g in range(groups):
        own_part, halo_part = call(
            "attend_back_%d" % g,
            functools.partial(attend_back_kernel, g),
            [shape(rows, own_len, 3 * WIDE), shape(rows, 2 * win, 2 * WIDE)],
            queries,
            keys,
            values,
            halo_keys,
            halo_values,
            mid_grad_attended,
            out_grad_attended,
            mid_probs,
            out_probs,
            angles,
            flops=4e9,
        )
        own_grads.append(own_part)
        halo_grads.append(halo_part)
    keep_two, send_two = call(
        "weight_in",
        weight_in_kernel,
        [shape(BLOCKS // 2, attention_in.shape[1] // BLOCKS, width)] * 2,
        normed,
        halo_normed,
        *[a for pair in zip(own_grads, halo_grads) for a in pair],
        flops=4e9,
        scratch=[pltpu.VMEM(attention_in.shape, BF16)],
    )
    to_low, to_high = call(
        "grad_halo", grad_halo_kernel, [shape(rows, win, width)] * 2, weight, *halo_grads, flops=1e9
    )
    (own_grad,) = call(
        "grad_own", grad_own_kernel, [shape(rows, own_len, width, kind=F32)], weight, *own_grads, flops=2e9
    )

    total_one = total_over_devices(keep_one, send_one)
    total_two = total_over_devices(keep_two, send_two)
    from_high = lax.ppermute(to_low, "seq", down_route)
    from_low = lax.ppermute(to_high, "seq", up_route)

    (activations,) = call(
        "result", result_kernel, [row_shape], mid_middle, out_middle, mid_mixed, out_mixed, feedforward_out, flops=2e9
    )
    (grad_tokens,) = call(
        "finish",
        finish_kernel,
        [shape(rows, own_len, width, kind=F32)],
        tokens,
        own_grad,
        from_low,
        from_high,
        mid_grad,
        out_grad,
        gain_one,
        flops=1e8,
    )

    def placed(parts, *weights):
        return call("place", place_kernel, [shape(*w.shape, kind=F32) for w in weights], *parts, flops=1e6)

    grad_up, grad_out, grad_down = placed(total_one, feedforward_in, attention_out, feedforward_out)
    (grad_in,) = placed(total_two, attention_in)
    grad_gain_one = jnp.sum(grad_in * attention_in.astype(F32), axis=1) / gain_first
    grad_gain_two = jnp.sum(grad_up * feedforward_in.astype(F32), axis=1) / gain_second
    return activations, grad_tokens, grad_in, grad_out, grad_up, grad_down, grad_gain_one, grad_gain_two


def solution(mesh):
    token, rest = P("dp", "seq", None), P()
    return jax.shard_map(
        shards,
        mesh=mesh,
        in_specs=(token, P("dp", None)) + (rest,) * 6 + (token,),
        out_specs=(token, token) + (rest,) * 6,
        check_vma=False,
    )
```

time: 648 us -> 195 us (0.30); the launches traced: 639 us -> 194 us
  matrix products: 251 us -> 0 us
  waiting for transfers between devices: 161 us -> 64.8 us
  local copies, waits for them, and re-layouts: 104 us -> 7.93 us
  Pallas kernels: 0 us -> 67.3 us
  blocking collectives: 43.5 us -> 0 us
  other arithmetic: 50.2 us -> 6.94 us
  starting transfers between devices: 14.3 us -> 45.9 us
  between operations: 15.4 us -> 1.43 us
    dot_general x17 -> x0, matrix products: 239 us -> none  [the longest x1 85.6 us: shards(): jnp.einsum('mhqk,mkhd->mqhd', grad_scores, wide_keys, preferred_element_t...]
    psum x1 -> x0, waiting for transfers between devices: 129 us -> none  [shards(): lax.psum((grad_in_weight, grad_out_weight, second_sums[0], second_sums[1]...]
    pallas_call x0 -> x16, Pallas kernels: none -> 67.3 us  [call(): pl.pallas_call(kernel, out_shape=outs, in_specs=[spec] * len(args), out_s...]
    reshape x11 -> x0, local copies, waits for them, and re-layouts: 46.4 us -> none  [the longest x2 11.7 us: shards(): projected[:, :model_width].reshape(head_shape)]
    psum x1 -> x0, blocking collectives: 43.5 us -> none  [shards(): lax.psum((grad_in_weight, grad_out_weight, second_sums[0], second_sums[1]...]
    ppermute x4 -> x32, waiting for transfers between devices: 31.9 us -> 64.8 us  [the longest x28 54.6 us: swap(): return lax.ppermute(values, ('dp', 'seq'), swap_route(core, x, y, z, rest))]
    ppermute x4 -> x32, starting transfers between devices: 14.3 us -> 45.9 us  [the longest x28 34 us: swap(): return lax.ppermute(values, ('dp', 'seq'), swap_route(core, x, y, z, rest))]
    slice x10 -> x3, local copies, waits for them, and re-layouts: 23.6 us -> 1.41 us  [the longest x1 1.29 us: shards(): high_tokens = lax.ppermute(tokens[:, :win], 'seq', down_route)]
  transfers between devices with their start and end apart: 5 -> 32, of which waited for: 3 -> 14; matrix products, arithmetic and copies ran while one was open for 7% -> 2% of each run, Pallas kernels for 0% -> 17%
where the time goes in v2:
time: 195 us; the launch traced here: 194 us
  Pallas kernels  67.3 us (35%)
  waiting for transfers between devices  64.8 us (33%)
  starting transfers between devices  45.9 us (24%)
  local copies, waits for them, and re-layouts  7.93 us (4%)
  other arithmetic  6.94 us (4%)
    pallas_call x16, Pallas kernels, call(): pl.pallas_call(kernel, out_shape=outs, in_specs=[spec] * len(args), out_s...  67.3 us
    ppermute x28, waiting for transfers between devices, swap(): return lax.ppermute(values, ('dp', 'seq'), swap_route(core, x, y, z, rest))  54.6 us
    ppermute x28, starting transfers between devices, swap(): return lax.ppermute(values, ('dp', 'seq'), swap_route(core, x, y, z, rest))  34 us
    ppermute x1, waiting for transfers between devices, shards(): from_low = lax.ppermute(to_high, 'seq', up_route)  10.2 us
    unnamed x86, local copies, waits for them, and re-layouts  6.44 us
    ppermute x1, starting transfers between devices, shards(): low_tokens = lax.ppermute(tokens[:, own_len - win:], 'seq', up_route)  5.52 us
  transfers between devices with their start and end apart: 32, of which 14 were waited for; matrix products, arithmetic and copies ran while one was open for 2% of the time, Pallas kernels for 17%

profile of v2, /device:TPU:0, one launch (start us, length us, event | category | flops | bytes accessed | tf_op | source)
XLA Modules:
  0.0 194.4 jit_solution(1436448750517526606)
XLA Ops:
  3.2 5.5 %collective-permute-start = (bf16[6,64,512]{2,1,0:T(8,128)(2,1)S(1)}, bf16[6,64,512]{2,1,0:T(8,128)(2,1)S(1)}, u32[]{:S(2)}, u32[]{:S(2)}) collective-permute-start(bf16[6,64,512]{2,1,0:T(8,128)(2,1)S(1)} %get-tuple-element.95), channel_id=1, source_target_pairs={{0,1},{1,2},{2,3},{3,4},{4,5},{5,6},{6,7},{8,9},{9,10},{10,11},{11... | collective-permute-start | bytes 1179656 | tf_op jit(solution)/shard_map/ppermute | solution.py:653
  8.8 1.4 copy-done.1
  12.6 4.4 %project.1 = (bf16[6,256,512]{2,1,0:T(8,128)(2,1)S(1)}, bf16[6,256,512]{2,1,0:T(8,128)(2,1)S(1)}, bf16[6,256,512]{2,1,0:T(8,128)(2,1)S(1)}, bf16[6,256,512]{2,1,...) custom-call(bf16[6,256,512]{2,1,0:T(8,128)(2,1)S(1)} %copy-done, ...), custom_call_target="tpu_custom_call" | custom-call | flops 3000000000 | bytes 11825536 | tf_op jit(solution)/shard_map/project/pallas_call | solution.py:613
  17.1 3.9 %attend_mid.1 = (bf16[6,128,512]{2,1,0:T(8,128)(2,1)S(1)}, f32[6,2,256,512]{3,2,1,0:T(8,128)S(1)}) custom-call(bf16[6,256,512]{2,1,0:T(8,128)(2,1)S(1)} %get-tuple-element.49.queries_ref, bf16[6,256,512]{2,1,0:T(8,128)(2,1)S(1)} %get-tuple-element.50.keys_ref, bf16[6,256,512]{2,1,0:T(8,128)(2,1)S(1)} %get-tuple-element.51.values_ref, ...), custom_call_target="tpu_custom_call" | custom-call | flops 2000000000 | bytes 11814912 | tf_op jit(solution)/shard_map/attend_mid/pallas_call | solution.py:613
  21.1 6.7 %dense_mid.1 = (f32[6,128,512]{2,1,0:T(8,128)S(1)}, bf16[6,128,512]{2,1,0:T(8,128)(2,1)S(1)}, bf16[6,128,768]{2,1,0:T(8,128)(2,1)S(1)}, bf16[6,128,1536]{2,1,0:T...) custom-call(bf16[6,256,512]{2,1,0:T(8,128)(2,1)S(1)} %copy-done, ...), custom_call_target="tpu_custom_call" | custom-call | flops 5000000000 | bytes 15861760 | tf_op jit(solution)/shard_map/dense_mid/pallas_call | solution.py:613
  28.7 1.7 halo.1
  30.4 4.1 %attend_out.1 = (bf16[6,128,512]{2,1,0:T(8,128)(2,1)S(1)}, f32[6,2,2,192,256]{4,3,2,1,0:T(8,128)S(1)}) custom-call(bf16[6,256,512]{2,1,0:T(8,128)(2,1)S(1)} %get-tuple-element.49.queries_ref, bf16[6,256,512]{2,1,0:T(8,128)(2,1)S(1)} %get-tuple-element.50.keys_ref, bf16[6,256,512]{2,1,0:T(8,128)(2,1)S(1)} %get-tuple-element.51.values_ref, ...), custom_call_target="tpu_custom_call" | custom-call | flops 2000000000 | bytes 11814912 | tf_op jit(solution)/shard_map/attend_out/pallas_call | solution.py:613
  34.6 6.6 %dense_out.1 = (f32[6,128,512]{2,1,0:T(8,128)S(1)}, bf16[6,128,512]{2,1,0:T(8,128)(2,1)S(1)}, bf16[6,128,768]{2,1,0:T(8,128)(2,1)S(1)}, bf16[6,128,1536]{2,1,0:T...) custom-call(bf16[6,256,512]{2,1,0:T(8,128)(2,1)S(1)} %copy-done, ...), custom_call_target="tpu_custom_call" | custom-call | flops 5000000000 | bytes 15861760 | tf_op jit(solution)/shard_map/dense_out/pallas_call | solution.py:613
  41.2 1.4 copy-done.30
  42.6 6.5 %attend_back_1.1 = (bf16[6,256,768]{2,1,0:T(8,128)(2,1)S(1)}, bf16[6,128,512]{2,1,0:T(8,128)(2,1)S(1)}) custom-call(bf16[6,256,512]{2,1,0:T(8,128)(2,1)S(1)} %get-tuple-element.49.queries_ref, bf16[6,256,512]{2,1,0:T(8,128)(2,1)S(1)} %get-tuple-element.50.keys_ref, bf16[6,256,512]{2,1,0:T(8,128)(2,1)S(1)} %get-tuple-element.51.values_ref, ...), custom_call_target="tpu_custom_call" | custom-call | flops 4000000000 | bytes 22413312 | tf_op jit(solution)/shard_map/attend_back_1/pallas_call | solution.py:613
  49.2 6.7 %attend_back_0.1 = (bf16[6,256,768]{2,1,0:T(8,128)(2,1)S(1)}, bf16[6,128,512]{2,1,0:T(8,128)(2,1)S(1)}) custom-call(bf16[6,256,512]{2,1,0:T(8,128)(2,1)S(1)} %get-tuple-element.49.queries_ref, bf16[6,256,512]{2,1,0:T(8,128)(2,1)S(1)} %get-tuple-element.50.keys_ref, bf16[6,256,512]{2,1,0:T(8,128)(2,1)S(1)} %get-tuple-element.51.values_ref, ...), custom_call_target="tpu_custom_call" | custom-call | flops 4000000000 | bytes 22413312 | tf_op jit(solution)/shard_map/attend_back_0/pallas_call | solution.py:613
  56.0 5.8 %weight_in.1 = (bf16[16,48,512]{2,1,0:T(8,128)(2,1)S(1)}, bf16[16,48,512]{2,1,0:T(8,128)(2,1)S(1)}) custom-call(bf16[6,256,512]{2,1,0:T(8,128)(2,1)S(1)} %copy-done.33, bf16[6,128,512]{2,1,0:T(8,128)(2,1)S(1)} %get-tuple-element.76.halo_normed_ref, bf16[6,256,768]{2,1,0:T(8,128)(2,1)S(1)} %get-tuple-element.67.refs_0_, ...), custom_call_target="tpu_custom_call" | custom-call | flops 4000000000 | bytes 10223616 | tf_op jit(solution)/shard_map/weight_in/pallas_call | solution.py:613
  62.0 5.2 %weights.1 = (bf16[16,88,512]{2,1,0:T(8,128)(2,1)S(1)}, bf16[16,88,512]{2,1,0:T(8,128)(2,1)S(1)}) custom-call(bf16[6,256,512]{2,1,0:T(8,128)(2,1)S(1)} %copy-done.15, bf16[6,128,512]{2,1,0:T(8,128)(2,1)S(1)} %copy-done.35, bf16[6,128,512]{2,1,0:T(8,128)(2,1)S(1)} %get-tuple-element.80.out_normed_ref, bf16[6,128,1536]{2,1,0:T(8,128)(2,1)S(1)} %copy-done.29, ...), custom_call_target="tpu_custom_call" | custom-call | flops 5000000000 | bytes 16252928 | tf_op jit(solution)/shard_map/weights/pallas_call | solution.py:613
  68.1 3.0 %collective-permute-start.5 = (bf16[4,48,512]{2,1,0:T(8,128)(2,1)S(1)}, bf16[4,48,512]{2,1,0:T(8,128)(2,1)S(1)}, u32[]{:S(2)}, u32[]{:S(2)}) collective-permute-start(bf16[4,48,512]{2,1,0:T(8,128)(2,1)S(1)} %get-tuple-element.99), channel_id=1, source_target_pairs={{0,1},{1,0},{2,3},{3,2},{4,5},{5,4},{6,7},{7,6},{8,9},{9,8},{10,11... | collective-permute-start | bytes 589832 | tf_op jit(solution)/shard_map/ppermute | solution.py:585
  72.6 7.8 %collective-permute-done.5 = bf16[4,48,512]{2,1,0:T(8,128)(2,1)S(1)} collective-permute-done((bf16[4,48,512]{2,1,0:T(8,128)(2,1)S(1)}, bf16[4,48,512]{2,1,0:T(8,128)(2,1)S(1)}, u32[]{:S(2)}, u32[]{:S(2)}) %collective-permute-start.5) | collective-permute-done | bytes 196640 | tf_op jit(solution)/shard_map/ppermute | solution.py:585
  80.3 1.3 collective-permute-done.6
  81.8 1.6 collective-permute-start.8
  83.4 2.5 %collective-permute-start.10 = (bf16[48,512]{1,0:T(8,128)(2,1)S(1)}, bf16[48,512]{1,0:T(8,128)(2,1)S(1)}, u32[]{:S(2)}, u32[]{:S(2)}) collective-permute-start(bf16[48,512]{1,0:T(8,128)(2,1)S(1)} %get-tuple-element.106), channel_id=1, source_target_pairs={{0,6},{1,7},{2,4},{3,5},{4,2},{5,3},{6,0},{7,1},{8,14},{9,15},{10,... | collective-permute-start | bytes 147464 | tf_op jit(solution)/shard_map/ppermute | solution.py:585
  85.9 3.4 %collective-permute-done.10 = bf16[48,512]{1,0:T(8,128)(2,1)S(1)} collective-permute-done((bf16[48,512]{1,0:T(8,128)(2,1)S(1)}, bf16[48,512]{1,0:T(8,128)(2,1)S(1)}, u32[]{:S(2)}, u32[]{:S(2)}) %collective-permute-start.10) | collective-permute-done | bytes 49184 | tf_op jit(solution)/shard_map/ppermute | solution.py:585
  89.4 1.8 collective-permute-done.9
  91.2 1.9 collective-permute-start.13
  93.0 2.6 %collective-permute-start.11 = (bf16[48,512]{1,0:T(8,128)(2,1)S(1)}, bf16[48,512]{1,0:T(8,128)(2,1)S(1)}, u32[]{:S(2)}, u32[]{:S(2)}) collective-permute-start(bf16[48,512]{1,0:T(8,128)(2,1)S(1)} %get-tuple-element.93), channel_id=1, source_target_pairs={{0,2},{1,3},{2,0},{3,1},{4,6},{5,7},{6,4},{7,5},{8,10},{9,11},{10,... | collective-permute-start | bytes 147464 | tf_op jit(solution)/shard_map/ppermute | solution.py:585
  96.1 1.8 collective-permute-start.19
  99.7 2.8 %collective-permute-start.16 = (bf16[4,48,512]{2,1,0:T(8,128)(2,1)S(1)}, bf16[4,48,512]{2,1,0:T(8,128)(2,1)S(1)}, u32[]{:S(2)}, u32[]{:S(2)}) collective-permute-start(bf16[4,48,512]{2,1,0:T(8,128)(2,1)S(1)} %pad_maximum_fusion.1), channel_id=1, source_target_pairs={{0,17},{1,16},{2,19},{3,18},{4,21},{5,20},{6,23},{7,22},{8,25},{9,... | collective-permute-start | bytes 589832 | tf_op jit(solution)/shard_map/ppermute | solution.py:585
  103.0 10.3 %collective-permute-done.19 = bf16[4,88,512]{2,1,0:T(8,128)(2,1)S(1)} collective-permute-done((bf16[4,88,512]{2,1,0:T(8,128)(2,1)S(1)}, bf16[4,88,512]{2,1,0:T(8,128)(2,1)S(1)}, u32[]{:S(2)}, u32[]{:S(2)}) %collective-permute-start.19) | collective-permute-done | bytes 360480 | tf_op jit(solution)/shard_map/ppermute | solution.py:585
  113.3 3.3 %collective-permute-done.20 = bf16[4,88,512]{2,1,0:T(8,128)(2,1)S(1)} collective-permute-done((bf16[4,88,512]{2,1,0:T(8,128)(2,1)S(1)}, bf16[4,88,512]{2,1,0:T(8,128)(2,1)S(1)}, u32[]{:S(2)}, u32[]{:S(2)}) %collective-permute-start.20) | collective-permute-done | bytes 360480 | tf_op jit(solution)/shard_map/ppermute | solution.py:585
  117.0 1.9 collective-permute-start.24
  118.9 1.5 collective-permute-start.23
  121.5 2.0 %collective-permute-done.24 = bf16[88,512]{1,0:T(8,128)(2,1)S(1)} collective-permute-done((bf16[88,512]{1,0:T(8,128)(2,1)S(1)}, bf16[88,512]{1,0:T(8,128)(2,1)S(1)}, u32[]{:S(2)}, u32[]{:S(2)}) %collective-permute-start.24) | collective-permute-done | bytes 90144 | tf_op jit(solution)/shard_map/ppermute | solution.py:585
  123.5 5.2 %collective-permute-done.23 = bf16[88,512]{1,0:T(8,128)(2,1)S(1)} collective-permute-done((bf16[88,512]{1,0:T(8,128)(2,1)S(1)}, bf16[88,512]{1,0:T(8,128)(2,1)S(1)}, u32[]{:S(2)}, u32[]{:S(2)}) %collective-permute-start.23) | collective-permute-done | bytes 90144 | tf_op jit(solution)/shard_map/ppermute | solution.py:585
  128.8 1.9 collective-permute-start.27
  130.7 2.5 %collective-permute-start.25 = (bf16[88,512]{1,0:T(8,128)(2,1)S(1)}, bf16[88,512]{1,0:T(8,128)(2,1)S(1)}, u32[]{:S(2)}, u32[]{:S(2)}) collective-permute-start(bf16[88,512]{1,0:T(8,128)(2,1)S(1)} %get-tuple-element.91), channel_id=1, source_target_pairs={{0,2},{1,3},{2,0},{3,1},{4,6},{5,7},{6,4},{7,5},{8,10},{9,11},{10,... | collective-permute-start | bytes 270344 | tf_op jit(solution)/shard_map/ppermute | solution.py:585
  133.2 2.0 %collective-permute-done.27 = bf16[88,512]{1,0:T(8,128)(2,1)S(1)} collective-permute-done((bf16[88,512]{1,0:T(8,128)(2,1)S(1)}, bf16[88,512]{1,0:T(8,128)(2,1)S(1)}, u32[]{:S(2)}, u32[]{:S(2)}) %collective-permute-start.27) | collective-permute-done | bytes 90144 | tf_op jit(solution)/shard_map/ppermute | solution.py:585
  135.2 1.9 collective-permute-done.26
  137.2 2.8 %collective-permute-start.30 = (bf16[4,88,512]{2,1,0:T(8,128)(2,1)S(1)}, bf16[4,88,512]{2,1,0:T(8,128)(2,1)S(1)}, u32[]{:S(2)}, u32[]{:S(2)}) collective-permute-start(bf16[4,88,512]{2,1,0:T(8,128)(2,1)S(1)} %pad_maximum_fusion), channel_id=1, source_target_pairs={{0,17},{1,16},{2,19},{3,18},{4,21},{5,20},{6,23},{7,22},{8,25},{9,... | collective-permute-start | bytes 1081352 | tf_op jit(solution)/shard_map/ppermute | solution.py:585
  140.8 10.7 %collective-permute-done.28 = bf16[4,88,512]{2,1,0:T(8,128)(2,1)S(1)} collective-permute-done((bf16[4,88,512]{2,1,0:T(8,128)(2,1)S(1)}, bf16[4,88,512]{2,1,0:T(8,128)(2,1)S(1)}, u32[]{:S(2)}, u32[]{:S(2)}) %collective-permute-start.28) | collective-permute-done | bytes 360480 | tf_op jit(solution)/shard_map/ppermute | solution.py:585
  151.5 1.8 collective-permute-start.14
  153.5 3.7 %collective-permute-done.14 = bf16[4,48,512]{2,1,0:T(8,128)(2,1)S(1)} collective-permute-done((bf16[4,48,512]{2,1,0:T(8,128)(2,1)S(1)}, bf16[4,48,512]{2,1,0:T(8,128)(2,1)S(1)}, u32[]{:S(2)}, u32[]{:S(2)}) %collective-permute-start.14) | collective-permute-done | bytes 196640 | tf_op jit(solution)/shard_map/ppermute | solution.py:585
  158.4 3.7 %collective-permute-start.2 = (bf16[6,64,512]{2,1,0:T(8,128)(2,1)S(1)}, bf16[6,64,512]{2,1,0:T(8,128)(2,1)S(1)}, u32[]{:S(2)}, u32[]{:S(2)}) collective-permute-start(bf16[6,64,512]{2,1,0:T(8,128)(2,1)S(1)} %get-tuple-element.71), channel_id=1, source_target_pairs={{0,1},{1,2},{2,3},{3,4},{4,5},{5,6},{6,7},{8,9},{9,10},{10,11},{11... | collective-permute-start | bytes 1179656 | tf_op jit(solution)/shard_map/ppermute | solution.py:803
  162.1 1.4 collective-permute-start.3
  163.6 3.0 %grad_own.1.own_ref = f32[6,256,512]{2,1,0:T(8,128)S(1)} custom-call(bf16[512,1536]{1,0:T(8,128)(2,1)S(1)} %get-tuple-element.55.weight_ref, bf16[6,256,768]{2,1,0:T(8,128)(2,1)S(1)} %get-tuple-element.67.refs_0_, bf16[6,256,768]{2,1,0:T(8,128)(2,1)S(1)} %get-tuple-element.68.refs_1_.refs_2_), custom_call_target="tpu_custom_call" | custom-call | flops 2000000000 | bytes 9437184 | tf_op jit(solution)/shard_map/grad_own/pallas_call | solution.py:613
  166.6 2.7 %result.1 = bf16[6,256,512]{2,1,0:T(8,128)(2,1)} custom-call(f32[6,128,512]{2,1,0:T(8,128)S(1)} %get-tuple-element.54.mid_middle_ref, f32[6,128,512]{2,1,0:T(8,128)S(1)} %copy-done.5, bf16[6,128,768]{2,1,0:T(8,128)(2,1)S(1)} %copy-done.7, bf16[6,128,768]{2,1,0:T(8,128)(2,1)S(1)} %copy-done.9, bf16[768,512]{1,0:T(8,128)(2,1)S(1)} %copy-done.11), custom_call_target="tpu_custom_call" | custom-call | flops 2000000000 | bytes 7864320 | tf_op jit(solution)/shard_map/result/pallas_call | solution.py:613
  169.3 10.2 %collective-permute-done.2.from_low_ref = bf16[6,64,512]{2,1,0:T(8,128)(2,1)S(1)} collective-permute-done((bf16[6,64,512]{2,1,0:T(8,128)(2,1)S(1)}, bf16[6,64,512]{2,1,0:T(8,128)(2,1)S(1)}, u32[]{:S(2)}, u32[]{:S(2)}) %collective-permute-start.2) | collective-permute-done | bytes 393248 | tf_op jit(solution)/shard_map/ppermute | solution.py:803
  179.5 4.0 %finish.1 = f32[6,256,512]{2,1,0:T(8,128)} custom-call(bf16[6,256,512]{2,1,0:T(8,128)(2,1)S(1)} %copy-done, f32[6,256,512]{2,1,0:T(8,128)S(1)} %grad_own.1.own_ref, bf16[6,64,512]{2,1,0:T(8,128)(2,1)S(1)} %collective-permute-done.2.from_low_ref, bf16[6,64,512]{2,1,0:T(8,128)(2,1)S(1)} %collective-permute-done.3.from_high_ref, ...), custom_call_target="tpu_custom_call" | custom-call | flops 100000000 | bytes 11798528 | tf_op jit(solution)/shard_map/finish/pallas_call | solution.py:613
  183.5 2.0 %place.2 = f32[512,1536]{1,0:T(8,128)} custom-call(bf16[16,48,512]{2,1,0:T(8,128)(2,1)S(1)} %constant_dynamic-update-slice_fusion.own_ref, bf16[16,48,512]{2,1,0:T(8,128)(2,1)S(1)} %collective-permute-done.17.other_ref), custom_call_target="tpu_custom_call" | custom-call | flops 1000000 | bytes 4718592 | tf_op jit(solution)/shard_map/place/pallas_call | solution.py:613
  185.5 2.3 %multiply_reduce_fusion.1 = f32[512]{0:T(512)S(1)} fusion(f32[512,1536]{1,0:T(8,128)} %place.2, bf16[512,1536]{1,0:T(8,128)(2,1)S(1)} %copy-done.2), kind=kLoop, calls=%fused_computation.1 | loop fusion | flops 2358784 | bytes 4720640 | tf_op jit(solution)/shard_map/reduce_sum | solution.py:827
  188.4 3.0 %place.3 = (f32[512,1536]{1,0:T(8,128)}, f32[512,512]{1,0:T(8,128)}, f32[768,512]{1,0:T(8,128)}) custom-call(bf16[16,88,512]{2,1,0:T(8,128)(2,1)S(1)} %constant_dynamic-update-slice_fusion.7.own_ref, bf16[16,88,512]{2,1,0:T(8,128)(2,1)S(1)} %collective-permute-done.31.other_ref), custom_call_target="tpu_custom_call" | custom-call | flops 1000000 | bytes 8650752 | tf_op jit(solution)/shard_map/place/pallas_call | solution.py:613
  191.4 2.3 %multiply_reduce_fusion = f32[512]{0:T(512)S(1)} fusion(f32[512,1536]{1,0:T(8,128)} %get-tuple-element.45, bf16[512,1536]{1,0:T(8,128)(2,1)S(1)} %copy-done.3), kind=kLoop, calls=%fused_computation | loop fusion | flops 2358784 | bytes 4720640 | tf_op jit(solution)/shard_map/reduce_sum | solution.py:828
  (137 shorter events, 16.3 us)
Async XLA Ops:
  0.6 8.1 %copy-start = (bf16[6,256,512]{2,1,0:T(8,128)(2,1)S(1)}, bf16[6,256,512]{2,1,0:T(8,128)(2,1)}, u32[]{:S(2)}) copy-start(bf16[6,256,512]{2,1,0:T(8,128)(2,1)} %tokens_ref.7) | copy-start | bytes 4718596
  0.6 8.1 %copy-start.12 = (f32[512]{0:T(512)S(1)}, f32[512]{0:T(512)}, u32[]{:S(2)}) copy-start(f32[512]{0:T(512)} %param.17) | copy-start | bytes 6148
  1.9 26.7 %collective-permute-start.1 = (bf16[6,64,512]{2,1,0:T(8,128)(2,1)S(1)}, bf16[6,64,512]{2,1,0:T(8,128)(2,1)S(1)}, u32[]{:S(2)}, u32[]{:S(2)}) collective-permute-start(bf16[6,64,512]{2,1,0:T(8,128)(2,1)S(1)} %get-tuple-element.94), channel_id=1, source_target_pairs={{1,0},{2,1},{3,2},{4,3},{5,4},{6,5},{7,6},{9,8},{10,9},{11,10},{12... | collective-permute-start | bytes 1179656 | tf_op jit(solution)/shard_map/ppermute | solution.py:654
  3.2 25.4 %collective-permute-start = (bf16[6,64,512]{2,1,0:T(8,128)(2,1)S(1)}, bf16[6,64,512]{2,1,0:T(8,128)(2,1)S(1)}, u32[]{:S(2)}, u32[]{:S(2)}) collective-permute-start(bf16[6,64,512]{2,1,0:T(8,128)(2,1)S(1)} %get-tuple-element.95), channel_id=1, source_target_pairs={{0,1},{1,2},{2,3},{3,4},{4,5},{5,6},{6,7},{8,9},{9,10},{10,11},{11... | collective-permute-start | bytes 1179656 | tf_op jit(solution)/shard_map/ppermute | solution.py:653
  21.0 6.7 %copy-start.26 = (bf16[6,128,512]{2,1,0:T(8,128)(2,1)}, bf16[6,128,512]{2,1,0:T(8,128)(2,1)S(1)}, u32[]{:S(2)}) copy-start(bf16[6,128,512]{2,1,0:T(8,128)(2,1)S(1)} %get-tuple-element.53.attended_ref.mid_attended_ref) | copy-start | bytes 2359300
  34.6 6.6 %copy-start.24 = (bf16[6,128,512]{2,1,0:T(8,128)(2,1)}, bf16[6,128,512]{2,1,0:T(8,128)(2,1)S(1)}, u32[]{:S(2)}) copy-start(bf16[6,128,512]{2,1,0:T(8,128)(2,1)S(1)} %get-tuple-element.59.attended_ref.out_attended_ref) | copy-start | bytes 2359300
  42.6 6.5 %copy-start.4 = (f32[6,128,512]{2,1,0:T(8,128)}, f32[6,128,512]{2,1,0:T(8,128)S(1)}, u32[]{:S(2)}) copy-start(f32[6,128,512]{2,1,0:T(8,128)S(1)} %get-tuple-element.60.out_middle_ref) | copy-start | bytes 4718596
  42.6 6.5 %copy-start.8 = (bf16[6,128,768]{2,1,0:T(8,128)(2,1)}, bf16[6,128,768]{2,1,0:T(8,128)(2,1)S(1)}, u32[]{:S(2)}) copy-start(bf16[6,128,768]{2,1,0:T(8,128)(2,1)S(1)} %get-tuple-element.62.out_mixed_ref) | copy-start | bytes 3538948
  42.6 6.5 %copy-start.36 = (bf16[6,128,512]{2,1,0:T(8,128)(2,1)}, bf16[6,128,512]{2,1,0:T(8,128)(2,1)S(1)}, u32[]{:S(2)}) copy-start(bf16[6,128,512]{2,1,0:T(8,128)(2,1)S(1)} %get-tuple-element.84.out_branch_ref) | copy-start | bytes 2359300
  49.1 6.7 %copy-start.16 = (bf16[6,128,512]{2,1,0:T(8,128)(2,1)}, bf16[6,128,512]{2,1,0:T(8,128)(2,1)S(1)}, u32[]{:S(2)}) copy-start(bf16[6,128,512]{2,1,0:T(8,128)(2,1)S(1)} %get-tuple-element.70.refs_1_.refs_3_) | copy-start | bytes 2359300
  49.1 6.7 %copy-start.33 = (bf16[6,256,512]{2,1,0:T(8,128)(2,1)S(1)}, bf16[6,256,512]{2,1,0:T(8,128)(2,1)}, u32[]{:S(2)}) copy-start(bf16[6,256,512]{2,1,0:T(8,128)(2,1)} %copy-done.32) | copy-start | bytes 4718596
  55.9 6.0 %copy-start.7 = (bf16[6,128,768]{2,1,0:T(8,128)(2,1)S(1)}, bf16[6,128,768]{2,1,0:T(8,128)(2,1)}, u32[]{:S(2)}) copy-start(bf16[6,128,768]{2,1,0:T(8,128)(2,1)} %copy-done.6) | copy-start | bytes 3538948
  55.9 6.0 %copy-start.9 = (bf16[6,128,768]{2,1,0:T(8,128)(2,1)S(1)}, bf16[6,128,768]{2,1,0:T(8,128)(2,1)}, u32[]{:S(2)}) copy-start(bf16[6,128,768]{2,1,0:T(8,128)(2,1)} %copy-done.8) | copy-start | bytes 3538948
  55.9 6.0 %copy-start.15 = (bf16[6,256,512]{2,1,0:T(8,128)(2,1)S(1)}, bf16[6,256,512]{2,1,0:T(8,128)(2,1)}, u32[]{:S(2)}) copy-start(bf16[6,256,512]{2,1,0:T(8,128)(2,1)} %top_ref.5) | copy-start | bytes 4718596
  55.9 6.0 %copy-start.25 = (bf16[6,128,512]{2,1,0:T(8,128)(2,1)S(1)}, bf16[6,128,512]{2,1,0:T(8,128)(2,1)}, u32[]{:S(2)}) copy-start(bf16[6,128,512]{2,1,0:T(8,128)(2,1)} %copy-done.24) | copy-start | bytes 2359300
  55.9 6.0 %copy-start.27 = (bf16[6,128,512]{2,1,0:T(8,128)(2,1)S(1)}, bf16[6,128,512]{2,1,0:T(8,128)(2,1)}, u32[]{:S(2)}) copy-start(bf16[6,128,512]{2,1,0:T(8,128)(2,1)} %copy-done.26) | copy-start | bytes 2359300
  61.8 6.0 %collective-permute-start.4 = (bf16[16,48,512]{2,1,0:T(8,128)(2,1)S(1)}, bf16[16,48,512]{2,1,0:T(8,128)(2,1)S(1)}, u32[]{:S(2)}, u32[]{:S(2)}) collective-permute-start(bf16[16,48,512]{2,1,0:T(8,128)(2,1)S(1)} %get-tuple-element.78), channel_id=1, source_target_pairs={{0,8},{1,9},{2,10},{3,11},{4,12},{5,13},{6,14},{7,15},{8,0},{9,1},... | collective-permute-start | bytes 2359304 | tf_op jit(solution)/shard_map/ppermute | solution.py:585
  67.2 28.4 %collective-permute-start.18 = (bf16[16,88,512]{2,1,0:T(8,128)(2,1)S(1)}, bf16[16,88,512]{2,1,0:T(8,128)(2,1)S(1)}, u32[]{:S(2)}, u32[]{:S(2)}) collective-permute-start(bf16[16,88,512]{2,1,0:T(8,128)(2,1)S(1)} %get-tuple-element.86), channel_id=1, source_target_pairs={{0,8},{1,9},{2,10},{3,11},{4,12},{5,13},{6,14},{7,15},{8,0},{9,1},... | collective-permute-start | bytes 4325384 | tf_op jit(solution)/shard_map/ppermute | solution.py:585
  68.1 12.3 %collective-permute-start.5 = (bf16[4,48,512]{2,1,0:T(8,128)(2,1)S(1)}, bf16[4,48,512]{2,1,0:T(8,128)(2,1)S(1)}, u32[]{:S(2)}, u32[]{:S(2)}) collective-permute-start(bf16[4,48,512]{2,1,0:T(8,128)(2,1)S(1)} %get-tuple-element.99), channel_id=1, source_target_pairs={{0,1},{1,0},{2,3},{3,2},{4,5},{5,4},{6,7},{7,6},{8,9},{9,8},{10,11... | collective-permute-start | bytes 589832 | tf_op jit(solution)/shard_map/ppermute | solution.py:585
  71.0 9.3 %collective-permute-start.7 = (bf16[4,48,512]{2,1,0:T(8,128)(2,1)S(1)}, bf16[4,48,512]{2,1,0:T(8,128)(2,1)S(1)}, u32[]{:S(2)}, u32[]{:S(2)}) collective-permute-start(bf16[4,48,512]{2,1,0:T(8,128)(2,1)S(1)} %get-tuple-element.100), channel_id=1, source_target_pairs={{0,17},{1,16},{2,19},{3,18},{4,21},{5,20},{6,23},{7,22},{8,25},{9,... | collective-permute-start | bytes 589832 | tf_op jit(solution)/shard_map/ppermute | solution.py:585
  72.0 9.6 %collective-permute-start.6 = (bf16[4,48,512]{2,1,0:T(8,128)(2,1)S(1)}, bf16[4,48,512]{2,1,0:T(8,128)(2,1)S(1)}, u32[]{:S(2)}, u32[]{:S(2)}) collective-permute-start(bf16[4,48,512]{2,1,0:T(8,128)(2,1)S(1)} %get-tuple-element.101), channel_id=1, source_target_pairs={{0,16},{1,17},{2,18},{3,19},{4,20},{5,21},{6,22},{7,23},{8,24},{9,... | collective-permute-start | bytes 589832 | tf_op jit(solution)/shard_map/ppermute | solution.py:585
  81.8 4.2 %collective-permute-start.8 = (bf16[48,512]{1,0:T(8,128)(2,1)S(1)}, bf16[48,512]{1,0:T(8,128)(2,1)S(1)}, u32[]{:S(2)}, u32[]{:S(2)}) collective-permute-start(bf16[48,512]{1,0:T(8,128)(2,1)S(1)} %get-tuple-element.105), channel_id=1, source_target_pairs={{0,2},{1,3},{2,0},{3,1},{4,6},{5,7},{6,4},{7,5},{8,10},{9,11},{10,... | collective-permute-start | bytes 147464 | tf_op jit(solution)/shard_map/ppermute | solution.py:585
  83.4 5.9 %collective-permute-start.10 = (bf16[48,512]{1,0:T(8,128)(2,1)S(1)}, bf16[48,512]{1,0:T(8,128)(2,1)S(1)}, u32[]{:S(2)}, u32[]{:S(2)}) collective-permute-start(bf16[48,512]{1,0:T(8,128)(2,1)S(1)} %get-tuple-element.106), channel_id=1, source_target_pairs={{0,6},{1,7},{2,4},{3,5},{4,2},{5,3},{6,0},{7,1},{8,14},{9,15},{10,... | collective-permute-start | bytes 147464 | tf_op jit(solution)/shard_map/ppermute | solution.py:585
  85.9 5.3 %collective-permute-start.9 = (bf16[48,512]{1,0:T(8,128)(2,1)S(1)}, bf16[48,512]{1,0:T(8,128)(2,1)S(1)}, u32[]{:S(2)}, u32[]{:S(2)}) collective-permute-start(bf16[48,512]{1,0:T(8,128)(2,1)S(1)} %get-tuple-element.107), channel_id=1, source_target_pairs={{0,4},{1,5},{2,6},{3,7},{4,0},{5,1},{6,2},{7,3},{8,12},{9,13},{10,... | collective-permute-start | bytes 147464 | tf_op jit(solution)/shard_map/ppermute | solution.py:585
  91.2 7.9 %collective-permute-start.13 = (bf16[48,512]{1,0:T(8,128)(2,1)S(1)}, bf16[48,512]{1,0:T(8,128)(2,1)S(1)}, u32[]{:S(2)}, u32[]{:S(2)}) collective-permute-start(bf16[48,512]{1,0:T(8,128)(2,1)S(1)} %get-tuple-element.93), channel_id=1, source_target_pairs={{0,6},{1,7},{2,4},{3,5},{4,2},{5,3},{6,0},{7,1},{8,14},{9,15},{10,... | collective-permute-start | bytes 147464 | tf_op jit(solution)/shard_map/ppermute | solution.py:585
  93.0 6.7 %collective-permute-start.12 = (bf16[48,512]{1,0:T(8,128)(2,1)S(1)}, bf16[48,512]{1,0:T(8,128)(2,1)S(1)}, u32[]{:S(2)}, u32[]{:S(2)}) collective-permute-start(bf16[48,512]{1,0:T(8,128)(2,1)S(1)} %get-tuple-element.93), channel_id=1, source_target_pairs={{0,4},{1,5},{2,6},{3,7},{4,0},{5,1},{6,2},{7,3},{8,12},{9,13},{10,... | collective-permute-start | bytes 147464 | tf_op jit(solution)/shard_map/ppermute | solution.py:585
  93.0 6.7 %collective-permute-start.11 = (bf16[48,512]{1,0:T(8,128)(2,1)S(1)}, bf16[48,512]{1,0:T(8,128)(2,1)S(1)}, u32[]{:S(2)}, u32[]{:S(2)}) collective-permute-start(bf16[48,512]{1,0:T(8,128)(2,1)S(1)} %get-tuple-element.93), channel_id=1, source_target_pairs={{0,2},{1,3},{2,0},{3,1},{4,6},{5,7},{6,4},{7,5},{8,10},{9,11},{10,... | collective-permute-start | bytes 147464 | tf_op jit(solution)/shard_map/ppermute | solution.py:585
  96.1 17.2 %collective-permute-start.19 = (bf16[4,88,512]{2,1,0:T(8,128)(2,1)S(1)}, bf16[4,88,512]{2,1,0:T(8,128)(2,1)S(1)}, u32[]{:S(2)}, u32[]{:S(2)}) collective-permute-start(bf16[4,88,512]{2,1,0:T(8,128)(2,1)S(1)} %get-tuple-element.96), channel_id=1, source_target_pairs={{0,1},{1,0},{2,3},{3,2},{4,5},{5,4},{6,7},{7,6},{8,9},{9,8},{10,11... | collective-permute-start | bytes 1081352 | tf_op jit(solution)/shard_map/ppermute | solution.py:585
  98.0 15.4 %collective-permute-start.21 = (bf16[4,88,512]{2,1,0:T(8,128)(2,1)S(1)}, bf16[4,88,512]{2,1,0:T(8,128)(2,1)S(1)}, u32[]{:S(2)}, u32[]{:S(2)}) collective-permute-start(bf16[4,88,512]{2,1,0:T(8,128)(2,1)S(1)} %get-tuple-element.97), channel_id=1, source_target_pairs={{0,17},{1,16},{2,19},{3,18},{4,21},{5,20},{6,23},{7,22},{8,25},{9,... | collective-permute-start | bytes 1081352 | tf_op jit(solution)/shard_map/ppermute | solution.py:585
  99.1 17.6 %collective-permute-start.20 = (bf16[4,88,512]{2,1,0:T(8,128)(2,1)S(1)}, bf16[4,88,512]{2,1,0:T(8,128)(2,1)S(1)}, u32[]{:S(2)}, u32[]{:S(2)}) collective-permute-start(bf16[4,88,512]{2,1,0:T(8,128)(2,1)S(1)} %get-tuple-element.98), channel_id=1, source_target_pairs={{0,16},{1,17},{2,18},{3,19},{4,20},{5,21},{6,22},{7,23},{8,24},{9,... | collective-permute-start | bytes 1081352 | tf_op jit(solution)/shard_map/ppermute | solution.py:585
  99.7 57.5 %collective-permute-start.16 = (bf16[4,48,512]{2,1,0:T(8,128)(2,1)S(1)}, bf16[4,48,512]{2,1,0:T(8,128)(2,1)S(1)}, u32[]{:S(2)}, u32[]{:S(2)}) collective-permute-start(bf16[4,48,512]{2,1,0:T(8,128)(2,1)S(1)} %pad_maximum_fusion.1), channel_id=1, source_target_pairs={{0,17},{1,16},{2,19},{3,18},{4,21},{5,20},{6,23},{7,22},{8,25},{9,... | collective-permute-start | bytes 589832 | tf_op jit(solution)/shard_map/ppermute | solution.py:585
  102.5 54.7 %collective-permute-start.15 = (bf16[4,48,512]{2,1,0:T(8,128)(2,1)S(1)}, bf16[4,48,512]{2,1,0:T(8,128)(2,1)S(1)}, u32[]{:S(2)}, u32[]{:S(2)}) collective-permute-start(bf16[4,48,512]{2,1,0:T(8,128)(2,1)S(1)} %pad_maximum_fusion.1), channel_id=1, source_target_pairs={{0,16},{1,17},{2,18},{3,19},{4,20},{5,21},{6,22},{7,23},{8,24},{9,... | collective-permute-start | bytes 589832 | tf_op jit(solution)/shard_map/ppermute | solution.py:585
  116.9 4.6 %collective-permute-start.22 = (bf16[88,512]{1,0:T(8,128)(2,1)S(1)}, bf16[88,512]{1,0:T(8,128)(2,1)S(1)}, u32[]{:S(2)}, u32[]{:S(2)}) collective-permute-start(bf16[88,512]{1,0:T(8,128)(2,1)S(1)} %get-tuple-element.102), channel_id=1, source_target_pairs={{0,2},{1,3},{2,0},{3,1},{4,6},{5,7},{6,4},{7,5},{8,10},{9,11},{10,... | collective-permute-start | bytes 270344 | tf_op jit(solution)/shard_map/ppermute | solution.py:585
  117.0 6.5 %collective-permute-start.24 = (bf16[88,512]{1,0:T(8,128)(2,1)S(1)}, bf16[88,512]{1,0:T(8,128)(2,1)S(1)}, u32[]{:S(2)}, u32[]{:S(2)}) collective-permute-start(bf16[88,512]{1,0:T(8,128)(2,1)S(1)} %get-tuple-element.103), channel_id=1, source_target_pairs={{0,6},{1,7},{2,4},{3,5},{4,2},{5,3},{6,0},{7,1},{8,14},{9,15},{10,... | collective-permute-start | bytes 270344 | tf_op jit(solution)/shard_map/ppermute | solution.py:585
  118.9 9.8 %collective-permute-start.23 = (bf16[88,512]{1,0:T(8,128)(2,1)S(1)}, bf16[88,512]{1,0:T(8,128)(2,1)S(1)}, u32[]{:S(2)}, u32[]{:S(2)}) collective-permute-start(bf16[88,512]{1,0:T(8,128)(2,1)S(1)} %get-tuple-element.104), channel_id=1, source_target_pairs={{0,4},{1,5},{2,6},{3,7},{4,0},{5,1},{6,2},{7,3},{8,12},{9,13},{10,... | collective-permute-start | bytes 270344 | tf_op jit(solution)/shard_map/ppermute | solution.py:585
  128.8 6.4 %collective-permute-start.27 = (bf16[88,512]{1,0:T(8,128)(2,1)S(1)}, bf16[88,512]{1,0:T(8,128)(2,1)S(1)}, u32[]{:S(2)}, u32[]{:S(2)}) collective-permute-start(bf16[88,512]{1,0:T(8,128)(2,1)S(1)} %get-tuple-element.91), channel_id=1, source_target_pairs={{0,6},{1,7},{2,4},{3,5},{4,2},{5,3},{6,0},{7,1},{8,14},{9,15},{10,... | collective-permute-start | bytes 270344 | tf_op jit(solution)/shard_map/ppermute | solution.py:585
  130.7 6.4 %collective-permute-start.26 = (bf16[88,512]{1,0:T(8,128)(2,1)S(1)}, bf16[88,512]{1,0:T(8,128)(2,1)S(1)}, u32[]{:S(2)}, u32[]{:S(2)}) collective-permute-start(bf16[88,512]{1,0:T(8,128)(2,1)S(1)} %get-tuple-element.91), channel_id=1, source_target_pairs={{0,4},{1,5},{2,6},{3,7},{4,0},{5,1},{6,2},{7,3},{8,12},{9,13},{10,... | collective-permute-start | bytes 270344 | tf_op jit(solution)/shard_map/ppermute | solution.py:585
  130.7 6.4 %collective-permute-start.25 = (bf16[88,512]{1,0:T(8,128)(2,1)S(1)}, bf16[88,512]{1,0:T(8,128)(2,1)S(1)}, u32[]{:S(2)}, u32[]{:S(2)}) collective-permute-start(bf16[88,512]{1,0:T(8,128)(2,1)S(1)} %get-tuple-element.91), channel_id=1, source_target_pairs={{0,2},{1,3},{2,0},{3,1},{4,6},{5,7},{6,4},{7,5},{8,10},{9,11},{10,... | collective-permute-start | bytes 270344 | tf_op jit(solution)/shard_map/ppermute | solution.py:585
  137.2 16.2 %collective-permute-start.30 = (bf16[4,88,512]{2,1,0:T(8,128)(2,1)S(1)}, bf16[4,88,512]{2,1,0:T(8,128)(2,1)S(1)}, u32[]{:S(2)}, u32[]{:S(2)}) collective-permute-start(bf16[4,88,512]{2,1,0:T(8,128)(2,1)S(1)} %pad_maximum_fusion), channel_id=1, source_target_pairs={{0,17},{1,16},{2,19},{3,18},{4,21},{5,20},{6,23},{7,22},{8,25},{9,... | collective-permute-start | bytes 1081352 | tf_op jit(solution)/shard_map/ppermute | solution.py:585
  139.9 13.4 %collective-permute-start.29 = (bf16[4,88,512]{2,1,0:T(8,128)(2,1)S(1)}, bf16[4,88,512]{2,1,0:T(8,128)(2,1)S(1)}, u32[]{:S(2)}, u32[]{:S(2)}) collective-permute-start(bf16[4,88,512]{2,1,0:T(8,128)(2,1)S(1)} %pad_maximum_fusion), channel_id=1, source_target_pairs={{0,16},{1,17},{2,18},{3,19},{4,20},{5,21},{6,22},{7,23},{8,24},{9,... | collective-permute-start | bytes 1081352 | tf_op jit(solution)/shard_map/ppermute | solution.py:585
  140.5 11.0 %collective-permute-start.28 = (bf16[4,88,512]{2,1,0:T(8,128)(2,1)S(1)}, bf16[4,88,512]{2,1,0:T(8,128)(2,1)S(1)}, u32[]{:S(2)}, u32[]{:S(2)}) collective-permute-start(bf16[4,88,512]{2,1,0:T(8,128)(2,1)S(1)} %pad_maximum_fusion), channel_id=1, source_target_pairs={{0,1},{1,0},{2,3},{3,2},{4,5},{5,4},{6,7},{7,6},{8,9},{9,8},{10,11... | collective-permute-start | bytes 1081352 | tf_op jit(solution)/shard_map/ppermute | solution.py:585
  140.7 16.6 %copy-start.17 = (bf16[6,128,512]{2,1,0:T(8,128)(2,1)S(1)}, bf16[6,128,512]{2,1,0:T(8,128)(2,1)}, u32[]{:S(2)}) copy-start(bf16[6,128,512]{2,1,0:T(8,128)(2,1)} %copy-done.16) | copy-start | bytes 2359300
  140.8 16.6 %copy-start.19 = (bf16[6,128,512]{2,1,0:T(8,128)(2,1)S(1)}, bf16[6,128,512]{2,1,0:T(8,128)(2,1)}, u32[]{:S(2)}) copy-start(bf16[6,128,512]{2,1,0:T(8,128)(2,1)} %copy-done.18) | copy-start | bytes 2359300
  151.5 5.7 %collective-permute-start.14 = (bf16[4,48,512]{2,1,0:T(8,128)(2,1)S(1)}, bf16[4,48,512]{2,1,0:T(8,128)(2,1)S(1)}, u32[]{:S(2)}, u32[]{:S(2)}) collective-permute-start(bf16[4,48,512]{2,1,0:T(8,128)(2,1)S(1)} %pad_maximum_fusion.1), channel_id=1, source_target_pairs={{0,1},{1,0},{2,3},{3,2},{4,5},{5,4},{6,7},{7,6},{8,9},{9,8},{10,11... | collective-permute-start | bytes 589832 | tf_op jit(solution)/shard_map/ppermute | solution.py:585
  153.4 35.0 %collective-permute-start.31 = (bf16[16,88,512]{2,1,0:T(8,128)(2,1)S(1)}, bf16[16,88,512]{2,1,0:T(8,128)(2,1)S(1)}, u32[]{:S(2)}, u32[]{:S(2)}) collective-permute-start(bf16[16,88,512]{2,1,0:T(8,128)(2,1)S(1)} %constant_dynamic-update-slice_fusion.7.own_ref), channel_id=1, source_target_pairs={{0,8},{1,9},{2,10},{3,11},{4,12},{5,13},{6,14},{7,15},{8,0},{9,1},... | collective-permute-start | bytes 4325384 | tf_op jit(solution)/shard_map/ppermute | solution.py:585
  157.3 26.2 %collective-permute-start.17 = (bf16[16,48,512]{2,1,0:T(8,128)(2,1)S(1)}, bf16[16,48,512]{2,1,0:T(8,128)(2,1)S(1)}, u32[]{:S(2)}, u32[]{:S(2)}) collective-permute-start(bf16[16,48,512]{2,1,0:T(8,128)(2,1)S(1)} %constant_dynamic-update-slice_fusion.own_ref), channel_id=1, source_target_pairs={{0,8},{1,9},{2,10},{3,11},{4,12},{5,13},{6,14},{7,15},{8,0},{9,1},... | collective-permute-start | bytes 2359304 | tf_op jit(solution)/shard_map/ppermute | solution.py:585
  158.4 21.1 %collective-permute-start.2 = (bf16[6,64,512]{2,1,0:T(8,128)(2,1)S(1)}, bf16[6,64,512]{2,1,0:T(8,128)(2,1)S(1)}, u32[]{:S(2)}, u32[]{:S(2)}) collective-permute-start(bf16[6,64,512]{2,1,0:T(8,128)(2,1)S(1)} %get-tuple-element.71), channel_id=1, source_target_pairs={{0,1},{1,2},{2,3},{3,4},{4,5},{5,6},{6,7},{8,9},{9,10},{10,11},{11... | collective-permute-start | bytes 1179656 | tf_op jit(solution)/shard_map/ppermute | solution.py:803
  162.1 17.4 %collective-permute-start.3 = (bf16[6,64,512]{2,1,0:T(8,128)(2,1)S(1)}, bf16[6,64,512]{2,1,0:T(8,128)(2,1)S(1)}, u32[]{:S(2)}, u32[]{:S(2)}) collective-permute-start(bf16[6,64,512]{2,1,0:T(8,128)(2,1)S(1)} %get-tuple-element.72), channel_id=1, source_target_pairs={{1,0},{2,1},{3,2},{4,3},{5,4},{6,5},{7,6},{9,8},{10,9},{11,10},{12... | collective-permute-start | bytes 1179656 | tf_op jit(solution)/shard_map/ppermute | solution.py:802
  (22 other events, 74.4 us)

commit v3 on v2

--- a/solution.py
+++ b/solution.py
@@ -97,6 +97,29 @@
 def turn_back(values, cosine, sines):
     first, second = values[:, :LANES], values[:, LANES:]
     return jnp.concatenate([first * cosine + second * sines, second * cosine - first * sines], axis=1)
+
+
+def load_kernel(count, *refs):
+    sources, outs, sems = refs[:count], refs[count:-1], refs[-1]
+    own_len, win = sources[0].shape[1], HALF_WIN
+    odd = lax.axis_index("seq") % 2
+    copies = []
+    for k, out in enumerate(outs):
+        source = sources[0] if k >= count else sources[k]
+        if k >= count:
+            high = odd == 0 if k == count else odd == 1
+            at = pl.multiple_of(jnp.where(high, own_len - win, 0), win)
+            source = source.at[:, pl.ds(at, win)]
+        copies.append(pltpu.make_async_copy(source, out, sems.at[k]))
+    for copy in copies:
+        copy.start()
+    for copy in copies:
+        copy.wait()
+
+
+def by_side(inner, other):
+    odd = lax.axis_index("seq") % 2 == 1
+    return jnp.where(odd, inner, other), jnp.where(odd, other, inner)
 
 
 def project_kernel(
@@ -161,8 +184,8 @@
         values_ref[at] = nn(normed, weight_ref[:, 2 * width :]).astype(BF16).reshape(pair, own_len, width)
 
 
-def halo_kernel(low_ref, high_ref, weight_ref, gain_ref, angles_ref, normed_ref, keys_ref, values_ref):
-    rows, win, width = low_ref.shape
+def halo_kernel(inner_ref, other_ref, weight_ref, gain_ref, angles_ref, normed_ref, keys_ref, values_ref):
+    rows, win, width = inner_ref.shape
     pair = 3
     span = angles_ref.shape[1]
     cosine = jnp.concatenate([angles_ref[0, :win], angles_ref[0, span - win :]] * pair)
@@ -171,7 +194,8 @@
     @pl.loop(0, rows // pair)
     def _(i):
         at = pl.ds(i * pair, pair)
-        unit, _ = normalize(flat(jnp.concatenate([low_ref[at], high_ref[at]], axis=1)).astype(F32))
+        sides = by_side(inner_ref[at], other_ref[at])
+        unit, _ = normalize(flat(jnp.concatenate(sides, axis=1)).astype(F32))
         normed = (unit * gain_ref[...]).astype(BF16)
         normed_ref[at] = normed.reshape(pair, 2 * win, width)
         for c in range(0, width, WIDE):
@@ -450,7 +474,7 @@
 
 
 def weight_in_kernel(normed_ref, halo_normed_ref, *refs):
-    *grads, keep_ref, send_ref, total = refs
+    *grads, total = refs
     width = normed_ref.shape[2]
     normed, halo_normed = flat(normed_ref[...]), flat(halo_normed_ref[...])
     normed_all = jnp.concatenate([normed, halo_normed], axis=0)
@@ -467,7 +491,12 @@
             if k < 2:
                 part = nt(part, order).astype(BF16)
             total[:, k * width + g * WIDE : k * width + (g + 1) * WIDE] = part
-    rows = width // BLOCKS
+
+
+def split_kernel(weight_ref, *refs):
+    *halos, total, inner_ref, other_ref, keep_ref, send_ref = refs
+    grad_halo_kernel(weight_ref, *halos, inner_ref, other_ref)
+    rows, width = total.shape[0] // BLOCKS, total.shape[0]
 
     def store(ref, i, block):
         own = pl.ds(pl.multiple_of(block * rows, rows), rows)
@@ -478,8 +507,8 @@
 
 
 def grad_halo_kernel(weight_ref, *refs):
-    *grads, low_ref, high_ref = refs
-    rows, win, width = low_ref.shape
+    *grads, inner_ref, other_ref = refs
+    rows, win, width = inner_ref.shape
     total = None
     for g, ref in enumerate(grads):
         weight = jnp.concatenate(
@@ -488,8 +517,14 @@
         part = nt(flat(ref[...]), weight)
         total = part if total is None else total + part
     total = total.astype(BF16).reshape(rows, 2 * win, width)
-    low_ref[...] = total[:, :win]
-    high_ref[...] = total[:, win:]
+    inner_ref[...], other_ref[...] = by_side(total[:, :win], total[:, win:])
+
+
+def backward_kernel(*refs):
+    shared, (normed_ref, halo_normed_ref), (*grads, total) = refs[:10], refs[10:12], refs[12:]
+    for group in range(len(grads) // 2):
+        attend_back_kernel(group, *shared, *grads[2 * group : 2 * group + 2])
+    weight_in_kernel(normed_ref, halo_normed_ref, *grads, total)
 
 
 def grad_own_kernel(weight_ref, *refs):
@@ -532,7 +567,7 @@
 
 
 def finish_kernel(
-    tokens_ref, own_ref, from_low_ref, from_high_ref, mid_grad_ref, out_grad_ref, gain_ref, grad_ref
+    tokens_ref, own_ref, inner_ref, other_ref, mid_grad_ref, out_grad_ref, gain_ref, grad_ref
 ):
     own_len, win = tokens_ref.shape[1], HALF_WIN
 
@@ -540,12 +575,9 @@
     def _(row):
         unit, inverse = normalize(tokens_ref[row].astype(F32))
         own = own_ref[row]
+        low, high = by_side(inner_ref[row].astype(F32), other_ref[row].astype(F32))
         grads = jnp.concatenate(
-            [
-                own[:win] + from_low_ref[row].astype(F32),
-                own[win : own_len - win],
-                own[own_len - win :] + from_high_ref[row].astype(F32),
-            ],
+            [own[:win] + low, own[win : own_len - win], own[own_len - win :] + high],
             axis=0,
         )
         outer = out_grad_ref[row]
@@ -553,7 +585,9 @@
         grad_ref[row] = middle + norm_back(grads * gain_ref[...], unit, inverse)
 
 
-def place_kernel(own_ref, other_ref, *out_refs):
+def place_kernel(own_ref, other_ref, weight_ref, gain_ref, *out_refs):
+    *out_refs, gain_grad_ref = out_refs
+
     def store(ref, i, block):
         at = 0
         for out in out_refs:
@@ -565,10 +599,40 @@
                 at += rows
 
     store_blocks(own_ref, other_ref, store)
-
-
-def shift_route(size, distance):
-    return [(i, i + distance) for i in range(size) if 0 <= i + distance < size]
+    total = None
+    for c in range(0, weight_ref.shape[1], LANES):
+        part = out_refs[0][:, c : c + LANES] * weight_ref[:, c : c + LANES].astype(F32)
+        total = part if total is None else total + part
+    gain_grad_ref[...] = jnp.sum(total.T, axis=0, keepdims=True) / gain_ref[...]
+
+
+def add_kernel(count, *refs):
+    parts, outs = refs[:count], refs[count:]
+    if len(outs) == 1:
+        outs[0][...] = sum(p[...].astype(F32) for p in parts).astype(BF16)
+        return
+    size = parts[0].shape[0] // len(outs)
+    for k, out in enumerate(outs):
+        at = slice(k * size, (k + 1) * size) if len(out.shape) == len(parts[0].shape) else k
+        out[...] = sum(p[at].astype(F32) for p in parts).astype(BF16)
+
+
+def join_kernel(*refs):
+    *parts, out = refs
+    if len(out.shape) > len(parts[0].shape):
+        for k, part in enumerate(parts):
+            out[k] = part[...]
+    else:
+        size = parts[0].shape[0]
+        for k, part in enumerate(parts):
+            out[k * size : (k + 1) * size] = part[...]
+
+
+def to_neighbours(inner, other):
+    size = lax.axis_size("seq")
+    pairs = [(i, i ^ 1) for i in range(size)]
+    between = [p for i in range(1, size - 1, 2) for p in ((i, i + 1), (i + 1, i))]
+    return lax.ppermute(inner, "seq", pairs), lax.ppermute(other, "seq", between)
 
 
 def swap_route(core, x, y, z, rest):
@@ -585,41 +649,53 @@
     return lax.ppermute(values, ("dp", "seq"), swap_route(core, x, y, z, rest))
 
 
-def add_all(*parts):
-    return sum(p.astype(F32) for p in parts).astype(BF16)
-
-
-def total_over_devices(keep, send):
-    own = add_all(keep, swap(send, core=1))
-    own = own.reshape((4, 4) + own.shape[1:])
-    own = add_all(own[0], *[swap(own[k], x=k >> 1, y=k & 1) for k in (1, 2, 3)])
-    own = add_all(own[0], *[swap(own[k], z=k) for k in (1, 2, 3)])
-    rest = 1
-    while 8 * rest < lax.axis_size("seq"):
-        own = add_all(own, swap(own, rest=rest))
-        rest *= 2
-    own = jnp.stack([own] + [swap(own, z=k) for k in (1, 2, 3)])
-    own = jnp.concatenate([own] + [swap(own, x=k >> 1, y=k & 1) for k in (1, 2, 3)])
-    return own, swap(own, core=1)
-
-
 def shape(*dims, kind=BF16):
     return jax.ShapeDtypeStruct(dims, kind)
 
 
-def call(name, kernel, outs, *args, grant=16, flops=1e9, scratch=()):
+def call(name, kernel, outs, *args, after=(), grant=6, flops=1e9, scratch=()):
     spec = pl.BlockSpec(memory_space=pltpu.VMEM)
     moved = sum(int(np.prod(a.shape)) * a.dtype.itemsize for a in (*args, *outs))
+
+    def body(*refs):
+        return kernel(*refs[len(after) :])
+
     return pl.pallas_call(
-        kernel,
+        body,
         out_shape=outs,
-        in_specs=[spec] * len(args),
+        in_specs=[pl.BlockSpec(memory_space=pl.ANY)] * len(after) + [spec] * len(args),
         out_specs=[spec] * len(outs),
         scratch_shapes=scratch,
         compiler_params=pltpu.CompilerParams(vmem_limit_bytes=grant * MB),
         cost_estimate=pl.CostEstimate(flops=int(flops), bytes_accessed=moved, transcendentals=0),
         name=name,
-    )(*args)
+    )(*after, *args)
+
+
+def add_up(parts, outs, after=()):
+    return call("add", functools.partial(add_kernel, len(parts)), outs, *parts, after=after, grant=4, flops=1e6)
+
+
+def join(parts, stacked, after=()):
+    size = parts[0].shape
+    out = shape(len(parts), *size) if stacked else shape(len(parts) * size[0], *size[1:])
+    return call("join", join_kernel, [out], *parts, after=after, grant=4, flops=1e6)[0]
+
+
+def swap_plane(parts):
+    return [swap(parts[k], x=k >> 1, y=k & 1) for k in (1, 2, 3)]
+
+
+def swap_line(parts):
+    return [swap(parts[k], z=k) for k in (1, 2, 3)]
+
+
+def swap_rest(own):
+    rest = 1
+    while 8 * rest < lax.axis_size("seq"):
+        (own,) = add_up([own, swap(own, rest=rest)], [shape(*own.shape)])
+        rest *= 2
+    return own
 
 
 def angle_tables(own_len, pieces):
@@ -649,9 +725,18 @@
     groups = width // WIDE
     gain_one, gain_two = gain_first[None], gain_second[None]
 
-    up_route, down_route = shift_route(seq, 1), shift_route(seq, -1)
-    low_tokens = lax.ppermute(tokens[:, own_len - win :], "seq", up_route)
-    high_tokens = lax.ppermute(tokens[:, :win], "seq", down_route)
+    loaded = [tokens, document_starts, attention_in, gain_one, *angle_tables(own_len, seq)]
+    outs = [pltpu.VMEM(a.shape, a.dtype) for a in loaded] + [pltpu.VMEM((rows, win, width), BF16)] * 2
+    tokens, document_starts, attention_in, gain_one, *tables, inner_tokens, other_tokens = pl.pallas_call(
+        functools.partial(load_kernel, len(loaded)),
+        out_shape=outs,
+        in_specs=[pl.BlockSpec(memory_space=pltpu.HBM)] * len(loaded),
+        out_specs=[pl.BlockSpec(memory_space=pltpu.VMEM)] * len(outs),
+        scratch_shapes=[pltpu.SemaphoreType.DMA((len(outs),))],
+        compiler_params=pltpu.CompilerParams(vmem_limit_bytes=MB),
+        name="load",
+    )(*[pltpu.with_memory_space_constraint(a, pltpu.HBM) for a in loaded])
+    inner_halo, other_halo = to_neighbours(inner_tokens, other_tokens)
 
     row_shape = shape(rows, own_len, width)
     normed, queries, keys, values, weight, angles, bounds = call(
@@ -667,7 +752,7 @@
         document_starts,
         attention_in,
         gain_one,
-        *angle_tables(own_len, seq),
+        *tables,
         flops=3e9,
     )
     mid_attended, mid_probs = call(
@@ -713,8 +798,8 @@
         "halo",
         halo_kernel,
         [shape(rows, 2 * win, width)] * 3,
-        low_tokens,
-        high_tokens,
+        inner_halo,
+        other_halo,
         weight,
         gain_one,
         angles,
@@ -760,73 +845,106 @@
         ],
     )
 
-    own_grads, halo_grads = [], []
-    for g in range(groups):
-        own_part, halo_part = call(
-            "attend_back_%d" % g,
-            functools.partial(attend_back_kernel, g),
-            [shape(rows, own_len, 3 * WIDE), shape(rows, 2 * win, 2 * WIDE)],
-            queries,
-            keys,
-            values,
-            halo_keys,
-            halo_values,
-            mid_grad_attended,
-            out_grad_attended,
-            mid_probs,
-            out_probs,
-            angles,
-            flops=4e9,
-        )
-        own_grads.append(own_part)
-        halo_grads.append(halo_part)
-    keep_two, send_two = call(
-        "weight_in",
-        weight_in_kernel,
-        [shape(BLOCKS // 2, attention_in.shape[1] // BLOCKS, width)] * 2,
+    def cut(blocks, parts, stacked=False):
+        if stacked:
+            return [shape(*blocks.shape[1:])] * parts
+        return [shape(blocks.shape[0] // parts, *blocks.shape[1:])] * parts
+
+    (activations,) = call(
+        "result",
+        result_kernel,
+        [row_shape],
+        mid_middle,
+        out_middle,
+        mid_mixed,
+        out_mixed,
+        feedforward_out,
+        flops=2e9,
+        after=[keep_one],
+    )
+    chip_one = add_up([keep_one, swap(send_one, core=1)], cut(keep_one, 4), after=[activations])
+    from_plane = swap_plane(chip_one)
+    grad_shapes = [shape(rows, own_len, 3 * WIDE), shape(rows, 2 * win, 2 * WIDE)] * groups
+    *grads, total_in = call(
+        "backward",
+        backward_kernel,
+        [shape(rows, own_len, 3 * WIDE), shape(rows, 2 * win, 2 * WIDE)] * groups + [shape(*attention_in.shape)],
+        queries,
+        keys,
+        values,
+        halo_keys,
+        halo_values,
+        mid_grad_attended,
+        out_grad_attended,
+        mid_probs,
+        out_probs,
+        angles,
         normed,
         halo_normed,
-        *[a for pair in zip(own_grads, halo_grads) for a in pair],
-        flops=4e9,
-        scratch=[pltpu.VMEM(attention_in.shape, BF16)],
-    )
-    to_low, to_high = call(
-        "grad_halo", grad_halo_kernel, [shape(rows, win, width)] * 2, weight, *halo_grads, flops=1e9
-    )
+        flops=16e9,
+        after=[chip_one[0]],
+    )
+    plane_one = add_up([chip_one[0], *from_plane], cut(chip_one[0], 4, True), after=[total_in])
+    from_line = swap_line(plane_one)
+    inner_grad, other_grad, keep_two, send_two = call(
+        "split",
+        split_kernel,
+        [shape(rows, win, width)] * 2 + [shape(BLOCKS // 2, attention_in.shape[1] // BLOCKS, width)] * 2,
+        weight,
+        *grads[1::2],
+        total_in,
+        flops=1e9,
+        after=[plane_one[0]],
+    )
+    from_core_two = swap(send_two, core=1)
+    inner_grad, other_grad = to_neighbours(inner_grad, other_grad)
     (own_grad,) = call(
-        "grad_own", grad_own_kernel, [shape(rows, own_len, width, kind=F32)], weight, *own_grads, flops=2e9
-    )
-
-    total_one = total_over_devices(keep_one, send_one)
-    total_two = total_over_devices(keep_two, send_two)
-    from_high = lax.ppermute(to_low, "seq", down_route)
-    from_low = lax.ppermute(to_high, "seq", up_route)
-
-    (activations,) = call(
-        "result", result_kernel, [row_shape], mid_middle, out_middle, mid_mixed, out_mixed, feedforward_out, flops=2e9
-    )
+        "grad_own",
+        grad_own_kernel,
+        [shape(rows, own_len, width, kind=F32)],
+        weight,
+        *grads[::2],
+        flops=2e9,
+        after=[keep_two],
+    )
+    chip_two = add_up([keep_two, from_core_two], cut(keep_two, 4), after=[own_grad])
+    from_plane = swap_plane(chip_two)
+    (line_one,) = add_up([plane_one[0], *from_line], cut(plane_one[0], 1), after=[chip_two[0]])
+    line_one = swap_rest(line_one)
+    plane_two = add_up([chip_two[0], *from_plane], cut(chip_two[0], 4, True))
+    line_one = join([line_one, *swap_line([line_one] * 4)], True, after=[plane_two[0], inner_grad, other_grad])
+    from_line = swap_line(plane_two)
+    from_plane = swap_plane([line_one] * 4)
     (grad_tokens,) = call(
         "finish",
         finish_kernel,
         [shape(rows, own_len, width, kind=F32)],
         tokens,
         own_grad,
-        from_low,
-        from_high,
+        inner_grad,
+        other_grad,
         mid_grad,
         out_grad,
         gain_one,
         flops=1e8,
-    )
-
-    def placed(parts, *weights):
-        return call("place", place_kernel, [shape(*w.shape, kind=F32) for w in weights], *parts, flops=1e6)
-
-    grad_up, grad_out, grad_down = placed(total_one, feedforward_in, attention_out, feedforward_out)
-    (grad_in,) = placed(total_two, attention_in)
-    grad_gain_one = jnp.sum(grad_in * attention_in.astype(F32), axis=1) / gain_first
-    grad_gain_two = jnp.sum(grad_up * feedforward_in.astype(F32), axis=1) / gain_second
-    return activations, grad_tokens, grad_in, grad_out, grad_up, grad_down, grad_gain_one, grad_gain_two
+        after=[line_one],
+    )
+    (line_two,) = add_up([plane_two[0], *from_line], cut(plane_two[0], 1))
+    line_two = swap_rest(line_two)
+    line_two = join([line_two, *swap_line([line_two] * 4)], True)
+    from_plane_two = swap_plane([line_two] * 4)
+    whole_one = join([line_one, *from_plane], False, after=[line_two, grad_tokens])
+
+    def placed(parts, gain, *weights):
+        outs = [shape(*w.shape, kind=F32) for w in weights] + [shape(1, width, kind=F32)]
+        return call("place", place_kernel, outs, *parts, weights[0], gain, flops=1e6)
+
+    grad_up, grad_out, grad_down, grad_gain_two = placed(
+        (whole_one, swap(whole_one, core=1)), gain_two, feedforward_in, attention_out, feedforward_out
+    )
+    whole_two = join([line_two, *from_plane_two], False, after=[grad_gain_two])
+    grad_in, grad_gain_one = placed((whole_two, swap(whole_two, core=1)), gain_one, attention_in)
+    return activations, grad_tokens, grad_in, grad_out, grad_up, grad_down, grad_gain_one[0], grad_gain_two[0]
 
 
 def solution(mesh):

time: 195 us -> 156 us (0.80)
  waiting for transfers between devices: 64.8 us -> 39.6 us
  other arithmetic: 6.94 us -> 0 us
  starting transfers between devices: 45.9 us -> 40.8 us
  local copies, waits for them, and re-layouts: 7.93 us -> 4.01 us
  Pallas kernels: 67.3 us -> 70.4 us
    ppermute x28, waiting for transfers between devices: 54.6 us -> 38.5 us  [swap(): return lax.ppermute(values, ('dp', 'seq'), swap_route(core, x, y, z, rest))]
    ppermute x4, waiting for transfers between devices: 10.2 us -> 1.1 us  [the longest x2 1.09 us: to_neighbours(): lax.ppermute(inner, 'seq', pairs)]
    ppermute x4, starting transfers between devices: 11.9 us -> 6.33 us  [the longest x2 4.98 us: to_neighbours(): lax.ppermute(inner, 'seq', pairs)]
    reduce_sum x2 -> x0, other arithmetic: 4.69 us -> none  [the longest x1 2.35 us: shards(): jnp.sum(grad_up * feedforward_in.astype(F32), axis=1) / gain_second]
    pallas_call x16 -> x25, Pallas kernels: 67.3 us -> 70.4 us  [the longest x24 68.1 us: call(): pl.pallas_call(body, out_shape=outs, in_specs=[pl.BlockSpec(memory_space=...]
    unnamed x86 -> x16, local copies, waits for them, and re-layouts: 6.44 us -> 4.01 us
  transfers between devices with their start and end apart: 32 -> 32, of which waited for: 14 -> 12; matrix products, arithmetic and copies ran while one was open for 2% -> 0% of each run, Pallas kernels for 17% -> 30%
where the time goes in v3:
time: 156 us
  Pallas kernels  70.4 us (45%)
  starting transfers between devices  40.8 us (26%)
  waiting for transfers between devices  39.6 us (25%)
  local copies, waits for them, and re-layouts  4.01 us (3%)
    pallas_call x24, Pallas kernels, call(): pl.pallas_call(body, out_shape=outs, in_specs=[pl.BlockSpec(memory_space=...  68.1 us
    ppermute x28, waiting for transfers between devices, swap(): return lax.ppermute(values, ('dp', 'seq'), swap_route(core, x, y, z, rest))  38.5 us
    ppermute x28, starting transfers between devices, swap(): return lax.ppermute(values, ('dp', 'seq'), swap_route(core, x, y, z, rest))  34.5 us
    ppermute x2, starting transfers between devices, to_neighbours(): lax.ppermute(inner, 'seq', pairs)  4.98 us
    unnamed x16, local copies, waits for them, and re-layouts  4.01 us
  transfers between devices with their start and end apart: 32, of which 12 were waited for; matrix products, arithmetic and copies ran while one was open for 0% of the time, Pallas kernels for 30%

profile of v3, /device:TPU:0, one launch (start us, length us, event | category | flops | bytes accessed | tf_op | source)
XLA Modules:
  0.0 155.8 jit_solution(3022815007902714090)
XLA Ops:
  0.6 2.3 %load.1 = (bf16[6,256,512]{2,1,0:T(8,128)(2,1)S(1)}, s32[6,16]{1,0:T(8,128)S(1)}, bf16[512,1536]{1,0:T(8,128)(2,1)S(1)}, f32[1,512]{1,0:T(1,128)S(1)}, f32[8,2,1...) custom-call(bf16[6,256,512]{2,1,0:T(8,128)(2,1)} %refs_0_.2, ...), custom_call_target="tpu_custom_call" | custom-call | tf_op jit(solution)/shard_map/load/pallas_call | solution.py:730
  2.9 3.0 %collective-permute-start = (bf16[6,64,512]{2,1,0:T(8,128)(2,1)S(1)}, bf16[6,64,512]{2,1,0:T(8,128)(2,1)S(1)}, u32[]{:S(2)}, u32[]{:S(2)}) collective-permute-start(bf16[6,64,512]{2,1,0:T(8,128)(2,1)S(1)} %get-tuple-element.89), channel_id=1, source_target_pairs={{0,1},{1,0},{2,3},{3,2},{4,5},{5,4},{6,7},{7,6},{8,9},{9,8},{10,11... | collective-permute-start | bytes 1179656 | tf_op jit(solution)/shard_map/ppermute | solution.py:635
  6.0 0.7 collective-permute-start.1
  6.7 4.4 %project.1 = (bf16[6,256,512]{2,1,0:T(8,128)(2,1)S(1)}, bf16[6,256,512]{2,1,0:T(8,128)(2,1)S(1)}, bf16[6,256,512]{2,1,0:T(8,128)(2,1)S(1)}, bf16[6,256,512]{2,1,...) custom-call(bf16[6,256,512]{2,1,0:T(8,128)(2,1)S(1)} %get-tuple-element.77., ...), custom_call_target="tpu_custom_call" | custom-call | flops 3000000000 | bytes 11825536 | tf_op jit(solution)/shard_map/project/pallas_call | solution.py:663
  11.1 3.9 %attend_mid.1 = (bf16[6,128,512]{2,1,0:T(8,128)(2,1)S(1)}, f32[6,2,256,512]{3,2,1,0:T(8,128)S(1)}) custom-call(bf16[6,256,512]{2,1,0:T(8,128)(2,1)S(1)} %get-tuple-element.83.refs_0_.refs_1_, bf16[6,256,512]{2,1,0:T(8,128)(2,1)S(1)} %get-tuple-element.84.refs_1_.refs_2_, bf16[6,256,512]{2,1,0:T(8,128)(2,1)S(1)} %get-tuple-element.85.refs_2_.refs_3_, ...), custom_call_target="tpu_custom_call" | custom-call | flops 2000000000 | bytes 11814912 | tf_op jit(solution)/shard_map/attend_mid/pallas_call | solution.py:663
  15.1 6.6 %dense_mid.1 = (f32[6,128,512]{2,1,0:T(8,128)S(1)}, bf16[6,128,512]{2,1,0:T(8,128)(2,1)S(1)}, bf16[6,128,768]{2,1,0:T(8,128)(2,1)S(1)}, bf16[6,128,1536]{2,1,0:T...) custom-call(bf16[6,256,512]{2,1,0:T(8,128)(2,1)S(1)} %get-tuple-elem, ...), custom_call_target="tpu_custom_call" | custom-call | flops 5000000000 | bytes 15861760 | tf_op jit(solution)/shard_map/dense_mid/pallas_call | solution.py:663
  21.7 1.1 collective-permute-done.refs_0_
  22.8 1.7 %halo.1 = (bf16[6,128,512]{2,1,0:T(8,128)(2,1)S(1)}, bf16[6,128,512]{2,1,0:T(8,128)(2,1)S(1)}, bf16[6,128,512]{2,1,0:T(8,128)(2,1)S(1)}) custom-call(bf16[6,64,512]{2,1,0:T(8,128)(2,1)S(1)} %collective-permute-done.refs_0_, bf16[6,64,512]{2,1,0:T(8,128)(2,1)S(1)} %collective-permute-done.1.refs_1_, bf16[512,1536]{1,0:T(8,128)(2,1)S(1)} %get-tuple-element.91.refs_2_.refs_1_, ...), custom_call_target="tpu_custom_call" | custom-call | flops 1000000000 | bytes 5113856 | tf_op jit(solution)/shard_map/halo/pallas_call | solution.py:663
  24.4 4.1 %attend_out.1 = (bf16[6,128,512]{2,1,0:T(8,128)(2,1)S(1)}, f32[6,2,2,192,256]{4,3,2,1,0:T(8,128)S(1)}) custom-call(bf16[6,256,512]{2,1,0:T(8,128)(2,1)S(1)} %get-tuple-element.83.refs_0_.refs_1_, bf16[6,256,512]{2,1,0:T(8,128)(2,1)S(1)} %get-tuple-element.84.refs_1_.refs_2_, bf16[6,256,512]{2,1,0:T(8,128)(2,1)S(1)} %get-tuple-element.85.refs_2_.refs_3_, ...), custom_call_target="tpu_custom_call" | custom-call | flops 2000000000 | bytes 11814912 | tf_op jit(solution)/shard_map/attend_out/pallas_call | solution.py:663
  28.6 6.7 %dense_out.1 = (f32[6,128,512]{2,1,0:T(8,128)S(1)}, bf16[6,128,512]{2,1,0:T(8,128)(2,1)S(1)}, bf16[6,128,768]{2,1,0:T(8,128)(2,1)S(1)}, bf16[6,128,1536]{2,1,0:T...) custom-call(bf16[6,256,512]{2,1,0:T(8,128)(2,1)S(1)} %get-tuple-elem, ...), custom_call_target="tpu_custom_call" | custom-call | flops 5000000000 | bytes 15861760 | tf_op jit(solution)/shard_map/dense_out/pallas_call | solution.py:663
  35.3 5.0 %weights.1 = (bf16[16,88,512]{2,1,0:T(8,128)(2,1)S(1)}, bf16[16,88,512]{2,1,0:T(8,128)(2,1)S(1)}) custom-call(bf16[6,256,512]{2,1,0:T(8,128)(2,1)S(1)} %copy-done.6, bf16[6,128,512]{2,1,0:T(8,128)(2,1)S(1)} %get-tuple-element.88.refs_1_, bf16[6,128,512]{2,1,0:T(8,128)(2,1)S(1)} %get-tuple-element.96.refs_2_, ...), custom_call_target="tpu_custom_call" | custom-call | flops 5000000000 | bytes 16252928 | tf_op jit(solution)/shard_map/weights/pallas_call | solution.py:663
  40.4 2.7 %result.1.refs_0_ = bf16[6,256,512]{2,1,0:T(8,128)(2,1)} custom-call(bf16[16,88,512]{2,1,0:T(8,128)(2,1)S(1)} %get-tuple-element.103.refs_0_.refs_1_, f32[6,128,512]{2,1,0:T(8,128)S(1)} %get-tuple-element.104.refs_1_, f32[6,128,512]{2,1,0:T(8,128)S(1)} %get-tuple-element.105.refs_2_, bf16[6,128,768]{2,1,0:T(8,128)(2,1)S(1)} %get-tuple-element.99.refs_5_.refs_3_, ...), custom_call_target="tpu_custom_call" | custom-call | flops 2000000000 | bytes 7864320 | tf_op jit(solution)/shard_map/result/pallas_call | solution.py:663
  43.6 1.4 copy-done.1
  45.4 3.3 %collective-permute-start.3 = (bf16[4,88,512]{2,1,0:T(8,128)(2,1)S(1)}, bf16[4,88,512]{2,1,0:T(8,128)(2,1)S(1)}, u32[]{:S(2)}, u32[]{:S(2)}) collective-permute-start(bf16[4,88,512]{2,1,0:T(8,128)(2,1)S(1)} %get-tuple-element.115), channel_id=1, source_target_pairs={{0,1},{1,0},{2,3},{3,2},{4,5},{5,4},{6,7},{7,6},{8,9},{9,8},{10,11... | collective-permute-start | bytes 1081352 | tf_op jit(solution)/shard_map/ppermute | solution.py:649
  48.7 1.5 collective-permute-start.4
  50.2 18.7 %backward.1 = (bf16[6,256,768]{2,1,0:T(8,128)(2,1)S(1)}, bf16[6,128,512]{2,1,0:T(8,128)(2,1)S(1)}, bf16[6,256,768]{2,1,0:T(8,128)(2,1)S(1)}, bf16[6,128,512]{2,1,0:T(8,128)(2,1)S(1)}, bf16[512,1536]{1,0:T(8,128)(2,1)S(1)}) custom-call(bf16[4,88,512]{2,1,0:T(8,128)(2,1)S(1)} %get-tuple-element.107.refs_0_.refs_1_, ...), custom_call_target="tpu_custom_call" | custom-call | flops 16000000000 | bytes 29491200 | tf_op jit(solution)/shard_map/backward/pallas_call | solution.py:663
  69.2 1.2 split.1
  70.5 1.6 %collective-permute-start.12 = (bf16[88,512]{1,0:T(8,128)(2,1)S(1)}, bf16[88,512]{1,0:T(8,128)(2,1)S(1)}, u32[]{:S(2)}, u32[]{:S(2)}) collective-permute-start(bf16[88,512]{1,0:T(8,128)(2,1)S(1)} %get-tuple-element.132), channel_id=1, source_target_pairs={{0,2},{1,3},{2,0},{3,1},{4,6},{5,7},{6,4},{7,5},{8,10},{9,11},{10,... | collective-permute-start | bytes 270344 | tf_op jit(solution)/shard_map/ppermute | solution.py:649
  72.1 2.3 %collective-permute-start.13 = (bf16[88,512]{1,0:T(8,128)(2,1)S(1)}, bf16[88,512]{1,0:T(8,128)(2,1)S(1)}, u32[]{:S(2)}, u32[]{:S(2)}) collective-permute-start(bf16[88,512]{1,0:T(8,128)(2,1)S(1)} %get-tuple-element.133), channel_id=1, source_target_pairs={{0,4},{1,5},{2,6},{3,7},{4,0},{5,1},{6,2},{7,3},{8,12},{9,13},{10,... | collective-permute-start | bytes 270344 | tf_op jit(solution)/shard_map/ppermute | solution.py:649
  74.9 1.9 %collective-permute-start.10 = (bf16[6,64,512]{2,1,0:T(8,128)(2,1)S(1)}, bf16[6,64,512]{2,1,0:T(8,128)(2,1)S(1)}, u32[]{:S(2)}, u32[]{:S(2)}) collective-permute-start(bf16[6,64,512]{2,1,0:T(8,128)(2,1)S(1)} %get-tuple-element.130), channel_id=1, source_target_pairs={{0,1},{1,0},{2,3},{3,2},{4,5},{5,4},{6,7},{7,6},{8,9},{9,8},{10,11... | collective-permute-start | bytes 1179656 | tf_op jit(solution)/shard_map/ppermute | solution.py:635
  76.9 0.7 collective-permute-start.11
  77.6 3.0 %grad_own.1.refs_0_.refs_2_ = f32[6,256,512]{2,1,0:T(8,128)S(1)} custom-call(bf16[16,48,512]{2,1,0:T(8,128)(2,1)S(1)} %get-tuple-element.121.refs_0_.refs_1_, bf16[512,1536]{1,0:T(8,128)(2,1)S(1)} %get-tuple-element.91.refs_2_.refs_1_, bf16[6,256,768]{2,1,0:T(8,128)(2,1)S(1)} %get-tuple-element.122.refs_2_, bf16[6,256,768]{2,1,0:T(8,128)(2,1)S(1)} %get-tuple-element.123.refs_3_), custom_call_target="tpu_custom_call" | custom-call | flops 2000000000 | bytes 9437184 | tf_op jit(solution)/shard_map/grad_own/pallas_call | solution.py:663
  80.8 3.4 %collective-permute-start.7 = (bf16[4,48,512]{2,1,0:T(8,128)(2,1)S(1)}, bf16[4,48,512]{2,1,0:T(8,128)(2,1)S(1)}, u32[]{:S(2)}, u32[]{:S(2)}) collective-permute-start(bf16[4,48,512]{2,1,0:T(8,128)(2,1)S(1)} %get-tuple-element.126), channel_id=1, source_target_pairs={{0,1},{1,0},{2,3},{3,2},{4,5},{5,4},{6,7},{7,6},{8,9},{9,8},{10,11... | collective-permute-start | bytes 589832 | tf_op jit(solution)/shard_map/ppermute | solution.py:649
  84.2 1.5 collective-permute-start.8
  85.8 16.1 %collective-permute-done.7.refs_1_ = bf16[4,48,512]{2,1,0:T(8,128)(2,1)S(1)} collective-permute-done((bf16[4,48,512]{2,1,0:T(8,128)(2,1)S(1)}, bf16[4,48,512]{2,1,0:T(8,128)(2,1)S(1)}, u32[]{:S(2)}, u32[]{:S(2)}) %collective-permute-start.7) | collective-permute-done | bytes 196640 | tf_op jit(solution)/shard_map/ppermute | solution.py:649
  101.9 3.8 %collective-permute-start.17 = (bf16[88,512]{1,0:T(8,128)(2,1)S(1)}, bf16[88,512]{1,0:T(8,128)(2,1)S(1)}, u32[]{:S(2)}, u32[]{:S(2)}) collective-permute-start(bf16[88,512]{1,0:T(8,128)(2,1)S(1)} %add.10.refs_3_), channel_id=1, source_target_pairs={{0,6},{1,7},{2,4},{3,5},{4,2},{5,3},{6,0},{7,1},{8,14},{9,15},{10,... | collective-permute-start | bytes 270344 | tf_op jit(solution)/shard_map/ppermute | solution.py:649
  105.7 0.6 collective-permute-start.15
  106.4 2.1 %collective-permute-done.17.refs_6_ = bf16[88,512]{1,0:T(8,128)(2,1)S(1)} collective-permute-done((bf16[88,512]{1,0:T(8,128)(2,1)S(1)}, bf16[88,512]{1,0:T(8,128)(2,1)S(1)}, u32[]{:S(2)}, u32[]{:S(2)}) %collective-permute-start.17) | collective-permute-done | bytes 90144 | tf_op jit(solution)/shard_map/ppermute | solution.py:649
  108.6 3.5 %collective-permute-done.16.refs_5_ = bf16[88,512]{1,0:T(8,128)(2,1)S(1)} collective-permute-done((bf16[88,512]{1,0:T(8,128)(2,1)S(1)}, bf16[88,512]{1,0:T(8,128)(2,1)S(1)}, u32[]{:S(2)}, u32[]{:S(2)}) %collective-permute-start.16) | collective-permute-done | bytes 90144 | tf_op jit(solution)/shard_map/ppermute | solution.py:649
  112.1 2.8 %collective-permute-start.26 = (bf16[4,88,512]{2,1,0:T(8,128)(2,1)S(1)}, bf16[4,88,512]{2,1,0:T(8,128)(2,1)S(1)}, u32[]{:S(2)}, u32[]{:S(2)}) collective-permute-start(bf16[4,88,512]{2,1,0:T(8,128)(2,1)S(1)} %join.4.refs_0_.refs_2_), channel_id=1, source_target_pairs={{0,17},{1,16},{2,19},{3,18},{4,21},{5,20},{6,23},{7,22},{8,25},{9,... | collective-permute-start | bytes 1081352 | tf_op jit(solution)/shard_map/ppermute | solution.py:649
  115.0 0.6 collective-permute-start.25
  115.7 0.8 collective-permute-start.18
  116.4 2.4 %collective-permute-start.19 = (bf16[48,512]{1,0:T(8,128)(2,1)S(1)}, bf16[48,512]{1,0:T(8,128)(2,1)S(1)}, u32[]{:S(2)}, u32[]{:S(2)}) collective-permute-start(bf16[48,512]{1,0:T(8,128)(2,1)S(1)} %get-tuple-element.138), channel_id=1, source_target_pairs={{0,4},{1,5},{2,6},{3,7},{4,0},{5,1},{6,2},{7,3},{8,12},{9,13},{10,... | collective-permute-start | bytes 147464 | tf_op jit(solution)/shard_map/ppermute | solution.py:649
  118.8 0.9 collective-permute-done.18.refs_1_
  119.8 2.6 %collective-permute-start.20 = (bf16[48,512]{1,0:T(8,128)(2,1)S(1)}, bf16[48,512]{1,0:T(8,128)(2,1)S(1)}, u32[]{:S(2)}, u32[]{:S(2)}) collective-permute-start(bf16[48,512]{1,0:T(8,128)(2,1)S(1)} %get-tuple-element.139), channel_id=1, source_target_pairs={{0,6},{1,7},{2,4},{3,5},{4,2},{5,3},{6,0},{7,1},{8,14},{9,15},{10,... | collective-permute-start | bytes 147464 | tf_op jit(solution)/shard_map/ppermute | solution.py:649
  122.4 3.3 %collective-permute-done.20.refs_3_ = bf16[48,512]{1,0:T(8,128)(2,1)S(1)} collective-permute-done((bf16[48,512]{1,0:T(8,128)(2,1)S(1)}, bf16[48,512]{1,0:T(8,128)(2,1)S(1)}, u32[]{:S(2)}, u32[]{:S(2)}) %collective-permute-start.20) | collective-permute-done | bytes 49184 | tf_op jit(solution)/shard_map/ppermute | solution.py:649
  125.7 2.7 %collective-permute-start.23 = (bf16[48,512]{1,0:T(8,128)(2,1)S(1)}, bf16[48,512]{1,0:T(8,128)(2,1)S(1)}, u32[]{:S(2)}, u32[]{:S(2)}) collective-permute-start(bf16[48,512]{1,0:T(8,128)(2,1)S(1)} %add.11.refs_0_), channel_id=1, source_target_pairs={{0,6},{1,7},{2,4},{3,5},{4,2},{5,3},{6,0},{7,1},{8,14},{9,15},{10,... | collective-permute-start | bytes 147464 | tf_op jit(solution)/shard_map/ppermute | solution.py:649
  128.4 3.6 %collective-permute-done.23.refs_3_ = bf16[48,512]{1,0:T(8,128)(2,1)S(1)} collective-permute-done((bf16[48,512]{1,0:T(8,128)(2,1)S(1)}, bf16[48,512]{1,0:T(8,128)(2,1)S(1)}, u32[]{:S(2)}, u32[]{:S(2)}) %collective-permute-start.23) | collective-permute-done | bytes 49184 | tf_op jit(solution)/shard_map/ppermute | solution.py:649
  131.9 3.9 %finish.1.refs_1_ = f32[6,256,512]{2,1,0:T(8,128)} custom-call(bf16[4,88,512]{2,1,0:T(8,128)(2,1)S(1)} %join.4.refs_0_.refs_2_, bf16[6,256,512]{2,1,0:T(8,128)(2,1)S(1)} %get-tuple-element.77.refs_0_.refs_1_, f32[6,256,512]{2,1,0:T(8,128)S(1)} %grad_own.1.refs_0_.refs_2_, bf16[6,64,512]{2,1,0:T(8,128)(2,1)S(1)} %collective-permute-done.10.refs_1_.refs_3_, ...), custom_call_target="tpu_custom_call" | custom-call | flops 100000000 | bytes 11798528 | tf_op jit(solution)/shard_map/finish/pallas_call | solution.py:663
  136.1 1.9 %copy-done = f32[6,256,512]{2,1,0:T(8,128)S(1)} copy-done((f32[6,256,512]{2,1,0:T(8,128)S(1)}, f32[6,256,512]{2,1,0:T(8,128)}, u32[]{:S(2)}) %copy-start) | copy-done | bytes 3145752
  138.1 2.6 %collective-permute-start.30 = (bf16[4,48,512]{2,1,0:T(8,128)(2,1)S(1)}, bf16[4,48,512]{2,1,0:T(8,128)(2,1)S(1)}, u32[]{:S(2)}, u32[]{:S(2)}) collective-permute-start(bf16[4,48,512]{2,1,0:T(8,128)(2,1)S(1)} %join.5.refs_0_.refs_1_), channel_id=1, source_target_pairs={{0,17},{1,16},{2,19},{3,18},{4,21},{5,20},{6,23},{7,22},{8,25},{9,... | collective-permute-start | bytes 589832 | tf_op jit(solution)/shard_map/ppermute | solution.py:649
  140.7 0.6 collective-permute-start.29
  141.7 3.0 %place.2 = (f32[512,1536]{1,0:T(8,128)}, f32[512,512]{1,0:T(8,128)}, f32[768,512]{1,0:T(8,128)}, f32[1,512]{1,0:T(1,128)}) custom-call(bf16[16,88,512]{2,1,0:T(8,128)(2,1)S(1)} %join.6.refs_0_, bf16[16,88,512]{2,1,0:T(8,128)(2,1)S(1)} %collective-permute-done.27.refs_1_, bf16[512,1536]{1,0:T(8,128)(2,1)S(1)} %copy-done.2, f32[1,512]{1,0:T(1,128)S(1)} %bitcast.6), custom_call_target="tpu_custom_call" | custom-call | flops 1000000 | bytes 10227712 | tf_op jit(solution)/shard_map/place/pallas_call | solution.py:663
  144.7 2.1 %collective-permute-done.30.refs_4_ = bf16[4,48,512]{2,1,0:T(8,128)(2,1)S(1)} collective-permute-done((bf16[4,48,512]{2,1,0:T(8,128)(2,1)S(1)}, bf16[4,48,512]{2,1,0:T(8,128)(2,1)S(1)}, u32[]{:S(2)}, u32[]{:S(2)}) %collective-permute-start.30) | collective-permute-done | bytes 196640 | tf_op jit(solution)/shard_map/ppermute | solution.py:649
  146.8 3.9 %collective-permute-done.29.refs_3_ = bf16[4,48,512]{2,1,0:T(8,128)(2,1)S(1)} collective-permute-done((bf16[4,48,512]{2,1,0:T(8,128)(2,1)S(1)}, bf16[4,48,512]{2,1,0:T(8,128)(2,1)S(1)}, u32[]{:S(2)}, u32[]{:S(2)}) %collective-permute-start.29) | collective-permute-done | bytes 196640 | tf_op jit(solution)/shard_map/ppermute | solution.py:649
  150.7 0.7 copy-done.5
  151.5 2.3 %collective-permute-done.31.refs_1_ = bf16[16,48,512]{2,1,0:T(8,128)(2,1)S(1)} collective-permute-done((bf16[16,48,512]{2,1,0:T(8,128)(2,1)S(1)}, bf16[16,48,512]{2,1,0:T(8,128)(2,1)S(1)}, u32[]{:S(2)}, u32[]{:S(2)}) %collective-permute-start.31) | collective-permute-done | bytes 786464 | tf_op jit(solution)/shard_map/ppermute | solution.py:649
  153.8 2.0 %place.3 = (f32[512,1536]{1,0:T(8,128)}, f32[1,512]{1,0:T(1,128)}) custom-call(bf16[16,48,512]{2,1,0:T(8,128)(2,1)S(1)} %join.7.refs_0_, bf16[16,48,512]{2,1,0:T(8,128)(2,1)S(1)} %collective-permute-done.31.refs_1_, bf16[512,1536]{1,0:T(8,128)(2,1)S(1)} %get-tuple-element.79.refs_2_, f32[1,512]{1,0:T(1,128)S(1)} %get-tuple-element.80.refs_3_.refs_7_), custom_call_target="tpu_custom_call" | custom-call | flops 1000000 | bytes 6295552 | tf_op jit(solution)/shard_map/place/pallas_call | solution.py:663
  (57 shorter events, 3.4 us)
Async XLA Ops:
  2.9 19.8 %collective-permute-start = (bf16[6,64,512]{2,1,0:T(8,128)(2,1)S(1)}, bf16[6,64,512]{2,1,0:T(8,128)(2,1)S(1)}, u32[]{:S(2)}, u32[]{:S(2)}) collective-permute-start(bf16[6,64,512]{2,1,0:T(8,128)(2,1)S(1)} %get-tuple-element.89), channel_id=1, source_target_pairs={{0,1},{1,0},{2,3},{3,2},{4,5},{5,4},{6,7},{7,6},{8,9},{9,8},{10,11... | collective-permute-start | bytes 1179656 | tf_op jit(solution)/shard_map/ppermute | solution.py:635
  6.0 16.8 %collective-permute-start.1 = (bf16[6,64,512]{2,1,0:T(8,128)(2,1)S(1)}, bf16[6,64,512]{2,1,0:T(8,128)(2,1)S(1)}, u32[]{:S(2)}, u32[]{:S(2)}) collective-permute-start(bf16[6,64,512]{2,1,0:T(8,128)(2,1)S(1)} %get-tuple-element.90), channel_id=1, source_target_pairs={{1,2},{2,1},{3,4},{4,3},{5,6},{6,5},{9,10},{10,9},{11,12},{12,11},... | collective-permute-start | bytes 1179656 | tf_op jit(solution)/shard_map/ppermute | solution.py:635
  11.1 4.0 %copy-start.2 = (bf16[512,1536]{1,0:T(8,128)(2,1)S(1)}, bf16[512,1536]{1,0:T(8,128)(2,1)}, u32[]{:S(2)}) copy-start(bf16[512,1536]{1,0:T(8,128)(2,1)} %refs_2_.3) | copy-start | bytes 4718596
  11.1 4.0 %copy-start.3 = (bf16[768,512]{1,0:T(8,128)(2,1)S(1)}, bf16[768,512]{1,0:T(8,128)(2,1)}, u32[]{:S(2)}) copy-start(bf16[768,512]{1,0:T(8,128)(2,1)} %refs_5_.6) | copy-start | bytes 2359300
  11.1 4.0 %copy-start.4 = (f32[512]{0:T(512)S(1)}, f32[512]{0:T(512)}, u32[]{:S(2)}) copy-start(f32[512]{0:T(512)} %param.18) | copy-start | bytes 6148
  11.1 4.0 %copy-start.6 = (bf16[6,256,512]{2,1,0:T(8,128)(2,1)S(1)}, bf16[6,256,512]{2,1,0:T(8,128)(2,1)}, u32[]{:S(2)}) copy-start(bf16[6,256,512]{2,1,0:T(8,128)(2,1)} %refs_0_.3) | copy-start | bytes 4718596
  11.1 4.0 %copy-start.7 = (bf16[512,512]{1,0:T(8,128)(2,1)S(1)}, bf16[512,512]{1,0:T(8,128)(2,1)}, u32[]{:S(2)}) copy-start(bf16[512,512]{1,0:T(8,128)(2,1)} %refs_3_.3) | copy-start | bytes 1572868
  40.4 3.3 %collective-permute-start.2 = (bf16[16,88,512]{2,1,0:T(8,128)(2,1)S(1)}, bf16[16,88,512]{2,1,0:T(8,128)(2,1)S(1)}, u32[]{:S(2)}, u32[]{:S(2)}) collective-permute-start(bf16[16,88,512]{2,1,0:T(8,128)(2,1)S(1)} %get-tuple-element.106), channel_id=1, source_target_pairs={{0,8},{1,9},{2,10},{3,11},{4,12},{5,13},{6,14},{7,15},{8,0},{9,1},... | collective-permute-start | bytes 4325384 | tf_op jit(solution)/shard_map/ppermute | solution.py:649
  43.6 1.4 copy-start.1
  45.4 23.6 %collective-permute-start.3 = (bf16[4,88,512]{2,1,0:T(8,128)(2,1)S(1)}, bf16[4,88,512]{2,1,0:T(8,128)(2,1)S(1)}, u32[]{:S(2)}, u32[]{:S(2)}) collective-permute-start(bf16[4,88,512]{2,1,0:T(8,128)(2,1)S(1)} %get-tuple-element.115), channel_id=1, source_target_pairs={{0,1},{1,0},{2,3},{3,2},{4,5},{5,4},{6,7},{7,6},{8,9},{9,8},{10,11... | collective-permute-start | bytes 1081352 | tf_op jit(solution)/shard_map/ppermute | solution.py:649
  48.7 20.3 %collective-permute-start.4 = (bf16[4,88,512]{2,1,0:T(8,128)(2,1)S(1)}, bf16[4,88,512]{2,1,0:T(8,128)(2,1)S(1)}, u32[]{:S(2)}, u32[]{:S(2)}) collective-permute-start(bf16[4,88,512]{2,1,0:T(8,128)(2,1)S(1)} %get-tuple-element.116), channel_id=1, source_target_pairs={{0,16},{1,17},{2,18},{3,19},{4,20},{5,21},{6,22},{7,23},{8,24},{9,... | collective-permute-start | bytes 1081352 | tf_op jit(solution)/shard_map/ppermute | solution.py:649
  50.1 18.8 %collective-permute-start.5 = (bf16[4,88,512]{2,1,0:T(8,128)(2,1)S(1)}, bf16[4,88,512]{2,1,0:T(8,128)(2,1)S(1)}, u32[]{:S(2)}, u32[]{:S(2)}) collective-permute-start(bf16[4,88,512]{2,1,0:T(8,128)(2,1)S(1)} %get-tuple-element.117), channel_id=1, source_target_pairs={{0,17},{1,16},{2,19},{3,18},{4,21},{5,20},{6,23},{7,22},{8,25},{9,... | collective-permute-start | bytes 1081352 | tf_op jit(solution)/shard_map/ppermute | solution.py:649
  70.4 6.5 %collective-permute-start.6 = (bf16[16,48,512]{2,1,0:T(8,128)(2,1)S(1)}, bf16[16,48,512]{2,1,0:T(8,128)(2,1)S(1)}, u32[]{:S(2)}, u32[]{:S(2)}) collective-permute-start(bf16[16,48,512]{2,1,0:T(8,128)(2,1)S(1)} %get-tuple-element.124), channel_id=1, source_target_pairs={{0,8},{1,9},{2,10},{3,11},{4,12},{5,13},{6,14},{7,15},{8,0},{9,1},... | collective-permute-start | bytes 2359304 | tf_op jit(solution)/shard_map/ppermute | solution.py:649
  70.5 10.3 %collective-permute-start.12 = (bf16[88,512]{1,0:T(8,128)(2,1)S(1)}, bf16[88,512]{1,0:T(8,128)(2,1)S(1)}, u32[]{:S(2)}, u32[]{:S(2)}) collective-permute-start(bf16[88,512]{1,0:T(8,128)(2,1)S(1)} %get-tuple-element.132), channel_id=1, source_target_pairs={{0,2},{1,3},{2,0},{3,1},{4,6},{5,7},{6,4},{7,5},{8,10},{9,11},{10,... | collective-permute-start | bytes 270344 | tf_op jit(solution)/shard_map/ppermute | solution.py:649
  72.1 12.1 %collective-permute-start.13 = (bf16[88,512]{1,0:T(8,128)(2,1)S(1)}, bf16[88,512]{1,0:T(8,128)(2,1)S(1)}, u32[]{:S(2)}, u32[]{:S(2)}) collective-permute-start(bf16[88,512]{1,0:T(8,128)(2,1)S(1)} %get-tuple-element.133), channel_id=1, source_target_pairs={{0,4},{1,5},{2,6},{3,7},{4,0},{5,1},{6,2},{7,3},{8,12},{9,13},{10,... | collective-permute-start | bytes 270344 | tf_op jit(solution)/shard_map/ppermute | solution.py:649
  74.4 11.3 %collective-permute-start.14 = (bf16[88,512]{1,0:T(8,128)(2,1)S(1)}, bf16[88,512]{1,0:T(8,128)(2,1)S(1)}, u32[]{:S(2)}, u32[]{:S(2)}) collective-permute-start(bf16[88,512]{1,0:T(8,128)(2,1)S(1)} %get-tuple-element.134), channel_id=1, source_target_pairs={{0,6},{1,7},{2,4},{3,5},{4,2},{5,3},{6,0},{7,1},{8,14},{9,15},{10,... | collective-permute-start | bytes 270344 | tf_op jit(solution)/shard_map/ppermute | solution.py:649
  74.9 31.5 %collective-permute-start.10 = (bf16[6,64,512]{2,1,0:T(8,128)(2,1)S(1)}, bf16[6,64,512]{2,1,0:T(8,128)(2,1)S(1)}, u32[]{:S(2)}, u32[]{:S(2)}) collective-permute-start(bf16[6,64,512]{2,1,0:T(8,128)(2,1)S(1)} %get-tuple-element.130), channel_id=1, source_target_pairs={{0,1},{1,0},{2,3},{3,2},{4,5},{5,4},{6,7},{7,6},{8,9},{9,8},{10,11... | collective-permute-start | bytes 1179656 | tf_op jit(solution)/shard_map/ppermute | solution.py:635
  76.9 29.5 %collective-permute-start.11 = (bf16[6,64,512]{2,1,0:T(8,128)(2,1)S(1)}, bf16[6,64,512]{2,1,0:T(8,128)(2,1)S(1)}, u32[]{:S(2)}, u32[]{:S(2)}) collective-permute-start(bf16[6,64,512]{2,1,0:T(8,128)(2,1)S(1)} %get-tuple-element.131), channel_id=1, source_target_pairs={{1,2},{2,1},{3,4},{4,3},{5,6},{6,5},{9,10},{10,9},{11,12},{12,11},... | collective-permute-start | bytes 1179656 | tf_op jit(solution)/shard_map/ppermute | solution.py:635
  80.8 21.1 %collective-permute-start.7 = (bf16[4,48,512]{2,1,0:T(8,128)(2,1)S(1)}, bf16[4,48,512]{2,1,0:T(8,128)(2,1)S(1)}, u32[]{:S(2)}, u32[]{:S(2)}) collective-permute-start(bf16[4,48,512]{2,1,0:T(8,128)(2,1)S(1)} %get-tuple-element.126), channel_id=1, source_target_pairs={{0,1},{1,0},{2,3},{3,2},{4,5},{5,4},{6,7},{7,6},{8,9},{9,8},{10,11... | collective-permute-start | bytes 589832 | tf_op jit(solution)/shard_map/ppermute | solution.py:649
  84.2 21.5 %collective-permute-start.8 = (bf16[4,48,512]{2,1,0:T(8,128)(2,1)S(1)}, bf16[4,48,512]{2,1,0:T(8,128)(2,1)S(1)}, u32[]{:S(2)}, u32[]{:S(2)}) collective-permute-start(bf16[4,48,512]{2,1,0:T(8,128)(2,1)S(1)} %get-tuple-element.127), channel_id=1, source_target_pairs={{0,16},{1,17},{2,18},{3,19},{4,20},{5,21},{6,22},{7,23},{8,24},{9,... | collective-permute-start | bytes 589832 | tf_op jit(solution)/shard_map/ppermute | solution.py:649
  85.7 20.0 %collective-permute-start.9 = (bf16[4,48,512]{2,1,0:T(8,128)(2,1)S(1)}, bf16[4,48,512]{2,1,0:T(8,128)(2,1)S(1)}, u32[]{:S(2)}, u32[]{:S(2)}) collective-permute-start(bf16[4,48,512]{2,1,0:T(8,128)(2,1)S(1)} %get-tuple-element.128), channel_id=1, source_target_pairs={{0,17},{1,16},{2,19},{3,18},{4,21},{5,20},{6,23},{7,22},{8,25},{9,... | collective-permute-start | bytes 589832 | tf_op jit(solution)/shard_map/ppermute | solution.py:649
  101.9 6.7 %collective-permute-start.17 = (bf16[88,512]{1,0:T(8,128)(2,1)S(1)}, bf16[88,512]{1,0:T(8,128)(2,1)S(1)}, u32[]{:S(2)}, u32[]{:S(2)}) collective-permute-start(bf16[88,512]{1,0:T(8,128)(2,1)S(1)} %add.10.refs_3_), channel_id=1, source_target_pairs={{0,6},{1,7},{2,4},{3,5},{4,2},{5,3},{6,0},{7,1},{8,14},{9,15},{10,... | collective-permute-start | bytes 270344 | tf_op jit(solution)/shard_map/ppermute | solution.py:649
  105.7 6.4 %collective-permute-start.16 = (bf16[88,512]{1,0:T(8,128)(2,1)S(1)}, bf16[88,512]{1,0:T(8,128)(2,1)S(1)}, u32[]{:S(2)}, u32[]{:S(2)}) collective-permute-start(bf16[88,512]{1,0:T(8,128)(2,1)S(1)} %add.10.refs_3_), channel_id=1, source_target_pairs={{0,4},{1,5},{2,6},{3,7},{4,0},{5,1},{6,2},{7,3},{8,12},{9,13},{10,... | collective-permute-start | bytes 270344 | tf_op jit(solution)/shard_map/ppermute | solution.py:649
  105.7 6.4 %collective-permute-start.15 = (bf16[88,512]{1,0:T(8,128)(2,1)S(1)}, bf16[88,512]{1,0:T(8,128)(2,1)S(1)}, u32[]{:S(2)}, u32[]{:S(2)}) collective-permute-start(bf16[88,512]{1,0:T(8,128)(2,1)S(1)} %add.10.refs_3_), channel_id=1, source_target_pairs={{0,2},{1,3},{2,0},{3,1},{4,6},{5,7},{6,4},{7,5},{8,10},{9,11},{10,... | collective-permute-start | bytes 270344 | tf_op jit(solution)/shard_map/ppermute | solution.py:649
  112.1 23.9 %collective-permute-start.26 = (bf16[4,88,512]{2,1,0:T(8,128)(2,1)S(1)}, bf16[4,88,512]{2,1,0:T(8,128)(2,1)S(1)}, u32[]{:S(2)}, u32[]{:S(2)}) collective-permute-start(bf16[4,88,512]{2,1,0:T(8,128)(2,1)S(1)} %join.4.refs_0_.refs_2_), channel_id=1, source_target_pairs={{0,17},{1,16},{2,19},{3,18},{4,21},{5,20},{6,23},{7,22},{8,25},{9,... | collective-permute-start | bytes 1081352 | tf_op jit(solution)/shard_map/ppermute | solution.py:649
  115.0 21.1 %collective-permute-start.25 = (bf16[4,88,512]{2,1,0:T(8,128)(2,1)S(1)}, bf16[4,88,512]{2,1,0:T(8,128)(2,1)S(1)}, u32[]{:S(2)}, u32[]{:S(2)}) collective-permute-start(bf16[4,88,512]{2,1,0:T(8,128)(2,1)S(1)} %join.4.refs_0_.refs_2_), channel_id=1, source_target_pairs={{0,16},{1,17},{2,18},{3,19},{4,20},{5,21},{6,22},{7,23},{8,24},{9,... | collective-permute-start | bytes 1081352 | tf_op jit(solution)/shard_map/ppermute | solution.py:649
  115.5 20.5 %collective-permute-start.24 = (bf16[4,88,512]{2,1,0:T(8,128)(2,1)S(1)}, bf16[4,88,512]{2,1,0:T(8,128)(2,1)S(1)}, u32[]{:S(2)}, u32[]{:S(2)}) collective-permute-start(bf16[4,88,512]{2,1,0:T(8,128)(2,1)S(1)} %join.4.refs_0_.refs_2_), channel_id=1, source_target_pairs={{0,1},{1,0},{2,3},{3,2},{4,5},{5,4},{6,7},{7,6},{8,9},{9,8},{10,11... | collective-permute-start | bytes 1081352 | tf_op jit(solution)/shard_map/ppermute | solution.py:649
  115.7 4.1 %collective-permute-start.18 = (bf16[48,512]{1,0:T(8,128)(2,1)S(1)}, bf16[48,512]{1,0:T(8,128)(2,1)S(1)}, u32[]{:S(2)}, u32[]{:S(2)}) collective-permute-start(bf16[48,512]{1,0:T(8,128)(2,1)S(1)} %get-tuple-element.137), channel_id=1, source_target_pairs={{0,2},{1,3},{2,0},{3,1},{4,6},{5,7},{6,4},{7,5},{8,10},{9,11},{10,... | collective-permute-start | bytes 147464 | tf_op jit(solution)/shard_map/ppermute | solution.py:649
  116.4 5.9 %collective-permute-start.19 = (bf16[48,512]{1,0:T(8,128)(2,1)S(1)}, bf16[48,512]{1,0:T(8,128)(2,1)S(1)}, u32[]{:S(2)}, u32[]{:S(2)}) collective-permute-start(bf16[48,512]{1,0:T(8,128)(2,1)S(1)} %get-tuple-element.138), channel_id=1, source_target_pairs={{0,4},{1,5},{2,6},{3,7},{4,0},{5,1},{6,2},{7,3},{8,12},{9,13},{10,... | collective-permute-start | bytes 147464 | tf_op jit(solution)/shard_map/ppermute | solution.py:649
  119.8 5.9 %collective-permute-start.20 = (bf16[48,512]{1,0:T(8,128)(2,1)S(1)}, bf16[48,512]{1,0:T(8,128)(2,1)S(1)}, u32[]{:S(2)}, u32[]{:S(2)}) collective-permute-start(bf16[48,512]{1,0:T(8,128)(2,1)S(1)} %get-tuple-element.139), channel_id=1, source_target_pairs={{0,6},{1,7},{2,4},{3,5},{4,2},{5,3},{6,0},{7,1},{8,14},{9,15},{10,... | collective-permute-start | bytes 147464 | tf_op jit(solution)/shard_map/ppermute | solution.py:649
  125.7 6.2 %collective-permute-start.23 = (bf16[48,512]{1,0:T(8,128)(2,1)S(1)}, bf16[48,512]{1,0:T(8,128)(2,1)S(1)}, u32[]{:S(2)}, u32[]{:S(2)}) collective-permute-start(bf16[48,512]{1,0:T(8,128)(2,1)S(1)} %add.11.refs_0_), channel_id=1, source_target_pairs={{0,6},{1,7},{2,4},{3,5},{4,2},{5,3},{6,0},{7,1},{8,14},{9,15},{10,... | collective-permute-start | bytes 147464 | tf_op jit(solution)/shard_map/ppermute | solution.py:649
  128.4 7.5 %collective-permute-start.22 = (bf16[48,512]{1,0:T(8,128)(2,1)S(1)}, bf16[48,512]{1,0:T(8,128)(2,1)S(1)}, u32[]{:S(2)}, u32[]{:S(2)}) collective-permute-start(bf16[48,512]{1,0:T(8,128)(2,1)S(1)} %add.11.refs_0_), channel_id=1, source_target_pairs={{0,4},{1,5},{2,6},{3,7},{4,0},{5,1},{6,2},{7,3},{8,12},{9,13},{10,... | collective-permute-start | bytes 147464 | tf_op jit(solution)/shard_map/ppermute | solution.py:649
  131.9 4.1 %collective-permute-start.21 = (bf16[48,512]{1,0:T(8,128)(2,1)S(1)}, bf16[48,512]{1,0:T(8,128)(2,1)S(1)}, u32[]{:S(2)}, u32[]{:S(2)}) collective-permute-start(bf16[48,512]{1,0:T(8,128)(2,1)S(1)} %add.11.refs_0_), channel_id=1, source_target_pairs={{0,2},{1,3},{2,0},{3,1},{4,6},{5,7},{6,4},{7,5},{8,10},{9,11},{10,... | collective-permute-start | bytes 147464 | tf_op jit(solution)/shard_map/ppermute | solution.py:649
  136.1 1.9 %copy-start = (f32[6,256,512]{2,1,0:T(8,128)S(1)}, f32[6,256,512]{2,1,0:T(8,128)}, u32[]{:S(2)}) copy-start(f32[6,256,512]{2,1,0:T(8,128)} %finish.1.refs_1_) | copy-start | bytes 9437188
  138.1 3.6 %collective-permute-start.27 = (bf16[16,88,512]{2,1,0:T(8,128)(2,1)S(1)}, bf16[16,88,512]{2,1,0:T(8,128)(2,1)S(1)}, u32[]{:S(2)}, u32[]{:S(2)}) collective-permute-start(bf16[16,88,512]{2,1,0:T(8,128)(2,1)S(1)} %join.6.refs_0_), channel_id=1, source_target_pairs={{0,8},{1,9},{2,10},{3,11},{4,12},{5,13},{6,14},{7,15},{8,0},{9,1},... | collective-permute-start | bytes 4325384 | tf_op jit(solution)/shard_map/ppermute | solution.py:649
  138.1 8.7 %collective-permute-start.30 = (bf16[4,48,512]{2,1,0:T(8,128)(2,1)S(1)}, bf16[4,48,512]{2,1,0:T(8,128)(2,1)S(1)}, u32[]{:S(2)}, u32[]{:S(2)}) collective-permute-start(bf16[4,48,512]{2,1,0:T(8,128)(2,1)S(1)} %join.5.refs_0_.refs_1_), channel_id=1, source_target_pairs={{0,17},{1,16},{2,19},{3,18},{4,21},{5,20},{6,23},{7,22},{8,25},{9,... | collective-permute-start | bytes 589832 | tf_op jit(solution)/shard_map/ppermute | solution.py:649
  140.7 10.0 %collective-permute-start.29 = (bf16[4,48,512]{2,1,0:T(8,128)(2,1)S(1)}, bf16[4,48,512]{2,1,0:T(8,128)(2,1)S(1)}, u32[]{:S(2)}, u32[]{:S(2)}) collective-permute-start(bf16[4,48,512]{2,1,0:T(8,128)(2,1)S(1)} %join.5.refs_0_.refs_1_), channel_id=1, source_target_pairs={{0,16},{1,17},{2,18},{3,19},{4,20},{5,21},{6,22},{7,23},{8,24},{9,... | collective-permute-start | bytes 589832 | tf_op jit(solution)/shard_map/ppermute | solution.py:649
  141.2 9.5 %collective-permute-start.28 = (bf16[4,48,512]{2,1,0:T(8,128)(2,1)S(1)}, bf16[4,48,512]{2,1,0:T(8,128)(2,1)S(1)}, u32[]{:S(2)}, u32[]{:S(2)}) collective-permute-start(bf16[4,48,512]{2,1,0:T(8,128)(2,1)S(1)} %join.5.refs_0_.refs_1_), channel_id=1, source_target_pairs={{0,1},{1,0},{2,3},{3,2},{4,5},{5,4},{6,7},{7,6},{8,9},{9,8},{10,11... | collective-permute-start | bytes 589832 | tf_op jit(solution)/shard_map/ppermute | solution.py:649
  150.7 0.7 copy-start.5
  151.5 2.4 %collective-permute-start.31 = (bf16[16,48,512]{2,1,0:T(8,128)(2,1)S(1)}, bf16[16,48,512]{2,1,0:T(8,128)(2,1)S(1)}, u32[]{:S(2)}, u32[]{:S(2)}) collective-permute-start(bf16[16,48,512]{2,1,0:T(8,128)(2,1)S(1)} %join.7.refs_0_), channel_id=1, source_target_pairs={{0,8},{1,9},{2,10},{3,11},{4,12},{5,13},{6,14},{7,15},{8,0},{9,1},... | collective-permute-start | bytes 2359304 | tf_op jit(solution)/shard_map/ppermute | solution.py:649

commit v4 on v3

--- a/solution.py
+++ b/solution.py
@@ -350,7 +350,7 @@
 
 def store_blocks(keep_ref, send_ref, store):
     seq, dp = lax.axis_index("seq"), lax.axis_index("dp")
-    place = (dp % 2) * 16 + (dp // 2) * 8 + (seq % 2) * 4 + (seq // 2) % 4
+    place = (dp % 2) * 16 + (dp // 2) * 8 + (seq % 2) * 4 + (seq // 2) % 2 * 2 + (seq // 4) % 2
     for ref, base in ((keep_ref, 0), (send_ref, BLOCKS // 2)):
 
         @pl.loop(0, BLOCKS // 2)
@@ -493,15 +493,13 @@
             total[:, k * width + g * WIDE : k * width + (g + 1) * WIDE] = part
 
 
-def split_kernel(weight_ref, *refs):
-    *halos, total, inner_ref, other_ref, keep_ref, send_ref = refs
-    grad_halo_kernel(weight_ref, *halos, inner_ref, other_ref)
-    rows, width = total.shape[0] // BLOCKS, total.shape[0]
+def split_kernel(total_ref, keep_ref, send_ref):
+    rows, width = total_ref.shape[0] // BLOCKS, total_ref.shape[0]
 
     def store(ref, i, block):
         own = pl.ds(pl.multiple_of(block * rows, rows), rows)
         for k in range(3):
-            ref[i, k * rows : (k + 1) * rows] = total[own, k * width : (k + 1) * width]
+            ref[i, k * rows : (k + 1) * rows] = total_ref[own, k * width : (k + 1) * width]
 
     store_blocks(keep_ref, send_ref, store)
 
@@ -521,10 +519,10 @@
 
 
 def backward_kernel(*refs):
-    shared, (normed_ref, halo_normed_ref), (*grads, total) = refs[:10], refs[10:12], refs[12:]
+    shared, (weight_ref, *grads, inner_ref, other_ref) = refs[:10], refs[10:]
     for group in range(len(grads) // 2):
         attend_back_kernel(group, *shared, *grads[2 * group : 2 * group + 2])
-    weight_in_kernel(normed_ref, halo_normed_ref, *grads, total)
+    grad_halo_kernel(weight_ref, *grads[1::2], inner_ref, other_ref)
 
 
 def grad_own_kernel(weight_ref, *refs):
@@ -608,24 +606,17 @@
 
 def add_kernel(count, *refs):
     parts, outs = refs[:count], refs[count:]
-    if len(outs) == 1:
-        outs[0][...] = sum(p[...].astype(F32) for p in parts).astype(BF16)
-        return
     size = parts[0].shape[0] // len(outs)
     for k, out in enumerate(outs):
-        at = slice(k * size, (k + 1) * size) if len(out.shape) == len(parts[0].shape) else k
+        at = slice(k * size, (k + 1) * size)
         out[...] = sum(p[at].astype(F32) for p in parts).astype(BF16)
 
 
 def join_kernel(*refs):
     *parts, out = refs
-    if len(out.shape) > len(parts[0].shape):
-        for k, part in enumerate(parts):
-            out[k] = part[...]
-    else:
-        size = parts[0].shape[0]
-        for k, part in enumerate(parts):
-            out[k * size : (k + 1) * size] = part[...]
+    size = parts[0].shape[0]
+    for k, part in enumerate(parts):
+        out[k * size : (k + 1) * size] = part[...]
 
 
 def to_neighbours(inner, other):
@@ -653,12 +644,18 @@
     return jax.ShapeDtypeStruct(dims, kind)
 
 
-def call(name, kernel, outs, *args, after=(), grant=6, flops=1e9, scratch=()):
+def call(name, kernel, outs, *args, after=(), token=False, grant=6, flops=1e9, scratch=()):
+    outs = [*outs, shape(8, LANES, kind=F32)] if token else outs
     spec = pl.BlockSpec(memory_space=pltpu.VMEM)
     moved = sum(int(np.prod(a.shape)) * a.dtype.itemsize for a in (*args, *outs))
 
     def body(*refs):
-        return kernel(*refs[len(after) :])
+        refs = refs[len(after) :]
+        if token:
+            at = len(args) + len(outs) - 1
+            refs[at][...] = jnp.zeros_like(refs[at])
+            refs = refs[:at] + refs[at + 1 :]
+        return kernel(*refs)
 
     return pl.pallas_call(
         body,
@@ -667,7 +664,7 @@
         out_specs=[spec] * len(outs),
         scratch_shapes=scratch,
         compiler_params=pltpu.CompilerParams(vmem_limit_bytes=grant * MB),
-        cost_estimate=pl.CostEstimate(flops=int(flops), bytes_accessed=moved, transcendentals=0),
+        cost_estimate=pl.CostEstimate(flops=int(flops) // 100, bytes_accessed=moved // 100, transcendentals=0),
         name=name,
     )(*after, *args)
 
@@ -676,18 +673,14 @@
     return call("add", functools.partial(add_kernel, len(parts)), outs, *parts, after=after, grant=4, flops=1e6)
 
 
-def join(parts, stacked, after=()):
+def join(parts, after=()):
     size = parts[0].shape
-    out = shape(len(parts), *size) if stacked else shape(len(parts) * size[0], *size[1:])
+    out = shape(len(parts) * size[0], *size[1:])
     return call("join", join_kernel, [out], *parts, after=after, grant=4, flops=1e6)[0]
 
 
 def swap_plane(parts):
     return [swap(parts[k], x=k >> 1, y=k & 1) for k in (1, 2, 3)]
-
-
-def swap_line(parts):
-    return [swap(parts[k], z=k) for k in (1, 2, 3)]
 
 
 def swap_rest(own):
@@ -845,12 +838,10 @@
         ],
     )
 
-    def cut(blocks, parts, stacked=False):
-        if stacked:
-            return [shape(*blocks.shape[1:])] * parts
+    def cut(blocks, parts):
         return [shape(blocks.shape[0] // parts, *blocks.shape[1:])] * parts
 
-    (activations,) = call(
+    activations, done_result = call(
         "result",
         result_kernel,
         [row_shape],
@@ -861,14 +852,15 @@
         feedforward_out,
         flops=2e9,
         after=[keep_one],
-    )
-    chip_one = add_up([keep_one, swap(send_one, core=1)], cut(keep_one, 4), after=[activations])
+        token=True,
+    )
+    chip_one = add_up([keep_one, swap(send_one, core=1)], cut(keep_one, 4), after=[done_result])
     from_plane = swap_plane(chip_one)
     grad_shapes = [shape(rows, own_len, 3 * WIDE), shape(rows, 2 * win, 2 * WIDE)] * groups
-    *grads, total_in = call(
+    *grads, inner_grad, other_grad = call(
         "backward",
         backward_kernel,
-        [shape(rows, own_len, 3 * WIDE), shape(rows, 2 * win, 2 * WIDE)] * groups + [shape(*attention_in.shape)],
+        [shape(rows, own_len, 3 * WIDE), shape(rows, 2 * win, 2 * WIDE)] * groups + [shape(rows, win, width)] * 2,
         queries,
         keys,
         values,
@@ -879,43 +871,56 @@
         mid_probs,
         out_probs,
         angles,
+        weight,
+        flops=12e9,
+        after=[chip_one[0]],
+    )
+    inner_grad, other_grad = to_neighbours(inner_grad, other_grad)
+    (total_in,) = call(
+        "weight_in",
+        weight_in_kernel,
+        [shape(*attention_in.shape)],
         normed,
         halo_normed,
-        flops=16e9,
-        after=[chip_one[0]],
-    )
-    plane_one = add_up([chip_one[0], *from_plane], cut(chip_one[0], 4, True), after=[total_in])
-    from_line = swap_line(plane_one)
-    inner_grad, other_grad, keep_two, send_two = call(
+        *grads,
+        flops=4e9,
+    )
+    plane_one = add_up([chip_one[0], *from_plane], cut(chip_one[0], 2), after=[total_in])
+    keep_two, send_two = call(
         "split",
         split_kernel,
-        [shape(rows, win, width)] * 2 + [shape(BLOCKS // 2, attention_in.shape[1] // BLOCKS, width)] * 2,
-        weight,
-        *grads[1::2],
+        [shape(BLOCKS // 2, attention_in.shape[1] // BLOCKS, width)] * 2,
         total_in,
         flops=1e9,
         after=[plane_one[0]],
     )
-    from_core_two = swap(send_two, core=1)
-    inner_grad, other_grad = to_neighbours(inner_grad, other_grad)
-    (own_grad,) = call(
+    chip_two = add_up([keep_two, swap(send_two, core=1)], cut(keep_two, 4))
+    near_one = add_up([plane_one[0], swap(plane_one[1], z=1)], cut(plane_one[0], 2), after=[chip_two[0]])
+    from_plane = swap_plane(chip_two)
+    own_grad, done_own = call(
         "grad_own",
         grad_own_kernel,
         [shape(rows, own_len, width, kind=F32)],
         weight,
         *grads[::2],
         flops=2e9,
-        after=[keep_two],
-    )
-    chip_two = add_up([keep_two, from_core_two], cut(keep_two, 4), after=[own_grad])
-    from_plane = swap_plane(chip_two)
-    (line_one,) = add_up([plane_one[0], *from_line], cut(plane_one[0], 1), after=[chip_two[0]])
+        after=[near_one[0]],
+        token=True,
+    )
+    (line_one,) = add_up([near_one[0], swap(near_one[1], z=2)], cut(near_one[0], 1), after=[done_own])
     line_one = swap_rest(line_one)
-    plane_two = add_up([chip_two[0], *from_plane], cut(chip_two[0], 4, True))
-    line_one = join([line_one, *swap_line([line_one] * 4)], True, after=[plane_two[0], inner_grad, other_grad])
-    from_line = swap_line(plane_two)
+    plane_two = add_up([chip_two[0], *from_plane], cut(chip_two[0], 2), after=[line_one, inner_grad])
+    line_one = join([line_one, swap(line_one, z=2)], after=[plane_two[0]])
+    near_two = add_up([plane_two[0], swap(plane_two[1], z=1)], cut(plane_two[0], 2), after=[line_one])
+    line_one = join([line_one, swap(line_one, z=1)], after=[near_two[0]])
     from_plane = swap_plane([line_one] * 4)
-    (grad_tokens,) = call(
+    (line_two,) = add_up([near_two[0], swap(near_two[1], z=2)], cut(near_two[0], 1), after=[line_one])
+    line_two = swap_rest(line_two)
+    line_two = join([line_two, swap(line_two, z=2)])
+    line_two = join([line_two, swap(line_two, z=1)], after=[other_grad])
+    from_plane_two = swap_plane([line_two] * 4)
+    whole_one = join([line_one, *from_plane], after=[line_two])
+    grad_tokens, done_finish = call(
         "finish",
         finish_kernel,
         [shape(rows, own_len, width, kind=F32)],
@@ -927,13 +932,9 @@
         out_grad,
         gain_one,
         flops=1e8,
-        after=[line_one],
-    )
-    (line_two,) = add_up([plane_two[0], *from_line], cut(plane_two[0], 1))
-    line_two = swap_rest(line_two)
-    line_two = join([line_two, *swap_line([line_two] * 4)], True)
-    from_plane_two = swap_plane([line_two] * 4)
-    whole_one = join([line_one, *from_plane], False, after=[line_two, grad_tokens])
+        after=[whole_one],
+        token=True,
+    )
 
     def placed(parts, gain, *weights):
         outs = [shape(*w.shape, kind=F32) for w in weights] + [shape(1, width, kind=F32)]
@@ -942,7 +943,7 @@
     grad_up, grad_out, grad_down, grad_gain_two = placed(
         (whole_one, swap(whole_one, core=1)), gain_two, feedforward_in, attention_out, feedforward_out
     )
-    whole_two = join([line_two, *from_plane_two], False, after=[grad_gain_two])
+    whole_two = join([line_two, *from_plane_two], after=[grad_gain_two, done_finish])
     grad_in, grad_gain_one = placed((whole_two, swap(whole_two, core=1)), gain_one, attention_in)
     return activations, grad_tokens, grad_in, grad_out, grad_up, grad_down, grad_gain_one[0], grad_gain_two[0]
 

time: 156 us -> 140 us (0.90)
  waiting for transfers between devices: 39.6 us -> 30.1 us
  local copies, waits for them, and re-layouts: 4.01 us -> 0.71 us
  starting transfers between devices: 40.8 us -> 38 us
    ppermute x28 -> x24, waiting for transfers between devices: 38.5 us -> 29.1 us  [swap(): return lax.ppermute(values, ('dp', 'seq'), swap_route(core, x, y, z, rest))]
    unnamed x16 -> x12, local copies, waits for them, and re-layouts: 4.01 us -> 0.71 us
    ppermute x28 -> x24, starting transfers between devices: 34.5 us -> 31.6 us  [swap(): return lax.ppermute(values, ('dp', 'seq'), swap_route(core, x, y, z, rest))]
    pallas_call x24 -> x29, Pallas kernels: 68.1 us -> 68.1 us  [call(): pl.pallas_call(body, out_shape=outs, in_specs=[pl.BlockSpec(memory_space=...]
  transfers between devices with their start and end apart: 32 -> 28, of which waited for: 12 -> 12; matrix products, arithmetic and copies ran while one was open for 0% -> 0% of each run, Pallas kernels for 30% -> 34%
where the time goes in v4:
time: 140 us
  Pallas kernels  70.4 us (50%)
  starting transfers between devices  38 us (27%)
  waiting for transfers between devices  30.1 us (22%)
    pallas_call x29, Pallas kernels, call(): pl.pallas_call(body, out_shape=outs, in_specs=[pl.BlockSpec(memory_space=...  68.1 us
    ppermute x24, starting transfers between devices, swap(): return lax.ppermute(values, ('dp', 'seq'), swap_route(core, x, y, z, rest))  31.6 us
    ppermute x24, waiting for transfers between devices, swap(): return lax.ppermute(values, ('dp', 'seq'), swap_route(core, x, y, z, rest))  29.1 us
    ppermute x2, starting transfers between devices, to_neighbours(): lax.ppermute(inner, 'seq', pairs)  5.05 us
  transfers between devices with their start and end apart: 28, of which 12 were waited for; matrix products, arithmetic and copies ran while one was open for 0% of the time, Pallas kernels for 34%

profile of v4, /device:TPU:0, one launch (start us, length us, event | category | flops | bytes accessed | tf_op | source)
XLA Modules:
  0.0 140.2 jit_solution(13512805236962482865)
XLA Ops:
  0.6 2.3 %load.1 = (bf16[6,256,512]{2,1,0:T(8,128)(2,1)S(1)}, s32[6,16]{1,0:T(8,128)S(1)}, bf16[512,1536]{1,0:T(8,128)(2,1)S(1)}, f32[1,512]{1,0:T(1,128)S(1)}, f32[8,2,1...) custom-call(bf16[6,256,512]{2,1,0:T(8,128)(2,1)} %refs_0_.2, ...), custom_call_target="tpu_custom_call" | custom-call | tf_op jit(solution)/shard_map/load/pallas_call | solution.py:723
  2.9 3.0 %collective-permute-start = (bf16[6,64,512]{2,1,0:T(8,128)(2,1)S(1)}, bf16[6,64,512]{2,1,0:T(8,128)(2,1)S(1)}, u32[]{:S(2)}, u32[]{:S(2)}) collective-permute-start(bf16[6,64,512]{2,1,0:T(8,128)(2,1)S(1)} %get-tuple-element.94), channel_id=1, source_target_pairs={{0,1},{1,0},{2,3},{3,2},{4,5},{5,4},{6,7},{7,6},{8,9},{9,8},{10,11... | collective-permute-start | bytes 1179656 | tf_op jit(solution)/shard_map/ppermute | solution.py:626
  6.0 0.7 collective-permute-start.1
  6.7 4.4 %project.1 = (bf16[6,256,512]{2,1,0:T(8,128)(2,1)S(1)}, bf16[6,256,512]{2,1,0:T(8,128)(2,1)S(1)}, bf16[6,256,512]{2,1,0:T(8,128)(2,1)S(1)}, bf16[6,256,512]{2,1,...) custom-call(bf16[6,256,512]{2,1,0:T(8,128)(2,1)S(1)} %get-tuple-element.82., ...), custom_call_target="tpu_custom_call" | custom-call | flops 30000000 | bytes 118255 | tf_op jit(solution)/shard_map/project/pallas_call | solution.py:660
  11.1 3.9 %attend_mid.1 = (bf16[6,128,512]{2,1,0:T(8,128)(2,1)S(1)}, f32[6,2,256,512]{3,2,1,0:T(8,128)S(1)}) custom-call(bf16[6,256,512]{2,1,0:T(8,128)(2,1)S(1)} %get-tuple-element.88.refs_0_.refs_1_, bf16[6,256,512]{2,1,0:T(8,128)(2,1)S(1)} %get-tuple-element.89.refs_1_.refs_2_, bf16[6,256,512]{2,1,0:T(8,128)(2,1)S(1)} %get-tuple-element.90.refs_2_.refs_3_, ...), custom_call_target="tpu_custom_call" | custom-call | flops 20000000 | bytes 118149 | tf_op jit(solution)/shard_map/attend_mid/pallas_call | solution.py:660
  15.1 6.7 %dense_mid.1 = (f32[6,128,512]{2,1,0:T(8,128)S(1)}, bf16[6,128,512]{2,1,0:T(8,128)(2,1)S(1)}, bf16[6,128,768]{2,1,0:T(8,128)(2,1)S(1)}, bf16[6,128,1536]{2,1,0:T...) custom-call(bf16[6,256,512]{2,1,0:T(8,128)(2,1)S(1)} %get-tuple-elem, ...), custom_call_target="tpu_custom_call" | custom-call | flops 50000000 | bytes 158617 | tf_op jit(solution)/shard_map/dense_mid/pallas_call | solution.py:660
  21.8 1.0 collective-permute-done.refs_0_
  22.8 1.7 %halo.1 = (bf16[6,128,512]{2,1,0:T(8,128)(2,1)S(1)}, bf16[6,128,512]{2,1,0:T(8,128)(2,1)S(1)}, bf16[6,128,512]{2,1,0:T(8,128)(2,1)S(1)}) custom-call(bf16[6,64,512]{2,1,0:T(8,128)(2,1)S(1)} %collective-permute-done.refs_0_, bf16[6,64,512]{2,1,0:T(8,128)(2,1)S(1)} %collective-permute-done.1.refs_1_, ...), custom_call_target="tpu_custom_call" | custom-call | flops 10000000 | bytes 51138 | tf_op jit(solution)/shard_map/halo/pallas_call | solution.py:660
  24.5 4.2 %attend_out.1 = (bf16[6,128,512]{2,1,0:T(8,128)(2,1)S(1)}, f32[6,2,2,192,256]{4,3,2,1,0:T(8,128)S(1)}) custom-call(bf16[6,256,512]{2,1,0:T(8,128)(2,1)S(1)} %get-tuple-element.88.refs_0_.refs_1_, bf16[6,256,512]{2,1,0:T(8,128)(2,1)S(1)} %get-tuple-element.89.refs_1_.refs_2_, bf16[6,256,512]{2,1,0:T(8,128)(2,1)S(1)} %get-tuple-element.90.refs_2_.refs_3_, ...), custom_call_target="tpu_custom_call" | custom-call | flops 20000000 | bytes 118149 | tf_op jit(solution)/shard_map/attend_out/pallas_call | solution.py:660
  28.6 6.8 %dense_out.1 = (f32[6,128,512]{2,1,0:T(8,128)S(1)}, bf16[6,128,512]{2,1,0:T(8,128)(2,1)S(1)}, bf16[6,128,768]{2,1,0:T(8,128)(2,1)S(1)}, bf16[6,128,1536]{2,1,0:T...) custom-call(bf16[6,256,512]{2,1,0:T(8,128)(2,1)S(1)} %get-tuple-elem, ...), custom_call_target="tpu_custom_call" | custom-call | flops 50000000 | bytes 158617 | tf_op jit(solution)/shard_map/dense_out/pallas_call | solution.py:660
  35.4 5.0 %weights.1 = (bf16[16,88,512]{2,1,0:T(8,128)(2,1)S(1)}, bf16[16,88,512]{2,1,0:T(8,128)(2,1)S(1)}) custom-call(bf16[6,256,512]{2,1,0:T(8,128)(2,1)S(1)} %copy-done, bf16[6,128,512]{2,1,0:T(8,128)(2,1)S(1)} %get-tuple-element.93.refs_1_, bf16[6,128,512]{2,1,0:T(8,128)(2,1)S(1)} %get-tuple-element.101.refs_2_, ...), custom_call_target="tpu_custom_call" | custom-call | flops 50000000 | bytes 162529 | tf_op jit(solution)/shard_map/weights/pallas_call | solution.py:660
  40.5 2.7 %result.1 = (bf16[6,256,512]{2,1,0:T(8,128)(2,1)}, f32[8,128]{1,0:T(8,128)S(1)}) custom-call(bf16[16,88,512]{2,1,0:T(8,128)(2,1)S(1)} %get-tuple-element.108.refs_0_.refs_1_, f32[6,128,512]{2,1,0:T(8,128)S(1)} %get-tuple-element.109.refs_1_, f32[6,128,512]{2,1,0:T(8,128)S(1)} %get-tuple-element.110.refs_2_, ...), custom_call_target="tpu_custom_call" | custom-call | flops 20000000 | bytes 78684 | tf_op jit(solution)/shard_map/result/pallas_call | solution.py:660
  44.1 3.4 %collective-permute-start.4 = (bf16[4,88,512]{2,1,0:T(8,128)(2,1)S(1)}, bf16[4,88,512]{2,1,0:T(8,128)(2,1)S(1)}, u32[]{:S(2)}, u32[]{:S(2)}) collective-permute-start(bf16[4,88,512]{2,1,0:T(8,128)(2,1)S(1)} %get-tuple-element.126), channel_id=1, source_target_pairs={{0,1},{1,0},{2,3},{3,2},{4,5},{5,4},{6,7},{7,6},{8,9},{9,8},{10,11... | collective-permute-start | bytes 1081352 | tf_op jit(solution)/shard_map/ppermute | solution.py:640
  47.5 1.5 %collective-permute-start.5 = (bf16[4,88,512]{2,1,0:T(8,128)(2,1)S(1)}, bf16[4,88,512]{2,1,0:T(8,128)(2,1)S(1)}, u32[]{:S(2)}, u32[]{:S(2)}) collective-permute-start(bf16[4,88,512]{2,1,0:T(8,128)(2,1)S(1)} %get-tuple-element.127), channel_id=1, source_target_pairs={{0,16},{1,17},{2,18},{3,19},{4,20},{5,21},{6,22},{7,23},{8,24},{9,... | collective-permute-start | bytes 1081352 | tf_op jit(solution)/shard_map/ppermute | solution.py:640
  49.0 13.9 %backward.1 = (bf16[6,256,768]{2,1,0:T(8,128)(2,1)S(1)}, bf16[6,128,512]{2,1,0:T(8,128)(2,1)S(1)}, bf16[6,256,768]{2,1,0:T(8,128)(2,1)S(1)}, bf16[6,128,512]{2,1...) custom-call(bf16[4,88,512]{2,1,0:T(8,128)(2,1)S(1)} %get-tuple-element.114.refs_0_.refs_1_, ...), custom_call_target="tpu_custom_call" | custom-call | flops 120000000 | bytes 279183 | tf_op jit(solution)/shard_map/backward/pallas_call | solution.py:660
  62.9 5.6 %weight_in.1.refs_0_.refs_1_ = bf16[512,1536]{1,0:T(8,128)(2,1)S(1)} custom-call(bf16[6,256,512]{2,1,0:T(8,128)(2,1)S(1)} %get-tuple-element.120.refs_0_, bf16[6,128,512]{2,1,0:T(8,128)(2,1)S(1)} %get-tuple-element.121.refs_1_, bf16[6,256,768]{2,1,0:T(8,128)(2,1)S(1)} %get-tuple-element.122.refs_2_, bf16[6,128,512]{2,1,0:T(8,128)(2,1)S(1)} %get-tuple-element.123.refs_3_, ...), custom_call_target="tpu_custom_call" | custom-call | flops 40000000 | bytes 102236 | tf_op jit(solution)/shard_map/weight_in/pallas_call | solution.py:660
  69.0 2.0 %collective-permute-start.10 = (bf16[6,64,512]{2,1,0:T(8,128)(2,1)S(1)}, bf16[6,64,512]{2,1,0:T(8,128)(2,1)S(1)}, u32[]{:S(2)}, u32[]{:S(2)}) collective-permute-start(bf16[6,64,512]{2,1,0:T(8,128)(2,1)S(1)} %get-tuple-element.137), channel_id=1, source_target_pairs={{0,1},{1,0},{2,3},{3,2},{4,5},{5,4},{6,7},{7,6},{8,9},{9,8},{10,11... | collective-permute-start | bytes 1179656 | tf_op jit(solution)/shard_map/ppermute | solution.py:626
  71.1 1.6 %collective-permute-start.8 = (bf16[2,88,512]{2,1,0:T(8,128)(2,1)S(1)}, bf16[2,88,512]{2,1,0:T(8,128)(2,1)S(1)}, u32[]{:S(2)}, u32[]{:S(2)}) collective-permute-start(bf16[2,88,512]{2,1,0:T(8,128)(2,1)S(1)} %get-tuple-element.133), channel_id=1, source_target_pairs={{0,2},{1,3},{2,0},{3,1},{4,6},{5,7},{6,4},{7,5},{8,10},{9,11},{10,... | collective-permute-start | bytes 540680 | tf_op jit(solution)/shard_map/ppermute | solution.py:640
  72.8 0.7 collective-permute-start.11
  73.5 1.5 %collective-permute-start.12 = (bf16[4,48,512]{2,1,0:T(8,128)(2,1)S(1)}, bf16[4,48,512]{2,1,0:T(8,128)(2,1)S(1)}, u32[]{:S(2)}, u32[]{:S(2)}) collective-permute-start(bf16[4,48,512]{2,1,0:T(8,128)(2,1)S(1)} %get-tuple-element.139), channel_id=1, source_target_pairs={{0,16},{1,17},{2,18},{3,19},{4,20},{5,21},{6,22},{7,23},{8,24},{9,... | collective-permute-start | bytes 589832 | tf_op jit(solution)/shard_map/ppermute | solution.py:640
  75.0 1.4 collective-permute-start.13
  76.4 1.3 collective-permute-done.8.refs_2_
  77.7 2.7 %collective-permute-start.9 = (bf16[1,88,512]{2,1,0:T(8,128)(2,1)S(1)}, bf16[1,88,512]{2,1,0:T(8,128)(2,1)S(1)}, u32[]{:S(2)}, u32[]{:S(2)}) collective-permute-start(bf16[1,88,512]{2,1,0:T(8,128)(2,1)S(1)} %get-tuple-element.136), channel_id=1, source_target_pairs={{0,4},{1,5},{2,6},{3,7},{4,0},{5,1},{6,2},{7,3},{8,12},{9,13},{10,... | collective-permute-start | bytes 270344 | tf_op jit(solution)/shard_map/ppermute | solution.py:640
  80.4 3.0 %grad_own.1 = (f32[6,256,512]{2,1,0:T(8,128)S(1)}, f32[8,128]{1,0:T(8,128)S(1)}) custom-call(bf16[1,88,512]{2,1,0:T(8,128)(2,1)S(1)} %get-tuple-element.134.refs_0_.refs_1_, bf16[512,1536]{1,0:T(8,128)(2,1)S(1)} %get-tuple-element.96.refs_2_.refs_11_.refs_1_, bf16[6,256,768]{2,1,0:T(8,128)(2,1)S(1)} %get-tuple-element.122.refs_2_, ...), custom_call_target="tpu_custom_call" | custom-call | flops 20000000 | bytes 94412 | tf_op jit(solution)/shard_map/grad_own/pallas_call | solution.py:660
  83.4 1.1 collective-permute-done.9.refs_2_
  84.6 1.4 %collective-permute-start.14 = (bf16[1,88,512]{2,1,0:T(8,128)(2,1)S(1)}, bf16[1,88,512]{2,1,0:T(8,128)(2,1)S(1)}, u32[]{:S(2)}, u32[]{:S(2)}) collective-permute-start(bf16[1,88,512]{2,1,0:T(8,128)(2,1)S(1)} %add.12.refs_0_.refs_1_), channel_id=1, source_target_pairs={{0,4},{1,5},{2,6},{3,7},{4,0},{5,1},{6,2},{7,3},{8,12},{9,13},{10,... | collective-permute-start | bytes 270344 | tf_op jit(solution)/shard_map/ppermute | solution.py:640
  86.0 3.2 %collective-permute-done.11.refs_3_ = bf16[4,48,512]{2,1,0:T(8,128)(2,1)S(1)} collective-permute-done((bf16[4,48,512]{2,1,0:T(8,128)(2,1)S(1)}, bf16[4,48,512]{2,1,0:T(8,128)(2,1)S(1)}, u32[]{:S(2)}, u32[]{:S(2)}) %collective-permute-start.11) | collective-permute-done | bytes 196640 | tf_op jit(solution)/shard_map/ppermute | solution.py:640
  89.3 1.5 %collective-permute-done.14.refs_2_ = bf16[1,88,512]{2,1,0:T(8,128)(2,1)S(1)} collective-permute-done((bf16[1,88,512]{2,1,0:T(8,128)(2,1)S(1)}, bf16[1,88,512]{2,1,0:T(8,128)(2,1)S(1)}, u32[]{:S(2)}, u32[]{:S(2)}) %collective-permute-start.14) | collective-permute-done | bytes 90144 | tf_op jit(solution)/shard_map/ppermute | solution.py:640
  91.0 1.9 %collective-permute-start.15 = (bf16[2,48,512]{2,1,0:T(8,128)(2,1)S(1)}, bf16[2,48,512]{2,1,0:T(8,128)(2,1)S(1)}, u32[]{:S(2)}, u32[]{:S(2)}) collective-permute-start(bf16[2,48,512]{2,1,0:T(8,128)(2,1)S(1)} %get-tuple-element.142), channel_id=1, source_target_pairs={{0,2},{1,3},{2,0},{3,1},{4,6},{5,7},{6,4},{7,5},{8,10},{9,11},{10,... | collective-permute-start | bytes 294920 | tf_op jit(solution)/shard_map/ppermute | solution.py:640
  92.9 0.7 collective-permute-start.3
  93.6 5.6 %collective-permute-done.15.refs_2_ = bf16[2,48,512]{2,1,0:T(8,128)(2,1)S(1)} collective-permute-done((bf16[2,48,512]{2,1,0:T(8,128)(2,1)S(1)}, bf16[2,48,512]{2,1,0:T(8,128)(2,1)S(1)}, u32[]{:S(2)}, u32[]{:S(2)}) %collective-permute-start.15) | collective-permute-done | bytes 98336 | tf_op jit(solution)/shard_map/ppermute | solution.py:640
  99.3 1.6 %collective-permute-start.22 = (bf16[4,88,512]{2,1,0:T(8,128)(2,1)S(1)}, bf16[4,88,512]{2,1,0:T(8,128)(2,1)S(1)}, u32[]{:S(2)}, u32[]{:S(2)}) collective-permute-start(bf16[4,88,512]{2,1,0:T(8,128)(2,1)S(1)} %join.7.refs_0_.refs_1_), channel_id=1, source_target_pairs={{0,17},{1,16},{2,19},{3,18},{4,21},{5,20},{6,23},{7,22},{8,25},{9,... | collective-permute-start | bytes 1081352 | tf_op jit(solution)/shard_map/ppermute | solution.py:640
  100.9 0.5 collective-permute-start.21
  101.4 1.4 %collective-permute-start.20 = (bf16[4,88,512]{2,1,0:T(8,128)(2,1)S(1)}, bf16[4,88,512]{2,1,0:T(8,128)(2,1)S(1)}, u32[]{:S(2)}, u32[]{:S(2)}) collective-permute-start(bf16[4,88,512]{2,1,0:T(8,128)(2,1)S(1)} %join.7.refs_0_.refs_1_), channel_id=1, source_target_pairs={{0,1},{1,0},{2,3},{3,2},{4,5},{5,4},{6,7},{7,6},{8,9},{9,8},{10,11... | collective-permute-start | bytes 1081352 | tf_op jit(solution)/shard_map/ppermute | solution.py:640
  102.9 2.3 %collective-permute-start.17 = (bf16[1,48,512]{2,1,0:T(8,128)(2,1)S(1)}, bf16[1,48,512]{2,1,0:T(8,128)(2,1)S(1)}, u32[]{:S(2)}, u32[]{:S(2)}) collective-permute-start(bf16[1,48,512]{2,1,0:T(8,128)(2,1)S(1)} %get-tuple-element.144), channel_id=1, source_target_pairs={{0,4},{1,5},{2,6},{3,7},{4,0},{5,1},{6,2},{7,3},{8,12},{9,13},{10,... | collective-permute-start | bytes 147464 | tf_op jit(solution)/shard_map/ppermute | solution.py:640
  105.2 4.5 %collective-permute-done.17.refs_2_ = bf16[1,48,512]{2,1,0:T(8,128)(2,1)S(1)} collective-permute-done((bf16[1,48,512]{2,1,0:T(8,128)(2,1)S(1)}, bf16[1,48,512]{2,1,0:T(8,128)(2,1)S(1)}, u32[]{:S(2)}, u32[]{:S(2)}) %collective-permute-start.17) | collective-permute-done | bytes 49184 | tf_op jit(solution)/shard_map/ppermute | solution.py:640
  109.7 0.6 collective-permute-start.18
  110.3 4.5 %collective-permute-done.18.refs_1_ = bf16[1,48,512]{2,1,0:T(8,128)(2,1)S(1)} collective-permute-done((bf16[1,48,512]{2,1,0:T(8,128)(2,1)S(1)}, bf16[1,48,512]{2,1,0:T(8,128)(2,1)S(1)}, u32[]{:S(2)}, u32[]{:S(2)}) %collective-permute-start.18) | collective-permute-done | bytes 49184 | tf_op jit(solution)/shard_map/ppermute | solution.py:640
  114.8 5.1 %collective-permute-start.19 = (bf16[2,48,512]{2,1,0:T(8,128)(2,1)S(1)}, bf16[2,48,512]{2,1,0:T(8,128)(2,1)S(1)}, u32[]{:S(2)}, u32[]{:S(2)}) collective-permute-start(bf16[2,48,512]{2,1,0:T(8,128)(2,1)S(1)} %join.8.refs_1_), channel_id=1, source_target_pairs={{0,2},{1,3},{2,0},{3,1},{4,6},{5,7},{6,4},{7,5},{8,10},{9,11},{10,... | collective-permute-start | bytes 294920 | tf_op jit(solution)/shard_map/ppermute | solution.py:640
  119.8 2.6 %collective-permute-done.19.refs_2_ = bf16[2,48,512]{2,1,0:T(8,128)(2,1)S(1)} collective-permute-done((bf16[2,48,512]{2,1,0:T(8,128)(2,1)S(1)}, bf16[2,48,512]{2,1,0:T(8,128)(2,1)S(1)}, u32[]{:S(2)}, u32[]{:S(2)}) %collective-permute-start.19) | collective-permute-done | bytes 98336 | tf_op jit(solution)/shard_map/ppermute | solution.py:640
  122.7 2.4 %collective-permute-start.26 = (bf16[4,48,512]{2,1,0:T(8,128)(2,1)S(1)}, bf16[4,48,512]{2,1,0:T(8,128)(2,1)S(1)}, u32[]{:S(2)}, u32[]{:S(2)}) collective-permute-start(bf16[4,48,512]{2,1,0:T(8,128)(2,1)S(1)} %join.9.refs_0_.refs_2_), channel_id=1, source_target_pairs={{0,17},{1,16},{2,19},{3,18},{4,21},{5,20},{6,23},{7,22},{8,25},{9,... | collective-permute-start | bytes 589832 | tf_op jit(solution)/shard_map/ppermute | solution.py:640
  125.6 0.6 collective-permute-start.24
  126.2 3.9 %finish.1 = (f32[6,256,512]{2,1,0:T(8,128)}, f32[8,128]{1,0:T(8,128)S(1)}) custom-call(bf16[16,88,512]{2,1,0:T(8,128)(2,1)S(1)} %join.10.refs_0_, bf16[6,256,512]{2,1,0:T(8,128)(2,1)S(1)} %get-tuple-element.82.refs_0_.refs_1_, f32[6,256,512]{2,1,0:T(8,128)S(1)} %get-tuple-element.145.refs_2_, ...), custom_call_target="tpu_custom_call" | custom-call | flops 1000000 | bytes 118026 | tf_op jit(solution)/shard_map/finish/pallas_call | solution.py:660
  130.1 3.0 %place.2 = (f32[512,1536]{1,0:T(8,128)}, f32[512,512]{1,0:T(8,128)}, f32[768,512]{1,0:T(8,128)}, f32[1,512]{1,0:T(1,128)}) custom-call(bf16[16,88,512]{2,1,0:T(8,128)(2,1)S(1)} %join.10.refs_0_, bf16[16,88,512]{2,1,0:T(8,128)(2,1)S(1)} %collective-permute-done.23.refs_1_, bf16[512,1536]{1,0:T(8,128)(2,1)S(1)} %copy-done.1, f32[1,512]{1,0:T(1,128)S(1)} %bitcast.6), custom_call_target="tpu_custom_call" | custom-call | flops 10000 | bytes 102277 | tf_op jit(solution)/shard_map/place/pallas_call | solution.py:660
  133.1 2.0 %collective-permute-done.25.refs_4_ = bf16[4,48,512]{2,1,0:T(8,128)(2,1)S(1)} collective-permute-done((bf16[4,48,512]{2,1,0:T(8,128)(2,1)S(1)}, bf16[4,48,512]{2,1,0:T(8,128)(2,1)S(1)}, u32[]{:S(2)}, u32[]{:S(2)}) %collective-permute-start.25) | collective-permute-done | bytes 196640 | tf_op jit(solution)/shard_map/ppermute | solution.py:640
  135.1 0.7 copy-done.5
  135.9 2.3 %collective-permute-done.27.refs_1_ = bf16[16,48,512]{2,1,0:T(8,128)(2,1)S(1)} collective-permute-done((bf16[16,48,512]{2,1,0:T(8,128)(2,1)S(1)}, bf16[16,48,512]{2,1,0:T(8,128)(2,1)S(1)}, u32[]{:S(2)}, u32[]{:S(2)}) %collective-permute-start.27) | collective-permute-done | bytes 786464 | tf_op jit(solution)/shard_map/ppermute | solution.py:640
  138.2 2.0 %place.3 = (f32[512,1536]{1,0:T(8,128)}, f32[1,512]{1,0:T(1,128)}) custom-call(bf16[16,48,512]{2,1,0:T(8,128)(2,1)S(1)} %join.11.refs_0_, bf16[16,48,512]{2,1,0:T(8,128)(2,1)S(1)} %collective-permute-done.27.refs_1_, bf16[512,1536]{1,0:T(8,128)(2,1)S(1)} %get-tuple-element.84.refs_2_, f32[1,512]{1,0:T(1,128)S(1)} %get-tuple-element.85.refs_3_.refs_7_), custom_call_target="tpu_custom_call" | custom-call | flops 10000 | bytes 62955 | tf_op jit(solution)/shard_map/place/pallas_call | solution.py:660
  (50 shorter events, 3.0 us)
Async XLA Ops:
  2.9 19.8 %collective-permute-start = (bf16[6,64,512]{2,1,0:T(8,128)(2,1)S(1)}, bf16[6,64,512]{2,1,0:T(8,128)(2,1)S(1)}, u32[]{:S(2)}, u32[]{:S(2)}) collective-permute-start(bf16[6,64,512]{2,1,0:T(8,128)(2,1)S(1)} %get-tuple-element.94), channel_id=1, source_target_pairs={{0,1},{1,0},{2,3},{3,2},{4,5},{5,4},{6,7},{7,6},{8,9},{9,8},{10,11... | collective-permute-start | bytes 1179656 | tf_op jit(solution)/shard_map/ppermute | solution.py:626
  6.0 16.8 %collective-permute-start.1 = (bf16[6,64,512]{2,1,0:T(8,128)(2,1)S(1)}, bf16[6,64,512]{2,1,0:T(8,128)(2,1)S(1)}, u32[]{:S(2)}, u32[]{:S(2)}) collective-permute-start(bf16[6,64,512]{2,1,0:T(8,128)(2,1)S(1)} %get-tuple-element.95), channel_id=1, source_target_pairs={{1,2},{2,1},{3,4},{4,3},{5,6},{6,5},{9,10},{10,9},{11,12},{12,11},... | collective-permute-start | bytes 1179656 | tf_op jit(solution)/shard_map/ppermute | solution.py:626
  11.1 4.0 %copy-start = (bf16[6,256,512]{2,1,0:T(8,128)(2,1)S(1)}, bf16[6,256,512]{2,1,0:T(8,128)(2,1)}, u32[]{:S(2)}) copy-start(bf16[6,256,512]{2,1,0:T(8,128)(2,1)} %refs_0_.3) | copy-start | bytes 4718596
  11.1 4.0 %copy-start.1 = (bf16[512,1536]{1,0:T(8,128)(2,1)S(1)}, bf16[512,1536]{1,0:T(8,128)(2,1)}, u32[]{:S(2)}) copy-start(bf16[512,1536]{1,0:T(8,128)(2,1)} %refs_2_.3) | copy-start | bytes 4718596
  11.1 4.0 %copy-start.2 = (bf16[768,512]{1,0:T(8,128)(2,1)S(1)}, bf16[768,512]{1,0:T(8,128)(2,1)}, u32[]{:S(2)}) copy-start(bf16[768,512]{1,0:T(8,128)(2,1)} %refs_5_.6) | copy-start | bytes 2359300
  11.1 4.0 %copy-start.3 = (bf16[512,512]{1,0:T(8,128)(2,1)S(1)}, bf16[512,512]{1,0:T(8,128)(2,1)}, u32[]{:S(2)}) copy-start(bf16[512,512]{1,0:T(8,128)(2,1)} %refs_3_.3) | copy-start | bytes 1572868
  11.1 4.0 %copy-start.4 = (f32[512]{0:T(512)S(1)}, f32[512]{0:T(512)}, u32[]{:S(2)}) copy-start(f32[512]{0:T(512)} %param.18) | copy-start | bytes 6148
  40.5 3.3 %collective-permute-start.2 = (bf16[16,88,512]{2,1,0:T(8,128)(2,1)S(1)}, bf16[16,88,512]{2,1,0:T(8,128)(2,1)S(1)}, u32[]{:S(2)}, u32[]{:S(2)}) collective-permute-start(bf16[16,88,512]{2,1,0:T(8,128)(2,1)S(1)} %get-tuple-element.113), channel_id=1, source_target_pairs={{0,8},{1,9},{2,10},{3,11},{4,12},{5,13},{6,14},{7,15},{8,0},{9,1},... | collective-permute-start | bytes 4325384 | tf_op jit(solution)/shard_map/ppermute | solution.py:640
  44.1 24.4 %collective-permute-start.4 = (bf16[4,88,512]{2,1,0:T(8,128)(2,1)S(1)}, bf16[4,88,512]{2,1,0:T(8,128)(2,1)S(1)}, u32[]{:S(2)}, u32[]{:S(2)}) collective-permute-start(bf16[4,88,512]{2,1,0:T(8,128)(2,1)S(1)} %get-tuple-element.126), channel_id=1, source_target_pairs={{0,1},{1,0},{2,3},{3,2},{4,5},{5,4},{6,7},{7,6},{8,9},{9,8},{10,11... | collective-permute-start | bytes 1081352 | tf_op jit(solution)/shard_map/ppermute | solution.py:640
  47.5 21.0 %collective-permute-start.5 = (bf16[4,88,512]{2,1,0:T(8,128)(2,1)S(1)}, bf16[4,88,512]{2,1,0:T(8,128)(2,1)S(1)}, u32[]{:S(2)}, u32[]{:S(2)}) collective-permute-start(bf16[4,88,512]{2,1,0:T(8,128)(2,1)S(1)} %get-tuple-element.127), channel_id=1, source_target_pairs={{0,16},{1,17},{2,18},{3,19},{4,20},{5,21},{6,22},{7,23},{8,24},{9,... | collective-permute-start | bytes 1081352 | tf_op jit(solution)/shard_map/ppermute | solution.py:640
  49.0 19.5 %collective-permute-start.6 = (bf16[4,88,512]{2,1,0:T(8,128)(2,1)S(1)}, bf16[4,88,512]{2,1,0:T(8,128)(2,1)S(1)}, u32[]{:S(2)}, u32[]{:S(2)}) collective-permute-start(bf16[4,88,512]{2,1,0:T(8,128)(2,1)S(1)} %get-tuple-element.128), channel_id=1, source_target_pairs={{0,17},{1,16},{2,19},{3,18},{4,21},{5,20},{6,23},{7,22},{8,25},{9,... | collective-permute-start | bytes 1081352 | tf_op jit(solution)/shard_map/ppermute | solution.py:640
  69.0 3.7 %collective-permute-start.7 = (bf16[16,48,512]{2,1,0:T(8,128)(2,1)S(1)}, bf16[16,48,512]{2,1,0:T(8,128)(2,1)S(1)}, u32[]{:S(2)}, u32[]{:S(2)}) collective-permute-start(bf16[16,48,512]{2,1,0:T(8,128)(2,1)S(1)} %get-tuple-element.131), channel_id=1, source_target_pairs={{0,8},{1,9},{2,10},{3,11},{4,12},{5,13},{6,14},{7,15},{8,0},{9,1},... | collective-permute-start | bytes 2359304 | tf_op jit(solution)/shard_map/ppermute | solution.py:640
  69.0 17.0 %collective-permute-start.10 = (bf16[6,64,512]{2,1,0:T(8,128)(2,1)S(1)}, bf16[6,64,512]{2,1,0:T(8,128)(2,1)S(1)}, u32[]{:S(2)}, u32[]{:S(2)}) collective-permute-start(bf16[6,64,512]{2,1,0:T(8,128)(2,1)S(1)} %get-tuple-element.137), channel_id=1, source_target_pairs={{0,1},{1,0},{2,3},{3,2},{4,5},{5,4},{6,7},{7,6},{8,9},{9,8},{10,11... | collective-permute-start | bytes 1179656 | tf_op jit(solution)/shard_map/ppermute | solution.py:626
  71.1 6.6 %collective-permute-start.8 = (bf16[2,88,512]{2,1,0:T(8,128)(2,1)S(1)}, bf16[2,88,512]{2,1,0:T(8,128)(2,1)S(1)}, u32[]{:S(2)}, u32[]{:S(2)}) collective-permute-start(bf16[2,88,512]{2,1,0:T(8,128)(2,1)S(1)} %get-tuple-element.133), channel_id=1, source_target_pairs={{0,2},{1,3},{2,0},{3,1},{4,6},{5,7},{6,4},{7,5},{8,10},{9,11},{10,... | collective-permute-start | bytes 540680 | tf_op jit(solution)/shard_map/ppermute | solution.py:640
  72.8 16.4 %collective-permute-start.11 = (bf16[4,48,512]{2,1,0:T(8,128)(2,1)S(1)}, bf16[4,48,512]{2,1,0:T(8,128)(2,1)S(1)}, u32[]{:S(2)}, u32[]{:S(2)}) collective-permute-start(bf16[4,48,512]{2,1,0:T(8,128)(2,1)S(1)} %get-tuple-element.138), channel_id=1, source_target_pairs={{0,1},{1,0},{2,3},{3,2},{4,5},{5,4},{6,7},{7,6},{8,9},{9,8},{10,11... | collective-permute-start | bytes 589832 | tf_op jit(solution)/shard_map/ppermute | solution.py:640
  73.5 15.7 %collective-permute-start.12 = (bf16[4,48,512]{2,1,0:T(8,128)(2,1)S(1)}, bf16[4,48,512]{2,1,0:T(8,128)(2,1)S(1)}, u32[]{:S(2)}, u32[]{:S(2)}) collective-permute-start(bf16[4,48,512]{2,1,0:T(8,128)(2,1)S(1)} %get-tuple-element.139), channel_id=1, source_target_pairs={{0,16},{1,17},{2,18},{3,19},{4,20},{5,21},{6,22},{7,23},{8,24},{9,... | collective-permute-start | bytes 589832 | tf_op jit(solution)/shard_map/ppermute | solution.py:640
  75.0 14.2 %collective-permute-start.13 = (bf16[4,48,512]{2,1,0:T(8,128)(2,1)S(1)}, bf16[4,48,512]{2,1,0:T(8,128)(2,1)S(1)}, u32[]{:S(2)}, u32[]{:S(2)}) collective-permute-start(bf16[4,48,512]{2,1,0:T(8,128)(2,1)S(1)} %get-tuple-element.140), channel_id=1, source_target_pairs={{0,17},{1,16},{2,19},{3,18},{4,21},{5,20},{6,23},{7,22},{8,25},{9,... | collective-permute-start | bytes 589832 | tf_op jit(solution)/shard_map/ppermute | solution.py:640
  77.7 6.8 %collective-permute-start.9 = (bf16[1,88,512]{2,1,0:T(8,128)(2,1)S(1)}, bf16[1,88,512]{2,1,0:T(8,128)(2,1)S(1)}, u32[]{:S(2)}, u32[]{:S(2)}) collective-permute-start(bf16[1,88,512]{2,1,0:T(8,128)(2,1)S(1)} %get-tuple-element.136), channel_id=1, source_target_pairs={{0,4},{1,5},{2,6},{3,7},{4,0},{5,1},{6,2},{7,3},{8,12},{9,13},{10,... | collective-permute-start | bytes 270344 | tf_op jit(solution)/shard_map/ppermute | solution.py:640
  84.6 6.3 %collective-permute-start.14 = (bf16[1,88,512]{2,1,0:T(8,128)(2,1)S(1)}, bf16[1,88,512]{2,1,0:T(8,128)(2,1)S(1)}, u32[]{:S(2)}, u32[]{:S(2)}) collective-permute-start(bf16[1,88,512]{2,1,0:T(8,128)(2,1)S(1)} %add.12.refs_0_.refs_1_), channel_id=1, source_target_pairs={{0,4},{1,5},{2,6},{3,7},{4,0},{5,1},{6,2},{7,3},{8,12},{9,13},{10,... | collective-permute-start | bytes 270344 | tf_op jit(solution)/shard_map/ppermute | solution.py:640
  90.8 8.4 %collective-permute-start.16 = (bf16[2,88,512]{2,1,0:T(8,128)(2,1)S(1)}, bf16[2,88,512]{2,1,0:T(8,128)(2,1)S(1)}, u32[]{:S(2)}, u32[]{:S(2)}) collective-permute-start(bf16[2,88,512]{2,1,0:T(8,128)(2,1)S(1)} %join.6.refs_0_.refs_1_), channel_id=1, source_target_pairs={{0,2},{1,3},{2,0},{3,1},{4,6},{5,7},{6,4},{7,5},{8,10},{9,11},{10,... | collective-permute-start | bytes 540680 | tf_op jit(solution)/shard_map/ppermute | solution.py:640
  91.0 8.2 %collective-permute-start.15 = (bf16[2,48,512]{2,1,0:T(8,128)(2,1)S(1)}, bf16[2,48,512]{2,1,0:T(8,128)(2,1)S(1)}, u32[]{:S(2)}, u32[]{:S(2)}) collective-permute-start(bf16[2,48,512]{2,1,0:T(8,128)(2,1)S(1)} %get-tuple-element.142), channel_id=1, source_target_pairs={{0,2},{1,3},{2,0},{3,1},{4,6},{5,7},{6,4},{7,5},{8,10},{9,11},{10,... | collective-permute-start | bytes 294920 | tf_op jit(solution)/shard_map/ppermute | solution.py:640
  92.9 26.9 %collective-permute-start.3 = (bf16[6,64,512]{2,1,0:T(8,128)(2,1)S(1)}, bf16[6,64,512]{2,1,0:T(8,128)(2,1)S(1)}, u32[]{:S(2)}, u32[]{:S(2)}) collective-permute-start(bf16[6,64,512]{2,1,0:T(8,128)(2,1)S(1)} %get-tuple-element.119), channel_id=1, source_target_pairs={{1,2},{2,1},{3,4},{4,3},{5,6},{6,5},{9,10},{10,9},{11,12},{12,11},... | collective-permute-start | bytes 1179656 | tf_op jit(solution)/shard_map/ppermute | solution.py:626
  99.3 23.1 %collective-permute-start.22 = (bf16[4,88,512]{2,1,0:T(8,128)(2,1)S(1)}, bf16[4,88,512]{2,1,0:T(8,128)(2,1)S(1)}, u32[]{:S(2)}, u32[]{:S(2)}) collective-permute-start(bf16[4,88,512]{2,1,0:T(8,128)(2,1)S(1)} %join.7.refs_0_.refs_1_), channel_id=1, source_target_pairs={{0,17},{1,16},{2,19},{3,18},{4,21},{5,20},{6,23},{7,22},{8,25},{9,... | collective-permute-start | bytes 1081352 | tf_op jit(solution)/shard_map/ppermute | solution.py:640
  100.9 21.6 %collective-permute-start.21 = (bf16[4,88,512]{2,1,0:T(8,128)(2,1)S(1)}, bf16[4,88,512]{2,1,0:T(8,128)(2,1)S(1)}, u32[]{:S(2)}, u32[]{:S(2)}) collective-permute-start(bf16[4,88,512]{2,1,0:T(8,128)(2,1)S(1)} %join.7.refs_0_.refs_1_), channel_id=1, source_target_pairs={{0,16},{1,17},{2,18},{3,19},{4,20},{5,21},{6,22},{7,23},{8,24},{9,... | collective-permute-start | bytes 1081352 | tf_op jit(solution)/shard_map/ppermute | solution.py:640
  101.4 21.0 %collective-permute-start.20 = (bf16[4,88,512]{2,1,0:T(8,128)(2,1)S(1)}, bf16[4,88,512]{2,1,0:T(8,128)(2,1)S(1)}, u32[]{:S(2)}, u32[]{:S(2)}) collective-permute-start(bf16[4,88,512]{2,1,0:T(8,128)(2,1)S(1)} %join.7.refs_0_.refs_1_), channel_id=1, source_target_pairs={{0,1},{1,0},{2,3},{3,2},{4,5},{5,4},{6,7},{7,6},{8,9},{9,8},{10,11... | collective-permute-start | bytes 1081352 | tf_op jit(solution)/shard_map/ppermute | solution.py:640
  102.9 6.8 %collective-permute-start.17 = (bf16[1,48,512]{2,1,0:T(8,128)(2,1)S(1)}, bf16[1,48,512]{2,1,0:T(8,128)(2,1)S(1)}, u32[]{:S(2)}, u32[]{:S(2)}) collective-permute-start(bf16[1,48,512]{2,1,0:T(8,128)(2,1)S(1)} %get-tuple-element.144), channel_id=1, source_target_pairs={{0,4},{1,5},{2,6},{3,7},{4,0},{5,1},{6,2},{7,3},{8,12},{9,13},{10,... | collective-permute-start | bytes 147464 | tf_op jit(solution)/shard_map/ppermute | solution.py:640
  109.7 5.1 %collective-permute-start.18 = (bf16[1,48,512]{2,1,0:T(8,128)(2,1)S(1)}, bf16[1,48,512]{2,1,0:T(8,128)(2,1)S(1)}, u32[]{:S(2)}, u32[]{:S(2)}) collective-permute-start(bf16[1,48,512]{2,1,0:T(8,128)(2,1)S(1)} %add.15.refs_0_), channel_id=1, source_target_pairs={{0,4},{1,5},{2,6},{3,7},{4,0},{5,1},{6,2},{7,3},{8,12},{9,13},{10,... | collective-permute-start | bytes 147464 | tf_op jit(solution)/shard_map/ppermute | solution.py:640
  114.8 7.7 %collective-permute-start.19 = (bf16[2,48,512]{2,1,0:T(8,128)(2,1)S(1)}, bf16[2,48,512]{2,1,0:T(8,128)(2,1)S(1)}, u32[]{:S(2)}, u32[]{:S(2)}) collective-permute-start(bf16[2,48,512]{2,1,0:T(8,128)(2,1)S(1)} %join.8.refs_1_), channel_id=1, source_target_pairs={{0,2},{1,3},{2,0},{3,1},{4,6},{5,7},{6,4},{7,5},{8,10},{9,11},{10,... | collective-permute-start | bytes 294920 | tf_op jit(solution)/shard_map/ppermute | solution.py:640
  122.6 7.5 %collective-permute-start.23 = (bf16[16,88,512]{2,1,0:T(8,128)(2,1)S(1)}, bf16[16,88,512]{2,1,0:T(8,128)(2,1)S(1)}, u32[]{:S(2)}, u32[]{:S(2)}) collective-permute-start(bf16[16,88,512]{2,1,0:T(8,128)(2,1)S(1)} %join.10.refs_0_), channel_id=1, source_target_pairs={{0,8},{1,9},{2,10},{3,11},{4,12},{5,13},{6,14},{7,15},{8,0},{9,1},... | collective-permute-start | bytes 4325384 | tf_op jit(solution)/shard_map/ppermute | solution.py:640
  122.7 10.5 %collective-permute-start.26 = (bf16[4,48,512]{2,1,0:T(8,128)(2,1)S(1)}, bf16[4,48,512]{2,1,0:T(8,128)(2,1)S(1)}, u32[]{:S(2)}, u32[]{:S(2)}) collective-permute-start(bf16[4,48,512]{2,1,0:T(8,128)(2,1)S(1)} %join.9.refs_0_.refs_2_), channel_id=1, source_target_pairs={{0,17},{1,16},{2,19},{3,18},{4,21},{5,20},{6,23},{7,22},{8,25},{9,... | collective-permute-start | bytes 589832 | tf_op jit(solution)/shard_map/ppermute | solution.py:640
  125.1 10.0 %collective-permute-start.25 = (bf16[4,48,512]{2,1,0:T(8,128)(2,1)S(1)}, bf16[4,48,512]{2,1,0:T(8,128)(2,1)S(1)}, u32[]{:S(2)}, u32[]{:S(2)}) collective-permute-start(bf16[4,48,512]{2,1,0:T(8,128)(2,1)S(1)} %join.9.refs_0_.refs_2_), channel_id=1, source_target_pairs={{0,16},{1,17},{2,18},{3,19},{4,20},{5,21},{6,22},{7,23},{8,24},{9,... | collective-permute-start | bytes 589832 | tf_op jit(solution)/shard_map/ppermute | solution.py:640
  125.6 9.5 %collective-permute-start.24 = (bf16[4,48,512]{2,1,0:T(8,128)(2,1)S(1)}, bf16[4,48,512]{2,1,0:T(8,128)(2,1)S(1)}, u32[]{:S(2)}, u32[]{:S(2)}) collective-permute-start(bf16[4,48,512]{2,1,0:T(8,128)(2,1)S(1)} %join.9.refs_0_.refs_2_), channel_id=1, source_target_pairs={{0,1},{1,0},{2,3},{3,2},{4,5},{5,4},{6,7},{7,6},{8,9},{9,8},{10,11... | collective-permute-start | bytes 589832 | tf_op jit(solution)/shard_map/ppermute | solution.py:640
  135.1 0.7 copy-start.5
  135.8 2.4 %collective-permute-start.27 = (bf16[16,48,512]{2,1,0:T(8,128)(2,1)S(1)}, bf16[16,48,512]{2,1,0:T(8,128)(2,1)S(1)}, u32[]{:S(2)}, u32[]{:S(2)}) collective-permute-start(bf16[16,48,512]{2,1,0:T(8,128)(2,1)S(1)} %join.11.refs_0_), channel_id=1, source_target_pairs={{0,8},{1,9},{2,10},{3,11},{4,12},{5,13},{6,14},{7,15},{8,0},{9,1},... | collective-permute-start | bytes 2359304 | tf_op jit(solution)/shard_map/ppermute | solution.py:640
